TPU v7x, 128 devices: a whole 4x4x4 slice. The times are simulated.
128 devices in a mesh: dp: 2 (over core), ctx: 16 (over y, z), tensor: 4 (over x).
Axes of the slice: x: 4, y: 4, z: 4, core: 2. Of those that a mesh axis runs over, the one named last changes fastest.
Arguments:
- inputs: bfloat16 [2, 2, 4096, 2048], P(None, 'dp', 'ctx'), may hold values from -6 to 6
- cotangent: bfloat16 [2, 2, 4096, 2048], P(None, 'dp', 'ctx'), may hold values from -6 to 6
- group_place: int32 [32], replicated, may hold values from 0 to 31, as said below
- attend_gain: bfloat16 [2048], P(('dp', 'ctx')), may hold values from 0.5 to 1.5
- attend_shift: bfloat16 [2048], P(('dp', 'ctx')), may hold values from -2 to 2
- project_weight: bfloat16 [2048, 3, 2048], P(('dp', 'ctx'), None, 'tensor'), may hold values from -0.125 to 0.125
- project_bias: bfloat16 [3, 32, 64], P(None, 'tensor', ('dp', 'ctx')), may hold values from -3 to 3
- output_weight: bfloat16 [2048, 2048], P('tensor', ('dp', 'ctx')), may hold values from -4 to 4
- mixer_gain: bfloat16 [2048], P(('dp', 'ctx')), may hold values from 0.5 to 1.5
- mixer_shift: bfloat16 [2048], P(('dp', 'ctx')), may hold values from -2 to 2
- gate_weight: bfloat16 [2048, 5632], P(('dp', 'ctx'), 'tensor'), may hold values from -0.125 to 0.125
- up_weight: bfloat16 [2048, 5632], P(('dp', 'ctx'), 'tensor'), may hold values from -0.125 to 0.125
- down_weight: bfloat16 [5632, 2048], P('tensor', ('dp', 'ctx')), may hold values from -0.078125 to 0.078125
Outputs:
- outputs: bfloat16 [2, 2, 4096, 2048], P(None, 'dp', 'ctx')
- input_grad: bfloat16 [2, 2, 4096, 2048], P(None, 'dp', 'ctx')
- attend_gain_grad: float32 [2048], P(('dp', 'ctx'))
- attend_shift_grad: float32 [2048], P(('dp', 'ctx'))
- project_weight_grad: float32 [2048, 3, 2048], P(('dp', 'ctx'), None, 'tensor')
- project_bias_grad: float32 [3, 32, 64], P(None, 'tensor', ('dp', 'ctx'))
- output_weight_grad: float32 [2048, 2048], P('tensor', ('dp', 'ctx'))
- mixer_gain_grad: float32 [2048], P(('dp', 'ctx'))
- mixer_shift_grad: float32 [2048], P(('dp', 'ctx'))
- gate_weight_grad: float32 [2048, 5632], P(('dp', 'ctx'), 'tensor')
- up_weight_grad: float32 [2048, 5632], P(('dp', 'ctx'), 'tensor')
- down_weight_grad: float32 [5632, 2048], P('tensor', ('dp', 'ctx'))
Inputs may be any that keep to these rules, and one draw needn't show every extreme that they name: `group_place`: stored blocks 2 j and 2 j + 1 of every sequence hold blocks of positions c and 31 - c for some c; every block of positions appears once; each block covers 256/2 consecutive positions.
All inputs are finite; a program needn't handle non-finite values.
Results may differ from a plain program's by a relative error of at most 0.029.
Values may be sent and summed in bfloat16 or wider, within the bound.
A program may use at most 320 MiB of HBM per device.

v0:
```python
import jax
import jax.numpy as jnp
from jax import lax
from jax.sharding import PartitionSpec as P

HEAD_DIM = 64
ROT = 16


EPSILON = 1e-05
SCORE_SCALE = 0.125
MASKED_SCORE = -1e30


def norm_forward(values, gain_row, shift_row):
    centre = jnp.mean(values, axis=-1, keepdims=True)
    spread = values - centre
    inverse = lax.rsqrt(jnp.mean(spread * spread, axis=-1, keepdims=True) + EPSILON)
    normed = spread * inverse
    return (normed * gain_row + shift_row, normed, inverse)


def norm_backward(upstream, normed, inverse, gain_row):
    scaled = upstream * gain_row
    first_mean = jnp.mean(scaled, axis=-1, keepdims=True)
    second_mean = jnp.mean(scaled * normed, axis=-1, keepdims=True)
    return inverse * (scaled - first_mean - normed * second_mean)


def rotary_tables(places, rot_dims):
    frequency = 10000.0 ** (-jnp.arange(0, rot_dims, 2, dtype=jnp.float32) / rot_dims)
    angles = places.astype(jnp.float32)[:, None] * frequency[None, :]
    cosine_table = jnp.concatenate([jnp.cos(angles), jnp.cos(angles)], axis=-1)
    sine_table = jnp.concatenate([jnp.sin(angles), jnp.sin(angles)], axis=-1)
    return (cosine_table, sine_table)


def rotate(values, cosine_table, sine_table):
    rot_dims = cosine_table.shape[-1]
    halfway = rot_dims // 2
    turned = values[..., :rot_dims]
    swapped = jnp.concatenate([-turned[..., halfway:], turned[..., :halfway]], axis=-1)
    result = turned * cosine_table[:, None, :] + swapped * sine_table[:, None, :]
    return jnp.concatenate([result, values[..., rot_dims:]], axis=-1)


def places_of(group_place, first_row, piece_rows, half_rows):
    row_index = first_row + jnp.arange(piece_rows, dtype=jnp.int32)
    slot_ids = row_index // half_rows
    group_ids = jnp.arange(group_place.shape[0], dtype=jnp.int32)
    chosen = jnp.sum(
        jnp.where(slot_ids[:, None] == group_ids[None, :], group_place[None, :], 0), axis=1
    )
    return chosen * half_rows + row_index % half_rows


def score_block(query_rows, key_rows, query_places, key_places):
    scores = (
        jnp.einsum("bqhe,bkhe->bhqk", query_rows, key_rows, preferred_element_type=jnp.float32)
        * SCORE_SCALE
    )
    allowed = query_places[:, None] >= key_places[None, :]
    return (scores, allowed)


def gather_weights(shards):
    return (
        lax.all_gather(shards[0], ("dp", "ctx"), axis=0, tiled=True),
        lax.all_gather(shards[1], ("dp", "ctx"), axis=0, tiled=True),
        lax.all_gather(shards[2], ("dp", "ctx"), axis=0, tiled=True),
        lax.all_gather(shards[3], ("dp", "ctx"), axis=2, tiled=True),
        lax.all_gather(shards[4], ("dp", "ctx"), axis=1, tiled=True),
        lax.all_gather(shards[5], ("dp", "ctx"), axis=0, tiled=True),
        lax.all_gather(shards[6], ("dp", "ctx"), axis=0, tiled=True),
        lax.all_gather(shards[7], ("dp", "ctx"), axis=0, tiled=True),
        lax.all_gather(shards[8], ("dp", "ctx"), axis=0, tiled=True),
        lax.all_gather(shards[9], ("dp", "ctx"), axis=1, tiled=True),
    )


def forward_pass(weights, inputs_now, places, cosine_table, sine_table, group_place, half_rows):
    seq_local, tok_local, model_width = inputs_now.shape
    tokens = seq_local * tok_local
    feature_local = weights[2].shape[2]
    heads_local = feature_local // HEAD_DIM
    residual = inputs_now.astype(jnp.float32).reshape(tokens, model_width)
    first_norm, first_normed, first_inverse = norm_forward(
        residual, weights[0].astype(jnp.float32), weights[1].astype(jnp.float32)
    )
    first_low = first_norm.astype(jnp.bfloat16)
    project = jnp.einsum("sd,dtf->stf", first_low, weights[2], preferred_element_type=jnp.float32)
    project = project + weights[3].astype(jnp.float32).reshape(3, feature_local)
    project = project.reshape(seq_local, tok_local, 3, heads_local, HEAD_DIM)
    query_heads = rotate(project[:, :, 0], cosine_table, sine_table).astype(jnp.bfloat16)
    key_heads = rotate(project[:, :, 1], cosine_table, sine_table).astype(jnp.bfloat16)
    value_heads = project[:, :, 2].astype(jnp.bfloat16)
    run_max = jnp.full((seq_local, heads_local, tok_local), MASKED_SCORE, jnp.float32)
    key_piece = lax.all_gather(key_heads, "ctx", axis=1, tiled=True)
    value_piece = lax.all_gather(value_heads, "ctx", axis=1, tiled=True)
    piece_rows = key_piece.shape[1]
    key_places = places_of(group_place, jnp.int32(0), piece_rows, half_rows)
    scores, allowed = score_block(query_heads, key_piece, places, key_places)
    scores = jnp.where(allowed, scores, MASKED_SCORE)
    new_max = jnp.maximum(run_max, jnp.max(scores, axis=-1))
    exp_weights = jnp.where(allowed, jnp.exp(scores - new_max[..., None]), 0.0)
    run_sum = jnp.sum(exp_weights, axis=-1)
    run_acc = jnp.einsum(
        "bhqk,bkhe->bhqe",
        exp_weights.astype(jnp.bfloat16),
        value_piece,
        preferred_element_type=jnp.float32,
    )
    run_max, run_sum, run_acc = (new_max, run_sum, run_acc)
    attended = run_acc / run_sum[..., None]
    logsum = run_max + jnp.log(run_sum)
    attended_low = attended.astype(jnp.bfloat16)
    branch_part = jnp.einsum(
        "bhqe,hef->bqf",
        attended_low,
        weights[4].reshape(heads_local, HEAD_DIM, model_width),
        preferred_element_type=jnp.float32,
    )
    branch = lax.psum(branch_part.astype(jnp.bfloat16), "tensor").astype(jnp.float32)
    hidden = residual + branch.reshape(tokens, model_width)
    second_norm, second_normed, second_inverse = norm_forward(
        hidden, weights[5].astype(jnp.float32), weights[6].astype(jnp.float32)
    )
    second_low = second_norm.astype(jnp.bfloat16)
    gate_value = jnp.dot(second_low, weights[7], preferred_element_type=jnp.float32)
    up_value = jnp.dot(second_low, weights[8], preferred_element_type=jnp.float32)
    mixed = (jax.nn.silu(gate_value) * up_value).astype(jnp.bfloat16)
    mixer_part = jnp.dot(mixed, weights[9], preferred_element_type=jnp.float32)
    mixer_out = lax.psum(mixer_part.astype(jnp.bfloat16), "tensor").astype(jnp.float32)
    result = (hidden + mixer_out).astype(jnp.bfloat16).reshape(seq_local, tok_local, model_width)
    kept = (
        first_normed,
        first_inverse,
        first_low,
        query_heads,
        key_heads,
        value_heads,
        attended,
        attended_low,
        logsum,
        second_normed,
        second_inverse,
        second_low,
        gate_value,
        up_value,
        mixed,
    )
    return (result, kept)


def backward_pass(
    weights, kept, grad_in, places, cosine_table, sine_table, group_place, half_rows, totals
):
    (
        first_normed,
        first_inverse,
        first_low,
        query_heads,
        key_heads,
        value_heads,
        attended,
        attended_low,
        logsum,
        second_normed,
        second_inverse,
        second_low,
        gate_value,
        up_value,
        mixed,
    ) = kept
    seq_local, tok_local, model_width = grad_in.shape
    tokens = seq_local * tok_local
    feature_local = weights[2].shape[2]
    heads_local = feature_local // HEAD_DIM
    grad_out = grad_in.reshape(tokens, model_width)
    grad_float = grad_out.astype(jnp.float32)
    down_grad = jnp.einsum("sf,sd->fd", mixed, grad_out, preferred_element_type=jnp.float32)
    grad_mixed = jnp.einsum("sd,fd->sf", grad_out, weights[9], preferred_element_type=jnp.float32)
    sigmoid_gate = jax.nn.sigmoid(gate_value)
    grad_gate = (
        grad_mixed * up_value * sigmoid_gate * (1.0 + gate_value * (1.0 - sigmoid_gate))
    ).astype(jnp.bfloat16)
    grad_up = (grad_mixed * gate_value * sigmoid_gate).astype(jnp.bfloat16)
    gate_grad = jnp.einsum("sd,sf->df", second_low, grad_gate, preferred_element_type=jnp.float32)
    up_grad = jnp.einsum("sd,sf->df", second_low, grad_up, preferred_element_type=jnp.float32)
    second_part = jnp.einsum(
        "sf,df->sd", grad_gate, weights[7], preferred_element_type=jnp.float32
    ) + jnp.einsum("sf,df->sd", grad_up, weights[8], preferred_element_type=jnp.float32)
    grad_second = lax.psum(second_part.astype(jnp.bfloat16), "tensor").astype(jnp.float32)
    mixer_gain_grad = jnp.sum(grad_second * second_normed, axis=0)
    mixer_shift_grad = jnp.sum(grad_second, axis=0)
    grad_hidden = grad_float + norm_backward(
        grad_second, second_normed, second_inverse, weights[5].astype(jnp.float32)
    )
    hidden_low = grad_hidden.astype(jnp.bfloat16).reshape(seq_local, tok_local, model_width)
    output_grad = jnp.einsum(
        "bhqe,bqf->hef", attended_low, hidden_low, preferred_element_type=jnp.float32
    ).reshape(feature_local, model_width)
    grad_attended = jnp.einsum(
        "bqf,hef->bhqe",
        hidden_low,
        weights[4].reshape(heads_local, HEAD_DIM, model_width),
        preferred_element_type=jnp.float32,
    ).astype(jnp.bfloat16)
    delta = jnp.sum(grad_attended.astype(jnp.float32) * attended, axis=-1)
    key_piece = lax.all_gather(key_heads, "ctx", axis=1, tiled=True)
    value_piece = lax.all_gather(value_heads, "ctx", axis=1, tiled=True)
    piece_rows = key_piece.shape[1]
    key_places = places_of(group_place, jnp.int32(0), piece_rows, half_rows)
    scores, allowed = score_block(query_heads, key_piece, places, key_places)
    probs = jnp.where(allowed, jnp.exp(scores - logsum[..., None]), 0.0)
    probs_low = probs.astype(jnp.bfloat16)
    grad_value = jnp.einsum(
        "bhqk,bhqe->bkhe", probs_low, grad_attended, preferred_element_type=jnp.float32
    )
    grad_probs = jnp.einsum(
        "bhqe,bkhe->bhqk", grad_attended, value_piece, preferred_element_type=jnp.float32
    )
    grad_scores = (probs * (grad_probs - delta[..., None]) * SCORE_SCALE).astype(jnp.bfloat16)
    grad_query = jnp.einsum(
        "bhqk,bkhe->bqhe", grad_scores, key_piece, preferred_element_type=jnp.float32
    )
    grad_key = jnp.einsum(
        "bhqk,bqhe->bkhe", grad_scores, query_heads, preferred_element_type=jnp.float32
    )
    fresh = jnp.concatenate(
        [
            grad_key.reshape(seq_local, piece_rows, feature_local),
            grad_value.reshape(seq_local, piece_rows, feature_local),
        ],
        axis=-1,
    )
    grad_keyvalue = fresh
    grad_query, grad_keyvalue = (grad_query, grad_keyvalue)
    own_keyvalue = lax.psum_scatter(
        grad_keyvalue.astype(jnp.bfloat16), "ctx", scatter_dimension=1, tiled=True
    ).astype(jnp.float32)
    grad_key_raw = own_keyvalue[..., :feature_local].reshape(
        seq_local, tok_local, heads_local, HEAD_DIM
    )
    grad_value_flat = own_keyvalue[..., feature_local:]
    grad_query = rotate(grad_query, cosine_table, -sine_table).reshape(
        seq_local, tok_local, feature_local
    )
    grad_key = rotate(grad_key_raw, cosine_table, -sine_table).reshape(
        seq_local, tok_local, feature_local
    )
    grad_project = jnp.stack([grad_query, grad_key, grad_value_flat], axis=2)
    grad_project = grad_project.astype(jnp.bfloat16).reshape(tokens, 3, feature_local)
    project_grad = jnp.einsum(
        "sd,stf->dtf", first_low, grad_project, preferred_element_type=jnp.float32
    )
    bias_grad = jnp.sum(grad_project.astype(jnp.float32), axis=0).reshape(3, heads_local, HEAD_DIM)
    first_part = jnp.einsum(
        "stf,dtf->sd", grad_project, weights[2], preferred_element_type=jnp.float32
    )
    grad_first = lax.psum(first_part.astype(jnp.bfloat16), "tensor").astype(jnp.float32)
    attend_gain_grad = jnp.sum(grad_first * first_normed, axis=0)
    attend_shift_grad = jnp.sum(grad_first, axis=0)
    grad_input = grad_hidden + norm_backward(
        grad_first, first_normed, first_inverse, weights[0].astype(jnp.float32)
    )
    fresh_grads = (
        attend_gain_grad,
        attend_shift_grad,
        project_grad,
        bias_grad,
        output_grad,
        mixer_gain_grad,
        mixer_shift_grad,
        gate_grad,
        up_grad,
        down_grad,
    )
    totals = tuple((old_sum + new_term for old_sum, new_term in zip(totals, fresh_grads)))
    return (grad_input.astype(jnp.bfloat16).reshape(seq_local, tok_local, model_width), totals)


def body(
    inputs,
    cotangent,
    group_place,
    attend_gain,
    attend_shift,
    project_weight,
    project_bias,
    output_weight,
    mixer_gain,
    mixer_shift,
    gate_weight,
    up_weight,
    down_weight,
):
    shards = (
        attend_gain,
        attend_shift,
        project_weight,
        project_bias,
        output_weight,
        mixer_gain,
        mixer_shift,
        gate_weight,
        up_weight,
        down_weight,
    )
    micro_count, seq_local, tok_local, model_width = inputs.shape
    half_rows = tok_local // 2
    ctx_index = lax.axis_index("ctx")
    places = places_of(group_place, ctx_index * tok_local, tok_local, half_rows)
    cosine_table, sine_table = rotary_tables(places, ROT)
    feature_local = project_weight.shape[2]
    heads_local = feature_local // HEAD_DIM
    units_local = gate_weight.shape[1]
    totals = (
        jnp.zeros((model_width,), jnp.float32),
        jnp.zeros((model_width,), jnp.float32),
        jnp.zeros((model_width, 3, feature_local), jnp.float32),
        jnp.zeros((3, heads_local, HEAD_DIM), jnp.float32),
        jnp.zeros((feature_local, model_width), jnp.float32),
        jnp.zeros((model_width,), jnp.float32),
        jnp.zeros((model_width,), jnp.float32),
        jnp.zeros((model_width, units_local), jnp.float32),
        jnp.zeros((model_width, units_local), jnp.float32),
        jnp.zeros((units_local, model_width), jnp.float32),
    )
    results_list = []
    grads_list = []
    for micro_index in range(micro_count):
        front_weights = gather_weights(shards)
        result, kept = forward_pass(
            front_weights,
            inputs[micro_index],
            places,
            cosine_table,
            sine_table,
            group_place,
            half_rows,
        )
        back_weights = gather_weights(shards)
        grad_input, totals = backward_pass(
            back_weights,
            kept,
            cotangent[micro_index],
            places,
            cosine_table,
            sine_table,
            group_place,
            half_rows,
            totals,
        )
        results_list.append(result)
        grads_list.append(grad_input)
    reduced = (
        lax.psum_scatter(
            totals[0].astype(jnp.bfloat16), ("dp", "ctx"), scatter_dimension=0, tiled=True
        ).astype(jnp.float32),
        lax.psum_scatter(
            totals[1].astype(jnp.bfloat16), ("dp", "ctx"), scatter_dimension=0, tiled=True
        ).astype(jnp.float32),
        lax.psum_scatter(
            totals[2].astype(jnp.bfloat16), ("dp", "ctx"), scatter_dimension=0, tiled=True
        ).astype(jnp.float32),
        lax.psum_scatter(
            totals[3].astype(jnp.bfloat16), ("dp", "ctx"), scatter_dimension=2, tiled=True
        ).astype(jnp.float32),
        lax.psum_scatter(
            totals[4].astype(jnp.bfloat16), ("dp", "ctx"), scatter_dimension=1, tiled=True
        ).astype(jnp.float32),
        lax.psum_scatter(
            totals[5].astype(jnp.bfloat16), ("dp", "ctx"), scatter_dimension=0, tiled=True
        ).astype(jnp.float32),
        lax.psum_scatter(
            totals[6].astype(jnp.bfloat16), ("dp", "ctx"), scatter_dimension=0, tiled=True
        ).astype(jnp.float32),
        lax.psum_scatter(
            totals[7].astype(jnp.bfloat16), ("dp", "ctx"), scatter_dimension=0, tiled=True
        ).astype(jnp.float32),
        lax.psum_scatter(
            totals[8].astype(jnp.bfloat16), ("dp", "ctx"), scatter_dimension=0, tiled=True
        ).astype(jnp.float32),
        lax.psum_scatter(
            totals[9].astype(jnp.bfloat16), ("dp", "ctx"), scatter_dimension=1, tiled=True
        ).astype(jnp.float32),
    )
    return (
        jnp.stack(results_list),
        jnp.stack(grads_list),
        reduced[0],
        reduced[1],
        reduced[2],
        reduced[3],
        reduced[4],
        reduced[5],
        reduced[6],
        reduced[7],
        reduced[8],
        reduced[9],
    )


def solution(mesh):
    placed = (
        P(None, "dp", "ctx", None),
        P(None, "dp", "ctx", None),
        P(),
        P(("dp", "ctx")),
        P(("dp", "ctx")),
        P(("dp", "ctx"), None, "tensor"),
        P(None, "tensor", ("dp", "ctx")),
        P("tensor", ("dp", "ctx")),
        P(("dp", "ctx")),
        P(("dp", "ctx")),
        P(("dp", "ctx"), "tensor"),
        P(("dp", "ctx"), "tensor"),
        P("tensor", ("dp", "ctx")),
    )
    return jax.shard_map(
        body,
        mesh=mesh,
        in_specs=placed,
        out_specs=(
            P(None, "dp", "ctx", None),
            P(None, "dp", "ctx", None),
            P(("dp", "ctx")),
            P(("dp", "ctx")),
            P(("dp", "ctx"), None, "tensor"),
            P(None, "tensor", ("dp", "ctx")),
            P("tensor", ("dp", "ctx")),
            P(("dp", "ctx")),
            P(("dp", "ctx")),
            P(("dp", "ctx"), "tensor"),
            P(("dp", "ctx"), "tensor"),
            P("tensor", ("dp", "ctx")),
        ),
        check_vma=False,
    )
```

profile of v0, /device:TPU:1, one launch (start us, length us, event | category | flops | bytes accessed | tf_op | source)
XLA Modules:
  0.0 1686.2 jit_solution(9475920510135851814)
XLA Ops:
  14.8 132.0 %all-reduce.10 = (bf16[2048]{0:T(1024)(128)(2,1)S(1)}, bf16[2048]{0:T(1024)(128)(2,1)S(1)}, bf16[2048]{0:T(1024)(128)(2,1)S(1)}, bf16[2048]{0:T(1024)(128)(2,1)S(1)}) all-reduce(bf16[2048]{0:T(1024)(128)(2,1)S(1)} %dynamic-update-slice.3, ...), channel_id=1, replica_groups=mesh['dp'=2,'ctx'=16,'tensor'=4] {'dp','ctx'}, use_global_device_ids=true, to_apply=%add.3 | all-reduce | flops 8192 | bytes 32768
  146.7 61.5 %all_gather.31 = bf16[3,8,64]{1,0,2:T(4,128)(2,1)S(1)} all-gather(bf16[3,8,2]{1,0,2:T(4,128)(2,1)S(1)} %copy.99), channel_id=1, replica_groups=mesh['dp'=2,'ctx'=16,'tensor'=4] {'dp','ctx'}, dimensions={2}, use_global_device_ids=true | all-gather | bytes 3168 | tf_op jit(solution)/shard_map/all_gather | solution.py:71
  232.0 47.0 %all-gather.14.cloned.1.call-done = bf16[1,4096,8,64]{1,3,2,0:T(8,128)(2,1)} async-done(((bf16[1,256,8,64]{1,3,2,0:T(8,128)(2,1)}), bf16[1,4096,8,64]{1,3,2,0:T(8,128)(2,1)}) %all-gather.14.cloned.1.call-update) | async-done | bytes 4194320 | tf_op jit(solution)/shard_map/all_gather | solution.py:98
  312.1 26.5 %all-gather.26.cloned.1.call-done = bf16[1,4096,1,8,64]{1,4,3,2,0:T(8,128)(2,1)} async-done(((bf16[1,256,1,8,64]{1,4,3,2,0:T(8,128)(2,1)}), bf16[1,4096,1,8,64]{1,4,3,2,0:T(8,128)(2,1)}) %all-gather.26.cloned.1.call-update) | async-done | bytes 4194320 | tf_op jit(solution)/shard_map/all_gather | solution.py:99
  338.6 16.8 fusion.197
  359.3 44.1 %all-reduce.18.cloned.1.call-done = bf16[256,2048]{1,0:T(8,128)(2,1)} async-done(((bf16[256,2048]{1,0:T(8,128)(2,1)}), bf16[256,2048]{1,0:T(8,128)(2,1)}) %all-reduce.18.cloned.1.call-update) | async-done | bytes 1048592 | tf_op jit(solution)/shard_map/psum | solution.py:123
  420.0 56.3 %all-gather.24.cloned.1.call-done = bf16[1,4096,8,64]{1,3,2,0:T(8,128)(2,1)} async-done(((bf16[1,256,8,64]{1,3,2,0:T(8,128)(2,1)}), bf16[1,4096,8,64]{1,3,2,0:T(8,128)(2,1)}) %all-gather.24.cloned.1.call-update) | async-done | bytes 4194320 | tf_op jit(solution)/shard_map/all_gather | solution.py:98
  508.7 27.4 %all-gather.28.cloned.1.call-done = bf16[1,4096,1,8,64]{1,4,3,2,0:T(8,128)(2,1)} async-done(((bf16[1,256,1,8,64]{1,4,3,2,0:T(8,128)(2,1)}), bf16[1,4096,1,8,64]{1,4,3,2,0:T(8,128)(2,1)}) %all-gather.28.cloned.1.call-update) | async-done | bytes 4194320 | tf_op jit(solution)/shard_map/all_gather | solution.py:99
  536.2 16.8 fusion.198
  558.7 42.3 %all-reduce.20.cloned.1.call-done = bf16[256,2048]{1,0:T(8,128)(2,1)} async-done(((bf16[256,2048]{1,0:T(8,128)(2,1)}), bf16[256,2048]{1,0:T(8,128)(2,1)}) %all-reduce.20.cloned.1.call-update) | async-done | bytes 1048592 | tf_op jit(solution)/shard_map/psum | solution.py:123
  607.1 47.4 %all-gather.20.cloned.1.call-done = bf16[2048,1408]{1,0:T(8,128)(2,1)} async-done(((bf16[64,1408]{1,0:T(8,128)(2,1)}), bf16[2048,1408]{1,0:T(8,128)(2,1)}) %all-gather.20.cloned.1.call-update) | async-done | bytes 5767184 | tf_op jit(solution)/shard_map/all_gather | solution.py:76
  660.4 43.7 %all-gather.18.cloned.1.call-done = bf16[2048,1408]{1,0:T(8,128)(2,1)} async-done(((bf16[64,1408]{1,0:T(8,128)(2,1)}), bf16[2048,1408]{1,0:T(8,128)(2,1)}) %all-gather.18.cloned.1.call-update) | async-done | bytes 5767184 | tf_op jit(solution)/shard_map/all_gather | solution.py:75
  716.0 37.8 %all-gather.22.cloned.1.call-done = bf16[1408,2048]{0,1:T(8,128)(2,1)} async-done(((bf16[1408,64]{0,1:T(8,128)(2,1)}), bf16[1408,2048]{0,1:T(8,128)(2,1)}) %all-gather.22.cloned.1.call-update) | async-done | bytes 5767184 | tf_op jit(solution)/shard_map/all_gather | solution.py:77
  777.4 57.5 %all-reduce.24.cloned.1.call-done = (bf16[256,2048]{1,0:T(8,128)(2,1)}, bf16[256,2048]{1,0:T(8,128)(2,1)}) async-done(((bf16[256,2048]{1,0:T(8,128)(2,1)}, bf16[256,2048]{1,0:T(8,128)(2,1)}), (bf16[256,2048]{1,0:T(8,128)(2,1)}, bf16[256,2048]{1,0:T(8,128)(2,1)})) %all-reduce.24.cloned.1.call-update) | async-done | bytes 2097168 | tf_op jit(solution)/shard_map/psum | solution.py:193
  860.2 23.9 %multiply_convert_fusion = bf16[8,256,4096]{2,1,0:T(8,128)(2,1)} fusion(f32[8,256,4096]{2,1,0:T(8,128)} %get-tuple-element.156, f32[8,256]{1,0:T(8,128)S(1)} %get-tuple-element.159, f32[8,256]{1,0:T(8,128)S(1)} %log_add_fusion, pred[256,4096]{1,0:T(8,128)(4,1)S(1)} %broadcast_compare_fusion, bf16[1,4096,1,8,64]{1,4,3,2,0:T(8,128)(2,1)} %all-gather.28.cloned.1.call-done, ...), kind=kOutput, calls=%fused_computation | convolution fusion | flops 1132462080 | bytes 55853056 | tf_op jit(solution)/shard_map/bhqe,bkhe->bhqk/dot_general | solution.py:220
  919.8 23.9 %multiply_convert_fusion.1 = bf16[8,256,4096]{2,1,0:T(8,128)(2,1)} fusion(f32[8,256,4096]{2,1,0:T(8,128)} %get-tuple-element.152, f32[8,256]{1,0:T(8,128)S(1)} %get-tuple-element.161, f32[8,256]{1,0:T(8,128)S(1)} %log_add_fusion.1, pred[256,4096]{1,0:T(8,128)(4,1)S(1)} %broadcast_compare_fusion, ...), kind=kOutput, calls=%fused_computation.2 | convolution fusion | flops 1132462080 | bytes 55853056 | tf_op jit(solution)/shard_map/bhqe,bkhe->bhqk/dot_general | solution.py:220
  961.5 16.9 %fusion.18 = bf16[8,64,4096]{2,1,0:T(8,128)(2,1)} fusion(f32[8,256,4096]{2,1,0:T(8,128)} %get-tuple-element.152, f32[8,256]{1,0:T(8,128)S(1)} %log_add_fusion.1, pred[256,4096]{1,0:T(8,128)(4,1)S(1)} %broadcast_compare_fusion, bf16[256,8,64]{0,2,1:T(8,128)(2,1)S(1)} %get-tuple-element.162), kind=kOutput, calls=%fused_computation.30 | convolution fusion | flops 1109393408 | bytes 39067648 | tf_op jit(solution)/shard_map/bhqk,bhqe->bkhe/dot_general | solution.py:217
  1061.9 25.9 %reduce-scatter.8.cloned.1.call-done = bf16[1,256,1024]{2,1,0:T(8,128)(2,1)} async-done(((bf16[1,4096,1024]{2,1,0:T(8,128)(2,1)}), bf16[1,256,1024]{2,1,0:T(8,128)(2,1)}) %reduce-scatter.8.cloned.1.call-update) | async-done | bytes 524304 | tf_op jit(solution)/shard_map/reduce_scatter | solution.py:239
  1115.7 54.4 %reduce-scatter.14.cloned.1.call-done = bf16[512,64]{0,1:T(8,128)(2,1)} async-done(((bf16[512,2048]{0,1:T(8,128)(2,1)}), bf16[512,64]{0,1:T(8,128)(2,1)}) %reduce-scatter.14.cloned.1.call-update) | async-done | bytes 65552 | tf_op jit(solution)/shard_map/reduce_scatter | solution.py:370
  1171.6 87.3 %reduce-scatter.18.cloned.1.call-done = bf16[64,1408]{1,0:T(8,128)(2,1)} async-done(((bf16[2048,1408]{1,0:T(8,128)(2,1)}), bf16[64,1408]{1,0:T(8,128)(2,1)}) %reduce-scatter.18.cloned.1.call-update) | async-done | bytes 180240 | tf_op jit(solution)/shard_map/reduce_scatter | solution.py:382
  1260.6 86.7 %reduce-scatter.16.cloned.1.call-done = bf16[64,1408]{1,0:T(8,128)(2,1)} async-done(((bf16[2048,1408]{1,0:T(8,128)(2,1)}), bf16[64,1408]{1,0:T(8,128)(2,1)}) %reduce-scatter.16.cloned.1.call-update) | async-done | bytes 180240 | tf_op jit(solution)/shard_map/reduce_scatter | solution.py:379
  1349.0 87.1 %reduce-scatter.20.cloned.1.call-done = bf16[1408,64]{0,1:T(8,128)(2,1)} async-done(((bf16[1408,2048]{0,1:T(8,128)(2,1)}), bf16[1408,64]{0,1:T(8,128)(2,1)}) %reduce-scatter.20.cloned.1.call-update) | async-done | bytes 180240 | tf_op jit(solution)/shard_map/reduce_scatter | solution.py:385
  1440.4 92.4 %all-reduce.22.cloned.1.call-done = (bf16[256,2048]{1,0:T(8,128)(2,1)}, bf16[256,2048]{1,0:T(8,128)(2,1)}, bf16[256,2048]{1,0:T(8,128)(2,1)}, bf16[256,2048]{1,0:T(8,128)(2,1)}) async-done(((bf16[256,2048]{1,0:T(8,128)(2,1)}, bf16[256,2048]{1,0:T(8,128)(2,1)}, bf16[256,2048]{1,0:T(8,128)(2,1)}, bf16[256,2048]{1,0:T(8,128)(2,1)}), (bf16[256,2048]{1,0:T(8,128)(2,1)}, bf16[256,2048]{1,0:T(8,128)(2,1)}, ...) | async-done | bytes 4194320 | tf_op jit(solution)/shard_map/psum | solution.py:133
  1537.1 129.8 %all-reduce.9 = (bf16[2048]{0:T(1024)(128)(2,1)S(1)}, bf16[2048]{0:T(1024)(128)(2,1)S(1)}, bf16[3,8,64]{1,0,2:T(4,128)(2,1)S(1)}, bf16[2048]{0:T(1024)(128)(2,1)S(1)}, bf16[2048]{0:T(1024)(128)(2,1)S(1)}) all-reduce(bf16[2048]{0:T(1024)(128)(2,1)S(1)} %add_convert_fusion.13, ...), channel_id=6, replica_groups=mesh['dp'=2,'ctx'=16,'tensor'=4] {'dp','ctx'}, use_global_device_ids=true, to_apply=%region_36.37.clone | all-reduce | flops 9728 | bytes 38912
  (379 shorter events, 383.1 us)
Async XLA Ops:
  7.2 205.1 %all-gather.12.cloned.1.call-start = ((), (), s32[]{:S(2)}) async-start(), calls=%async_computation.7 | async-start | bytes 6488064 | tf_op jit(solution)/shard_map/all_gather | solution.py:70
  7.9 219.1 %all-gather.16.cloned.1.call-start = ((), (), s32[]{:S(2)}) async-start(), calls=%async_computation.9 | async-start | bytes 2162688 | tf_op jit(solution)/shard_map/all_gather | solution.py:72
  8.7 270.4 %all-gather.14.cloned.1.call-start = ((), (), s32[]{:S(2)}) async-start(), calls=%async_computation.8 | async-start | bytes 4456448 | tf_op jit(solution)/shard_map/all_gather | solution.py:98
  146.7 258.5 %copy-start.52 = (f32[2048]{0:T(1024)}, f32[2048]{0:T(1024)S(1)}, u32[]{:S(2)}) copy-start(f32[2048]{0:T(1024)S(1)} %convert_element_type.372) | copy-start | bytes 24580
  146.7 258.5 %copy-start.54 = (f32[2048]{0:T(1024)}, f32[2048]{0:T(1024)S(1)}, u32[]{:S(2)}) copy-start(f32[2048]{0:T(1024)S(1)} %convert_element_type.373) | copy-start | bytes 24580
  209.9 205.6 %copy-start.48 = (f32[256,16]{0,1:T(8,128)}, f32[256,16]{0,1:T(8,128)S(1)}, u32[]{:S(2)}) copy-start(f32[256,16]{0,1:T(8,128)S(1)} %get-tuple-element.165) | copy-start | bytes 49156
  224.1 114.5 %all-gather.26.cloned.1.call-start = ((), (), s32[]{:S(2)}) async-start(), calls=%async_computation.23 | async-start | bytes 4456448 | tf_op jit(solution)/shard_map/all_gather | solution.py:99
  225.9 177.5 %all-reduce.18.cloned.1.call-start = ((), (), s32[]{:S(2)}) async-start(), calls=%async_computation.10 | async-start | bytes 2097152 | tf_op jit(solution)/shard_map/psum | solution.py:123
  358.8 117.5 %all-gather.24.cloned.1.call-start = ((), (), s32[]{:S(2)}) async-start(), calls=%async_computation.14 | async-start | bytes 4456448 | tf_op jit(solution)/shard_map/all_gather | solution.py:98
  417.0 119.2 %all-gather.28.cloned.1.call-start = ((), (), s32[]{:S(2)}) async-start(), calls=%async_computation.24 | async-start | bytes 4456448 | tf_op jit(solution)/shard_map/all_gather | solution.py:99
  418.9 182.2 %all-reduce.20.cloned.1.call-start = ((), (), s32[]{:S(2)}) async-start(), calls=%async_computation.15 | async-start | bytes 2097152 | tf_op jit(solution)/shard_map/psum | solution.py:123
  556.4 98.1 %all-gather.20.cloned.1.call-start = ((), (), s32[]{:S(2)}) async-start(), calls=%async_computation.12 | async-start | bytes 5947392 | tf_op jit(solution)/shard_map/all_gather | solution.py:76
  557.2 146.9 %all-gather.18.cloned.1.call-start = ((), (), s32[]{:S(2)}) async-start(), calls=%async_computation.11 | async-start | bytes 5947392 | tf_op jit(solution)/shard_map/all_gather | solution.py:75
  557.7 196.1 %all-gather.22.cloned.1.call-start = ((), (), s32[]{:S(2)}) async-start(), calls=%async_computation.13 | async-start | bytes 5947392 | tf_op jit(solution)/shard_map/all_gather | solution.py:77
  558.5 276.4 %all-reduce.24.cloned.1.call-start = ((), (), s32[]{:S(2)}) async-start(), calls=%async_computation.26 | async-start | bytes 4194304 | tf_op jit(solution)/shard_map/psum | solution.py:193
  777.3 282.6 %reduce-scatter.10.cloned.1.call-start = ((), (), s32[]{:S(2)}) async-start(), calls=%async_computation.17 | async-start | bytes 8912896 | tf_op jit(solution)/shard_map/reduce_scatter | solution.py:239
  915.8 172.0 %reduce-scatter.8.cloned.1.call-start = ((), (), s32[]{:S(2)}) async-start(), calls=%async_computation.16 | async-start | bytes 8912896 | tf_op jit(solution)/shard_map/reduce_scatter | solution.py:239
  993.1 177.0 %reduce-scatter.14.cloned.1.call-start = ((), (), s32[]{:S(2)}) async-start(), calls=%async_computation.19 | async-start | bytes 2162688 | tf_op jit(solution)/shard_map/reduce_scatter | solution.py:370
  998.4 260.5 %reduce-scatter.18.cloned.1.call-start = ((), (), s32[]{:S(2)}) async-start(), calls=%async_computation.21 | async-start | bytes 5947392 | tf_op jit(solution)/shard_map/reduce_scatter | solution.py:382
  1006.0 341.3 %reduce-scatter.16.cloned.1.call-start = ((), (), s32[]{:S(2)}) async-start(), calls=%async_computation.20 | async-start | bytes 5947392 | tf_op jit(solution)/shard_map/reduce_scatter | solution.py:379
  1013.2 422.9 %reduce-scatter.20.cloned.1.call-start = ((), (), s32[]{:S(2)}) async-start(), calls=%async_computation.22 | async-start | bytes 5947392 | tf_op jit(solution)/shard_map/reduce_scatter | solution.py:385
  1021.2 511.5 %all-reduce.22.cloned.1.call-start = ((), (), s32[]{:S(2)}) async-start(), calls=%async_computation.25 | async-start | bytes 8388608 | tf_op jit(solution)/shard_map/psum | solution.py:133
  1104.8 572.6 %reduce-scatter.12.cloned.1.call-start = ((), (), s32[]{:S(2)}) async-start(), calls=%async_computation.18 | async-start | bytes 6488064 | tf_op jit(solution)/shard_map/reduce_scatter | solution.py:364
  1114.3 418.5 %copy-start.6 = (bf16[256,2048]{1,0:T(8,128)(2,1)S(1)}, bf16[256,2048]{1,0:T(8,128)(2,1)}, u32[]{:S(2)}) copy-start(bf16[256,2048]{1,0:T(8,128)(2,1)} %all-reduce.20.cloned.1.call-done) | copy-start | bytes 3145732
  (79 other events, 832.4 us)
Sparse Core Ops, SparseCore 0:
  10.3 53.1 all-gather.11
  65.8 42.8 all-gather.15
  224.2 54.8 all-gather.13
  281.6 56.9 all-gather.25
  358.9 44.4 all-reduce.17
  417.1 59.0 all-gather.23
  479.2 56.9 all-gather.27
  556.5 44.4 all-reduce.19
  603.4 51.0 all-gather.19
  656.6 47.4 all-gather.17
  706.4 47.4 all-gather.21
  777.4 57.3 all-reduce.23
  915.9 83.6 reduce-scatter.9
  1003.2 84.5 reduce-scatter.7
  1092.2 77.9 reduce-scatter.13
  1174.2 84.7 reduce-scatter.17
  1262.5 84.7 reduce-scatter.15
  1351.4 84.6 reduce-scatter.19
  1438.6 94.0 all-reduce.21
  1536.8 84.9 reduce-scatter.11
where the time goes:
time: 1690 us
  waiting for transfers between devices  867 us (51%)
  blocking collectives  323 us (19%)
  matrix products  309 us (18%)
  other arithmetic  98.2 us (6%)
  local copies, waits for them, and re-layouts  68.6 us (4%)
  between operations  17.8 us (1%)
    unnamed x2, blocking collectives  262 us
    all_gather x2, waiting for transfers between devices, forward_pass(): key_piece = lax.all_gather(key_heads, 'ctx', axis=1, tiled=True)  103 us
    psum x1, waiting for transfers between devices, forward_pass(): lax.psum(mixer_part.astype(jnp.bfloat16), 'tensor').astype(jnp.float32)  92.4 us
    reduce_scatter x1, waiting for transfers between devices, body(): lax.psum_scatter(totals[8].astype(jnp.bfloat16), ('dp', 'ctx'), scatter_d...  87.3 us
    reduce_scatter x1, waiting for transfers between devices, body(): lax.psum_scatter(totals[9].astype(jnp.bfloat16), ('dp', 'ctx'), scatter_d...  87.1 us
    reduce_scatter x1, waiting for transfers between devices, body(): lax.psum_scatter(totals[7].astype(jnp.bfloat16), ('dp', 'ctx'), scatter_d...  86.7 us
    psum x2, waiting for transfers between devices, forward_pass(): lax.psum(branch_part.astype(jnp.bfloat16), 'tensor').astype(jnp.float32)  86.4 us
    all_gather x1, blocking collectives, gather_weights(): lax.all_gather(shards[3], ('dp', 'ctx'), axis=2, tiled=True)  61.5 us
  transfers between devices with their start and end apart: 20, of which 16 were waited for; matrix products, arithmetic and copies ran while one was open for 18% of the time, Pallas kernels for 0%

commit v1 on v0

v1 whole, which is shorter than its diff:
```python
import functools

import jax
import jax.numpy as jnp
from jax import lax
from jax.experimental import pallas as pl
from jax.experimental.pallas import tpu as pltpu
from jax.sharding import PartitionSpec as P

MESH = pl.DeviceIdType.MESH
D = 2048
UNITS = 1408
HEAD_DIM = 64
ROT = 16
EPSILON = 1e-05
LOG2E = 1.4426950408889634
LOW = -1e30
TILE = 512
VMEM_LIMIT = 58 * 2**20
STEPS = (1, 3, 2)
BF = jnp.bfloat16
F32 = jnp.float32


def here():
    ctx = lax.axis_index("ctx")
    return (lax.axis_index("dp"), ctx // 4, lax.rem(ctx, 4), lax.axis_index("tensor"))


def at(c, y, z, x):
    return (c, lax.rem(y, 4) * 4 + lax.rem(z, 4), lax.rem(x, 4))


def up(i, d):
    return lax.rem(i + d, 4)


def down(i, d):
    return lax.rem(i + 4 - d, 4)


class Net:
    def __init__(self, send_sems, recv_sems):
        self.send_sems, self.recv_sems = send_sems, recv_sems
        self.sent = []

    def send(self, src, dst, device):
        n = len(self.sent)
        copy = pltpu.make_async_remote_copy(
            src_ref=src,
            dst_ref=dst,
            send_sem=self.send_sems.at[n],
            recv_sem=self.recv_sems.at[n],
            device_id=device,
            device_id_type=MESH,
        )
        copy.start()
        self.sent.append(copy)
        return copy

    def finish(self):
        for copy in self.sent:
            copy.wait_send()


class Local:
    def __init__(self, sems):
        self.sems, self.n = sems, 0

    def copy(self, src, dst):
        copy = pltpu.make_async_copy(src, dst, self.sems.at[self.n])
        copy.start()
        self.n += 1
        return copy


def greet(peers):
    barrier = pltpu.get_barrier_semaphore()
    for peer in peers:
        pl.semaphore_signal(barrier, inc=1, device_id=peer, device_id_type=MESH)
    pl.semaphore_wait(barrier, len(peers))


def y_peers(c, y, z, x):
    return [at(c, y + d, z, x) for d in (1, 2, 3)]


def z_peers(c, y, z, x):
    return [at(c, y, z + d, x) for d in (1, 2, 3)]


def x_peers(c, y, z, x):
    return [at(c, y, z, x + d) for d in (1, 2, 3)]


def core_peer(c, y, z, x):
    return [at(1 - c, y, z, x)]


FIRST, SECOND = pl.ds(0, 32), pl.ds(32, 32)


class Gather:
    def __init__(self, net, local, src, out, me):
        self.net, self.local, self.src, self.out, self.me = net, local, src, out, me
        self.one, self.two, self.core = {}, {}, []

    def start(self):
        net, src, out = self.net, self.src, self.out
        c, y, z, x = self.me
        self.own = self.local.copy(src, out.at[c, y, z])
        for d in STEPS:
            self.one["a", d] = net.send(
                src.at[FIRST], out.at[c, y, z, FIRST], at(c, y + d, z, x)
            )
            self.one["b", d] = net.send(
                src.at[SECOND], out.at[c, y, z, SECOND], at(c, y, z + d, x)
            )
        self.core.append(net.send(src, out.at[c, y, z], at(1 - c, y, z, x)))
        for e in STEPS:
            self.two["a", 0, e] = net.send(
                src.at[FIRST], out.at[c, y, z, FIRST], at(c, y, z + e, x)
            )
            self.two["b", 0, e] = net.send(
                src.at[SECOND], out.at[c, y, z, SECOND], at(c, y + e, z, x)
            )

    def hand_over(self, piece):
        c, y, z, x = self.me
        self.core.append(self.net.send(piece, piece, at(1 - c, y, z, x)))

    def second(self):
        net, out = self.net, self.out
        c, y, z, x = self.me
        for d in STEPS:
            self.one["a", d].wait_recv()
            piece = out.at[c, down(y, d), z, FIRST]
            for e in STEPS:
                self.two["a", d, e] = net.send(piece, piece, at(c, y, z + e, x))
            self.hand_over(piece)
            self.one["b", d].wait_recv()
            piece = out.at[c, y, down(z, d), SECOND]
            for e in STEPS:
                self.two["b", d, e] = net.send(piece, piece, at(c, y + e, z, x))
            self.hand_over(piece)

    def third(self):
        c, y, z, x = self.me
        for d in (0,) + STEPS:
            for e in STEPS:
                self.two["a", d, e].wait_recv()
                self.hand_over(self.out.at[c, down(y, d), down(z, e), FIRST])
                self.two["b", d, e].wait_recv()
                self.hand_over(self.out.at[c, down(y, e), down(z, d), SECOND])

    def finish(self):
        for copy in self.core:
            copy.wait_recv()
        self.own.wait()


GATHER_COPIES = 6 + 6 + 1 + 18 + 6 + 24


def scatter_scratch(width):
    return [
        pltpu.VMEM((4, 4, 64, width), BF),
        pltpu.VMEM((4, 4, 64, width), BF),
        pltpu.VMEM((3, 4, 32, width), BF),
        pltpu.VMEM((3, 4, 32, width), BF),
        pltpu.VMEM((4, 32, width), BF),
        pltpu.VMEM((4, 32, width), BF),
        pltpu.VMEM((3, 32, width), BF),
        pltpu.VMEM((3, 32, width), BF),
    ]


SCATTER_COPIES = 1 + 6 + 6


class Scatter:
    def __init__(self, net, local, grads, out, scratch, me):
        self.net, self.local, self.grads, self.out, self.me = net, local, grads, out, me
        (self.held, self.other, self.one_a, self.one_b, self.sum_a, self.sum_b, self.two_a, self.two_b) = scratch
        self.width = grads.shape[-1]

    def start(self):
        c, y, z, x = self.me
        self.own = self.local.copy(self.grads.at[c], self.held)
        self.zero = self.net.send(self.grads.at[1 - c], self.other, at(1 - c, y, z, x))

    def first(self):
        c, y, z, x = self.me
        self.own.wait()
        self.zero.wait_recv()
        held, other = self.held, self.other

        def add(i, carry):
            for q in range(4):
                rows = pl.ds(q * 16, 16)
                held[i // 4, lax.rem(i, 4), rows, :] = (
                    held[i // 4, lax.rem(i, 4), rows, :].astype(F32)
                    + other[i // 4, lax.rem(i, 4), rows, :].astype(F32)
                ).astype(BF)
            return carry

        lax.fori_loop(0, 16, add, 0)
        self.to_a, self.to_b = {}, {}
        for e in STEPS:
            self.to_a[e] = self.net.send(
                held.at[:, up(z, e), FIRST, :], self.one_a.at[e - 1], at(c, y, z + e, x)
            )
            self.to_b[e] = self.net.send(
                held.at[up(y, e), :, SECOND, :], self.one_b.at[e - 1], at(c, y + e, z, x)
            )

    def second(self):
        c, y, z, x = self.me
        held, one_a, one_b = self.held, self.one_a, self.one_b
        for e in STEPS:
            self.to_a[e].wait_recv()

        def add_a(i, carry):
            for q in range(2):
                rows = pl.ds(q * 16, 16)
                total = held[i, z, rows, :].astype(F32)
                for n in range(3):
                    total += one_a[n, i, rows, :].astype(F32)
                self.sum_a[i, rows, :] = total.astype(BF)
            return carry

        lax.fori_loop(0, 4, add_a, 0)
        self.last_a, self.last_b = {}, {}
        for d in STEPS:
            self.last_a[d] = self.net.send(
                self.sum_a.at[up(y, d)], self.two_a.at[d - 1], at(c, y + d, z, x)
            )
        for e in STEPS:
            self.to_b[e].wait_recv()

        def add_b(i, carry):
            for q in range(2):
                rows = pl.ds(q * 16, 16)
                far = pl.ds(32 + q * 16, 16)
                total = held[y, i, far, :].astype(F32)
                for n in range(3):
                    total += one_b[n, i, rows, :].astype(F32)
                self.sum_b[i, rows, :] = total.astype(BF)
            return carry

        lax.fori_loop(0, 4, add_b, 0)
        for d in STEPS:
            self.last_b[d] = self.net.send(
                self.sum_b.at[up(z, d)], self.two_b.at[d - 1], at(c, y, z + d, x)
            )

    def third(self):
        c, y, z, x = self.me
        for d in STEPS:
            self.last_a[d].wait_recv()
            self.last_b[d].wait_recv()
        for q in range(2):
            rows = pl.ds(q * 16, 16)
            total = self.sum_a[y, rows, :].astype(F32)
            for n in range(3):
                total += self.two_a[n, rows, :].astype(F32)
            self.out[rows, :] = total
            total = self.sum_b[z, rows, :].astype(F32)
            for n in range(3):
                total += self.two_b[n, rows, :].astype(F32)
            self.out[pl.ds(32 + q * 16, 16), :] = total


class SumX:
    def __init__(self, net, local, parts, held, me):
        self.net, self.local, self.parts, self.held, self.me = net, local, parts, held, me

    def start(self):
        c, y, z, x = self.me
        self.own = self.local.copy(self.parts.at[x], self.held.at[3])
        self.copies = [
            self.net.send(self.parts.at[up(x, d)], self.held.at[d - 1], at(c, y, z, x + d))
            for d in STEPS
        ]

    def arrive(self):
        self.own.wait()
        for copy in self.copies:
            copy.wait_recv()

    def total(self, rows):
        value = self.held[3, rows, :].astype(F32)
        for n in range(3):
            value += self.held[n, rows, :].astype(F32)
        return value

    def gather(self, block, out):
        c, y, z, x = self.me
        self.mine = self.local.copy(block, out.at[x])
        self.backs = [self.net.send(block, out.at[x], at(c, y, z, x + d)) for d in STEPS]

    def finish(self):
        self.mine.wait()
        for copy in self.backs:
            copy.wait_recv()


def row_chunks(step):
    def loop(i, carry):
        step(pl.ds(pl.multiple_of(i * 16, 16), 16))
        return carry

    lax.fori_loop(0, 8, loop, 0)


def normed(values):
    centre = jnp.mean(values, axis=-1, keepdims=True)
    spread = values - centre
    inverse = lax.rsqrt(jnp.mean(spread * spread, axis=-1, keepdims=True) + EPSILON)
    return spread * inverse, inverse


def norm_pullback(upstream, norm, inverse, gain):
    scaled = upstream * gain
    first = jnp.mean(scaled, axis=-1, keepdims=True)
    second = jnp.mean(scaled * norm, axis=-1, keepdims=True)
    return inverse * (scaled - first - norm * second)


ANY = pl.BlockSpec(memory_space=pl.ANY)
IN_VMEM = pl.BlockSpec(memory_space=pltpu.VMEM)


def remote_call(body, name, cid, ins, outs, scratch, copies, locals_):
    return pl.pallas_call(
        body,
        name=name,
        in_specs=ins,
        out_specs=[spec for _, _, spec in outs],
        out_shape=[jax.ShapeDtypeStruct(shape, dtype) for shape, dtype, _ in outs],
        scratch_shapes=scratch
        + [
            pltpu.SemaphoreType.DMA((copies,)),
            pltpu.SemaphoreType.DMA((copies,)),
            pltpu.SemaphoreType.DMA((locals_,)),
        ],
        compiler_params=pltpu.CompilerParams(
            collective_id=cid, has_side_effects=True, vmem_limit_bytes=VMEM_LIMIT
        ),
    )


def gather_front(shard):
    def kernel(src, out, ss, rs, ls):
        me = here()
        greet(y_peers(*me) + z_peers(*me) + core_peer(*me))
        net, local = Net(ss, rs), Local(ls)
        gather = Gather(net, local, src, out, me)
        gather.start()
        gather.second()
        gather.third()
        gather.finish()
        net.finish()

    width = shard.shape[1]
    return remote_call(
        kernel, "gather_front", 0, [ANY], [((2, 4, 4, 64, width), BF, ANY)], [], GATHER_COPIES, 1
    )(shard)[0]


def spread_heads(qkv):
    def kernel(src, out, ss, rs, ls):
        me = here()
        c, y, z, x = me
        greet(y_peers(*me) + z_peers(*me))
        net, local = Net(ss, rs), Local(ls)
        kv = pl.ds(0, 2)
        owns = [local.copy(src.at[0, z], out.at[0, y, z]), local.copy(src.at[1, y], out.at[1, y, z])]
        first, second = {}, []
        for d in STEPS:
            first[0, d] = net.send(src.at[0, up(z, d)], out.at[0, y, z], at(c, y, z + d, x))
            first[1, d] = net.send(src.at[1, up(y, d)], out.at[1, y, z], at(c, y + d, z, x))
        for e in STEPS:
            second.append(net.send(src.at[0, z, kv], out.at[0, y, z, kv], at(c, y + e, z, x)))
            second.append(net.send(src.at[1, y, kv], out.at[1, y, z, kv], at(c, y, z + e, x)))
        for d in STEPS:
            first[0, d].wait_recv()
            piece = out.at[0, y, down(z, d), kv]
            for e in STEPS:
                second.append(net.send(piece, piece, at(c, y + e, z, x)))
            first[1, d].wait_recv()
            piece = out.at[1, down(y, d), z, kv]
            for e in STEPS:
                second.append(net.send(piece, piece, at(c, y, z + e, x)))
        for copy in second:
            copy.wait_recv()
        for copy in owns:
            copy.wait()
        net.finish()

    return remote_call(
        kernel, "spread_heads", 1, [ANY], [((2, 4, 4, 3, 256, 128), BF, ANY)], [], 6 + 6 + 18, 2
    )(qkv)[0]


def swap_rows(blocks, cid, name):
    def kernel(src, out, ss, rs, ls):
        me = here()
        c, y, z, x = me
        greet(y_peers(*me) + z_peers(*me))
        net, local = Net(ss, rs), Local(ls)
        owns = [local.copy(src.at[0, z], out.at[0, z]), local.copy(src.at[1, y], out.at[1, y])]
        copies = []
        for d in STEPS:
            copies.append(net.send(src.at[0, up(z, d)], out.at[0, z], at(c, y, z + d, x)))
            copies.append(net.send(src.at[1, up(y, d)], out.at[1, y], at(c, y + d, z, x)))
        for copy in copies:
            copy.wait_recv()
        for copy in owns:
            copy.wait()
        net.finish()

    return remote_call(kernel, name, cid, [ANY], [((2, 4, 256, 128), BF, ANY)], [], 6, 2)(blocks)[0]


def middle_forward(parts, inputs, gain, shift, shard):
    width = shard.shape[1]

    def kernel(parts, inputs, gain, shift, shard, hidden, second, weights, held, base, low, ss, rs, ls):
        me = here()
        c, y, z, x = me
        greet(y_peers(*me) + z_peers(*me) + core_peer(*me) + x_peers(*me))
        net, local = Net(ss, rs), Local(ls)
        sums = SumX(net, local, parts, held, me)
        sums.start()
        residual = local.copy(inputs.at[x], base)
        gather = Gather(net, local, shard, weights, me)
        gather.start()
        gather.second()
        residual.wait()
        sums.arrive()

        def step(rows):
            value = base[rows, :].astype(F32) + sums.total(rows)
            hidden[rows, :] = value
            norm, _ = normed(value)
            low[rows, :] = (norm * gain[...] + shift[...]).astype(BF)

        row_chunks(step)
        sums.gather(low, second)
        gather.third()
        gather.finish()
        sums.finish()
        net.finish()

    return remote_call(
        kernel,
        "middle_forward",
        3,
        [ANY, ANY, IN_VMEM, IN_VMEM, ANY],
        [
            ((128, D), F32, IN_VMEM),
            ((4, 128, D), BF, ANY),
            ((2, 4, 4, 64, width), BF, ANY),
        ],
        [pltpu.VMEM((4, 128, D), BF), pltpu.VMEM((128, D), BF), pltpu.VMEM((128, D), BF)],
        GATHER_COPIES + 6,
        4,
    )(parts, inputs, gain, shift, shard)


def middle_backward(parts, cotangent, hidden, gain, grads):
    widths = [g.shape[-1] for g in grads]
    count = len(grads)

    def kernel(parts, cotangent, hidden, gain, *rest):
        grad_refs = rest[:count]
        dhidden, hidden_low, vectors = rest[count : count + 3]
        outs = rest[count + 3 : 2 * count + 3]
        held, base, low = rest[2 * count + 3 : 2 * count + 6]
        scratch = rest[2 * count + 6 : -3]
        ss, rs, ls = rest[-3:]
        me = here()
        c, y, z, x = me
        greet(y_peers(*me) + z_peers(*me) + core_peer(*me) + x_peers(*me))
        net, local = Net(ss, rs), Local(ls)
        sums = SumX(net, local, parts, held, me)
        sums.start()
        upstream = local.copy(cotangent.at[x], base)
        scatters = [
            Scatter(net, local, grad_refs[k], outs[k], scratch[8 * k : 8 * k + 8], me)
            for k in range(count)
        ]
        for scatter in scatters:
            scatter.start()
        for scatter in scatters:
            scatter.first()
        upstream.wait()
        sums.arrive()
        vectors[...] = jnp.zeros_like(vectors)

        def step(rows):
            dsecond = sums.total(rows)
            norm, inverse = normed(hidden[rows, :])
            value = base[rows, :].astype(F32) + norm_pullback(dsecond, norm, inverse, gain[...])
            dhidden[rows, :] = value
            low[rows, :] = value.astype(BF)
            vectors[0:1, :] += jnp.sum(dsecond * norm, axis=0, keepdims=True)
            vectors[1:2, :] += jnp.sum(dsecond, axis=0, keepdims=True)

        row_chunks(step)
        sums.gather(low, hidden_low)
        for scatter in scatters:
            scatter.second()
        for scatter in scatters:
            scatter.third()
        sums.finish()
        net.finish()

    scratch = [pltpu.VMEM((4, 128, D), BF), pltpu.VMEM((128, D), BF), pltpu.VMEM((128, D), BF)]
    for width in widths:
        scratch += scatter_scratch(width)
    return remote_call(
        kernel,
        "middle_backward",
        4,
        [ANY, ANY, IN_VMEM, IN_VMEM] + [ANY] * count,
        [((128, D), F32, IN_VMEM), ((4, 128, D), BF, ANY), ((2, D), F32, IN_VMEM)]
        + [((64, width), F32, IN_VMEM) for width in widths],
        scratch,
        6 + SCATTER_COPIES * count,
        3 + count,
    )(parts, cotangent, hidden, gain, *grads)


def collect_heads(dkv, dq, parts, hidden):
    def kernel(dkv, dq, parts, hidden, dproject, outputs, got, mine, summed, held, low, ss, rs, ls):
        me = here()
        c, y, z, x = me
        greet(y_peers(*me) + z_peers(*me) + x_peers(*me))
        net, local = Net(ss, rs), Local(ls)
        kv = pl.ds(0, 2)
        one, two = {}, []
        owns = [
            local.copy(dkv.at[0, y], mine.at[0]),
            local.copy(dkv.at[1, :, z], mine.at[1]),
        ]
        for i in (1, 3, 2, 0):
            for d in STEPS:
                one[0, i, d] = net.send(
                    dkv.at[0, up(y, d), up(z, i)], got.at[0, d - 1, up(z, i)], at(c, y + d, z, x)
                )
                one[1, i, d] = net.send(
                    dkv.at[1, up(y, i), up(z, d)], got.at[1, d - 1, up(y, i)], at(c, y, z + d, x)
                )
        sums = SumX(net, local, parts, held, me)
        sums.start()
        lates = [
            local.copy(dq.at[0, z], dproject.at[0, z, 2]),
            local.copy(dq.at[1, y], dproject.at[1, y, 2]),
        ]
        for d in STEPS:
            two.append(net.send(dq.at[0, up(z, d)], dproject.at[0, z, 2], at(c, y, z + d, x)))
            two.append(net.send(dq.at[1, up(y, d)], dproject.at[1, y, 2], at(c, y + d, z, x)))
        for copy in owns:
            copy.wait()
        for i in (1, 3, 2, 0):
            for m, spot in ((0, z), (1, y)):
                for d in STEPS:
                    one[m, i, d].wait_recv()
                block = up(spot, i)

                def add(r, carry, m=m, block=block):
                    k, rows = r // 8, pl.ds(pl.multiple_of(lax.rem(r, 8) * 32, 32), 32)
                    total = mine[m, block, k, rows, :].astype(F32)
                    for n in range(3):
                        total += got[m, n, block, k, rows, :].astype(F32)
                    summed[m, block, k, rows, :] = total.astype(BF)
                    return carry

                lax.fori_loop(0, 16, add, 0)
            if i:
                two.append(
                    net.send(
                        summed.at[0, up(z, i)], dproject.at[0, z, kv], at(c, y, z + i, x)
                    )
                )
                two.append(
                    net.send(
                        summed.at[1, up(y, i)], dproject.at[1, y, kv], at(c, y + i, z, x)
                    )
                )
            else:
                lates.append(local.copy(summed.at[0, z], dproject.at[0, z, kv]))
                lates.append(local.copy(summed.at[1, y], dproject.at[1, y, kv]))
        sums.arrive()

        def step(rows):
            low[rows, :] = (hidden[rows, :] + sums.total(rows)).astype(BF)

        row_chunks(step)
        sums.gather(low, outputs)
        for copy in two:
            copy.wait_recv()
        for copy in lates:
            copy.wait()
        sums.finish()
        net.finish()

    return remote_call(
        kernel,
        "collect_heads",
        6,
        [ANY, ANY, ANY, IN_VMEM],
        [((2, 4, 3, 256, 128), BF, ANY), ((4, 128, D), BF, ANY)],
        [
            pltpu.VMEM((2, 3, 4, 2, 256, 128), BF),
            pltpu.VMEM((2, 4, 2, 256, 128), BF),
            pltpu.VMEM((2, 4, 2, 256, 128), BF),
            pltpu.VMEM((4, 128, D), BF),
            pltpu.VMEM((128, D), BF),
        ],
        24 + 6 + 6 + 6,
        8,
    )(dkv, dq, parts, hidden)


def last_backward(parts, inputs, dhidden, gain, vectors, grads):
    widths = [g.shape[-1] for g in grads]
    count = len(grads)

    def kernel(parts, inputs, dhidden, gain, vectors, *rest):
        grad_refs = rest[:count]
        input_grad, sums_out = rest[count : count + 2]
        outs = rest[count + 2 : 2 * count + 2]
        held, base, low, small, got = rest[2 * count + 2 : 2 * count + 7]
        scratch = rest[2 * count + 7 : -3]
        ss, rs, ls = rest[-3:]
        me = here()
        c, y, z, x = me
        greet(y_peers(*me) + z_peers(*me) + core_peer(*me) + x_peers(*me))
        net, local = Net(ss, rs), Local(ls)
        sums = SumX(net, local, parts, held, me)
        sums.start()
        residual = local.copy(inputs.at[x], base)
        scatters = [
            Scatter(net, local, grad_refs[k], outs[k], scratch[8 * k : 8 * k + 8], me)
            for k in range(count)
        ]
        for scatter in scatters:
            scatter.start()
        for scatter in scatters:
            scatter.first()
        residual.wait()
        sums.arrive()
        small[0, ...] = vectors[...]

        def step(rows):
            dfirst = sums.total(rows)
            norm, inverse = normed(base[rows, :].astype(F32))
            value = dhidden[rows, :] + norm_pullback(dfirst, norm, inverse, gain[...])
            low[rows, :] = value.astype(BF)
            small[0, 0:1, :] += jnp.sum(dfirst * norm, axis=0, keepdims=True)
            small[0, 1:2, :] += jnp.sum(dfirst, axis=0, keepdims=True)

        row_chunks(step)
        copies = [
            net.send(small.at[0], got.at[0, d - 1], at(c, y, z, x + d)) for d in STEPS
        ]
        sums.gather(low, input_grad)
        for scatter in scatters:
            scatter.second()
        for copy in copies:
            copy.wait_recv()
        small[1, ...] = small[0, ...]
        for n in range(3):
            small[1, 0:4, :] += got[0, n, 0:4, :]
        copies = [
            net.send(small.at[1], got.at[1, d - 1], at(c, y + d, z, x)) for d in STEPS
        ]
        for copy in copies:
            copy.wait_recv()
        small[2, ...] = small[1, ...] + got[1, 0] + got[1, 1] + got[1, 2]
        copies = [
            net.send(small.at[2], got.at[2, d - 1], at(c, y, z + d, x)) for d in STEPS
        ]
        for copy in copies:
            copy.wait_recv()
        small[3, ...] = small[2, ...] + got[2, 0] + got[2, 1] + got[2, 2]
        copy = net.send(small.at[3], got.at[3, 0], at(1 - c, y, z, x))
        for scatter in scatters:
            scatter.third()
        copy.wait_recv()
        sums_out[...] = small[3, ...] + got[3, 0]
        sums.finish()
        net.finish()

    scratch = [
        pltpu.VMEM((4, 128, D), BF),
        pltpu.VMEM((128, D), BF),
        pltpu.VMEM((128, D), BF),
        pltpu.VMEM((4, 8, D), F32),
        pltpu.VMEM((4, 3, 8, D), F32),
    ]
    for width in widths:
        scratch += scatter_scratch(width)
    return remote_call(
        kernel,
        "last_backward",
        7,
        [ANY, ANY, IN_VMEM, IN_VMEM, IN_VMEM] + [ANY] * count,
        [((4, 128, D), BF, ANY), ((8, D), F32, IN_VMEM)]
        + [((64, width), F32, IN_VMEM) for width in widths],
        scratch,
        6 + 10 + SCATTER_COPIES * count,
        3 + count,
    )(parts, inputs, dhidden, gain, vectors, *grads)


def turn(values, cosine, minus_sine, plus_sine):
    return (
        values * cosine
        + pltpu.roll(values, 120, 1) * minus_sine
        + pltpu.roll(values, 8, 1) * plus_sine
    )


def project_heads(tokens, gain, shift, weights, bias, tables):
    def kernel(x_ref, gain_ref, shift_ref, w_ref, b_ref, t_ref, out_ref, low_ref):
        j = pl.program_id(0)

        @pl.when(j == 0)
        def _():
            def step(i, carry):
                rows = pl.ds(pl.multiple_of(i * 16, 16), 16)
                norm, _ = normed(x_ref[rows, :].astype(F32))
                low_ref[rows, :] = (norm * gain_ref[...] + shift_ref[...]).astype(BF)
                return carry

            lax.fori_loop(0, 32, step, 0)

        for m in range(2):
            acc = jnp.dot(low_ref[m * 256 : m * 256 + 256, :], w_ref[...], preferred_element_type=F32)
            acc = acc + b_ref[0]
            for h in range(2):
                part = acc[:, h * 128 : h * 128 + 128]

                @pl.when(j < 4)
                def _():
                    out_ref[m, h, 0] = turn(part, t_ref[0], t_ref[1], t_ref[2]).astype(BF)

                @pl.when(j >= 4)
                def _():
                    out_ref[m, h, 0] = part.astype(BF)

    return pl.pallas_call(
        kernel,
        name="project_heads",
        grid=(6,),
        in_specs=[
            pl.BlockSpec((512, D), lambda j: (0, 0)),
            pl.BlockSpec((1, D), lambda j: (0, 0)),
            pl.BlockSpec((1, D), lambda j: (0, 0)),
            pl.BlockSpec((D, 256), lambda j: (0, j)),
            pl.BlockSpec((1, 1, 256), lambda j: (j, 0, 0)),
            pl.BlockSpec((3, 256, 128), lambda j: (0, 0, 0)),
        ],
        out_specs=[
            pl.BlockSpec((2, 2, 1, 256, 128), lambda j: (0, j % 2, (j // 2 + 2) % 3, 0, 0)),
            pl.BlockSpec((512, D), lambda j: (0, 0)),
        ],
        out_shape=[
            jax.ShapeDtypeStruct((2, 4, 3, 256, 128), BF),
            jax.ShapeDtypeStruct((512, D), BF),
        ],
        compiler_params=pltpu.CompilerParams(vmem_limit_bytes=VMEM_LIMIT),
    )(tokens, gain, shift, weights, bias, tables)


def two_heads(block):
    lane = lax.broadcasted_iota(jnp.int32, (128, 128), 1)
    value = block.astype(F32)
    return jnp.concatenate(
        [jnp.where(lane < HEAD_DIM, value, 0.0), jnp.where(lane >= HEAD_DIM, value, 0.0)], axis=0
    )


def one_block(stacked):
    feature = lax.broadcasted_iota(jnp.int32, (128, 128), 0)
    return jnp.where(feature < HEAD_DIM, stacked[:, :128], stacked[:, 128:]).T


def nt(left, right):
    return lax.dot_general(left, right, (((1,), (1,)), ((), ())), preferred_element_type=F32)


def masked_places(tile, place):
    key = tile * TILE + lax.broadcasted_iota(jnp.int32, (TILE, 256), 0)
    query = place * 128 + lax.rem(lax.broadcasted_iota(jnp.int32, (TILE, 256), 1), 128)
    return key <= query


def attend(slots, places, rows_of, spread):
    def kernel(slots, places, rows_of, k_ref, v_ref, q_ref, o_ref, full_ref, log_ref, keys, values_t):
        m, i = pl.program_id(0), pl.program_id(1)

        @pl.when(i == 0)
        def _():
            def lay(b, carry):
                slot = slots[b]
                rows = pl.ds(pl.multiple_of(lax.rem(slot, 2) * 128, 128), 128)
                to = pl.ds(pl.multiple_of(b * 128, 128), 128)
                keys[to, :] = k_ref[0, slot // 2, 0, rows, :]
                values_t[:, to] = v_ref[0, slot // 2, 0, rows, :].astype(F32).T.astype(BF)
                return carry

            lax.fori_loop(0, 32, lay, 0)

        for half in range(2):
            place = places[(m * 4 + i) * 2 + half]
            query = (two_heads(q_ref[0, 0, 0, half * 128 : half * 128 + 128, :]) * 0.125).astype(BF)

            def step(t, carry, masked):
                top, total, acc = carry
                span = pl.ds(pl.multiple_of(t * TILE, TILE), TILE)
                scores = nt(keys[span, :], query) * LOG2E
                if masked:
                    scores = jnp.where(masked_places(t, place), scores, LOW)
                new_top = jnp.maximum(top, jnp.max(scores, axis=0, keepdims=True))
                weights = jnp.exp2(scores - new_top)
                shrink = jnp.exp2(top - new_top)
                total = total * shrink + jnp.sum(weights, axis=0, keepdims=True)
                acc = acc * shrink + jnp.dot(
                    values_t[:, span], weights.astype(BF), preferred_element_type=F32
                )
                return new_top, total, acc

            carry = (
                jnp.full((1, 256), LOW, F32),
                jnp.zeros((1, 256), F32),
                jnp.zeros((128, 256), F32),
            )
            last = place // (TILE // 128)
            carry = lax.fori_loop(0, last, lambda t, s: step(t, s, False), carry)
            top, total, acc = step(last, carry, True)
            result = one_block(acc / total)
            full_ref[0, 0, half * 128 : half * 128 + 128, :] = result
            o_ref[0, 0, half * 128 : half * 128 + 128, :] = result.astype(BF)
            log_ref[0, 0, half : half + 1, :] = top + jnp.log2(total)

    grid_spec = pltpu.PrefetchScalarGridSpec(
        num_scalar_prefetch=3,
        grid=(2, 4),
        in_specs=[
            pl.BlockSpec((1, 16, 1, 256, 128), lambda m, i, s, p, r: (m, 0, 0, 0, 0)),
            pl.BlockSpec((1, 16, 1, 256, 128), lambda m, i, s, p, r: (m, 0, 1, 0, 0)),
            pl.BlockSpec((1, 1, 1, 256, 128), lambda m, i, s, p, r: (m, r[m * 4 + i], 2, 0, 0)),
        ],
        out_specs=[
            pl.BlockSpec((1, 1, 256, 128), lambda m, i, s, p, r: (m, i, 0, 0)),
            pl.BlockSpec((1, 1, 256, 128), lambda m, i, s, p, r: (m, i, 0, 0)),
            pl.BlockSpec((1, 1, 2, 256), lambda m, i, s, p, r: (m, i, 0, 0)),
        ],
        scratch_shapes=[pltpu.VMEM((4096, 128), BF), pltpu.VMEM((128, 4096), BF)],
    )
    return pl.pallas_call(
        kernel,
        name="attend",
        grid_spec=grid_spec,
        out_shape=[
            jax.ShapeDtypeStruct((2, 4, 256, 128), BF),
            jax.ShapeDtypeStruct((2, 4, 256, 128), F32),
            jax.ShapeDtypeStruct((2, 4, 2, 256), F32),
        ],
        compiler_params=pltpu.CompilerParams(vmem_limit_bytes=VMEM_LIMIT),
    )(slots, places, rows_of, spread, spread, spread)


def attend_back(slots, places, rows_of, spread, full, logs, upstream, tables):
    def kernel(
        slots, places, rows_of, k_ref, v_ref, q_ref, full_ref, log_ref, up_ref, t_ref, dq_ref, dkv_ref,
        keys, keys_t, values, dkeys, dvalues,
    ):
        m, i = pl.program_id(0), pl.program_id(1)

        @pl.when(i == 0)
        def _():
            def lay(b, carry):
                slot = slots[b]
                rows = pl.ds(pl.multiple_of(lax.rem(slot, 2) * 128, 128), 128)
                to = pl.ds(pl.multiple_of(b * 128, 128), 128)
                keys[to, :] = k_ref[0, slot // 2, 0, rows, :]
                keys_t[:, to] = k_ref[0, slot // 2, 0, rows, :].astype(F32).T.astype(BF)
                values[to, :] = v_ref[0, slot // 2, 0, rows, :]
                dkeys[to, :] = jnp.zeros((128, 128), F32)
                dvalues[to, :] = jnp.zeros((128, 128), F32)
                return carry

            lax.fori_loop(0, 32, lay, 0)

        for half in range(2):
            rows = slice(half * 128, half * 128 + 128)
            place = places[(m * 4 + i) * 2 + half]
            query = (two_heads(q_ref[0, 0, 0, rows, :]) * 0.125).astype(BF)
            ups = up_ref[0, 0, rows, :]
            grad = two_heads(ups).astype(BF)
            product = (ups.astype(F32) * full_ref[0, 0, rows, :]).T
            delta = jnp.concatenate(
                [
                    jnp.sum(product[:HEAD_DIM], axis=0, keepdims=True),
                    jnp.sum(product[HEAD_DIM:], axis=0, keepdims=True),
                ],
                axis=1,
            )
            logs = log_ref[0, 0, half : half + 1, :]

            def step(t, dquery, masked):
                span = pl.ds(pl.multiple_of(t * TILE, TILE), TILE)
                scores = nt(keys[span, :], query) * LOG2E
                probs = jnp.exp2(scores - logs)
                if masked:
                    probs = jnp.where(masked_places(t, place), probs, 0.0)
                dprobs = nt(values[span, :], grad)
                dscores = (probs * (dprobs - delta)).astype(BF)
                dvalues[span, :] += jnp.dot(probs.astype(BF), grad, preferred_element_type=F32)
                dkeys[span, :] += jnp.dot(dscores, query, preferred_element_type=F32)
                return dquery + jnp.dot(keys_t[:, span], dscores, preferred_element_type=F32)

            last = place // (TILE // 128)
            dquery = lax.fori_loop(
                0, last, lambda t, s: step(t, s, False), jnp.zeros((128, 256), F32)
            )
            dquery = one_block(step(last, dquery, True)) * 0.125
            own = pl.ds(pl.multiple_of(place * 128, 128), 128)
            dq_ref[0, 0, rows, :] = turn(
                dquery, t_ref[0, own, :], -t_ref[1, own, :], -t_ref[2, own, :]
            ).astype(BF)

        @pl.when(i == 3)
        def _():
            def flush(b, carry):
                slot = slots[b]
                rows = pl.ds(pl.multiple_of(lax.rem(slot, 2) * 128, 128), 128)
                to = pl.ds(pl.multiple_of(b * 128, 128), 128)
                dkv_ref[0, slot // 2, 0, rows, :] = turn(
                    dkeys[to, :], t_ref[0, to, :], -t_ref[1, to, :], -t_ref[2, to, :]
                ).astype(BF)
                dkv_ref[0, slot // 2, 1, rows, :] = dvalues[to, :].astype(BF)
                return carry

            lax.fori_loop(0, 32, flush, 0)

    grid_spec = pltpu.PrefetchScalarGridSpec(
        num_scalar_prefetch=3,
        grid=(2, 4),
        in_specs=[
            pl.BlockSpec((1, 16, 1, 256, 128), lambda m, i, s, p, r: (m, 0, 0, 0, 0)),
            pl.BlockSpec((1, 16, 1, 256, 128), lambda m, i, s, p, r: (m, 0, 1, 0, 0)),
            pl.BlockSpec((1, 1, 1, 256, 128), lambda m, i, s, p, r: (m, r[m * 4 + i], 2, 0, 0)),
            pl.BlockSpec((1, 1, 256, 128), lambda m, i, s, p, r: (m, i, 0, 0)),
            pl.BlockSpec((1, 1, 2, 256), lambda m, i, s, p, r: (m, i, 0, 0)),
            pl.BlockSpec((1, 1, 256, 128), lambda m, i, s, p, r: (m, i, 0, 0)),
            pl.BlockSpec((3, 4096, 128), lambda m, i, s, p, r: (0, 0, 0)),
        ],
        out_specs=[
            pl.BlockSpec((1, 1, 256, 128), lambda m, i, s, p, r: (m, i, 0, 0)),
            pl.BlockSpec((1, 16, 2, 256, 128), lambda m, i, s, p, r: (m, 0, 0, 0, 0)),
        ],
        scratch_shapes=[
            pltpu.VMEM((4096, 128), BF),
            pltpu.VMEM((128, 4096), BF),
            pltpu.VMEM((4096, 128), BF),
            pltpu.VMEM((4096, 128), F32),
            pltpu.VMEM((4096, 128), F32),
        ],
    )
    return pl.pallas_call(
        kernel,
        name="attend_back",
        grid_spec=grid_spec,
        out_shape=[
            jax.ShapeDtypeStruct((2, 4, 256, 128), BF),
            jax.ShapeDtypeStruct((2, 16, 2, 256, 128), BF),
        ],
        compiler_params=pltpu.CompilerParams(vmem_limit_bytes=VMEM_LIMIT),
    )(slots, places, rows_of, spread, spread, spread, full, logs, upstream, tables)


def rotary_tables(places):
    frequency = 10000.0 ** (-jnp.arange(0, ROT, 2, dtype=F32) / ROT)
    angles = places.astype(F32)[:, None] * frequency[None, :]
    cosine, sine = jnp.cos(angles), jnp.sin(angles)
    rows, half = places.shape[0], ROT // 2
    rest = HEAD_DIM - ROT
    zeros, ones = jnp.zeros((rows, half), F32), jnp.ones((rows, rest), F32)
    tables = (
        jnp.concatenate([cosine, cosine, ones], axis=1),
        jnp.concatenate([-sine, zeros, 0.0 * ones], axis=1),
        jnp.concatenate([zeros, sine, 0.0 * ones], axis=1),
    )
    return jnp.stack([jnp.concatenate([t, t], axis=1) for t in tables])


def body(
    inputs,
    cotangent,
    group_place,
    attend_gain,
    attend_shift,
    project_weight,
    project_bias,
    output_weight,
    mixer_gain,
    mixer_shift,
    gate_weight,
    up_weight,
    down_weight,
):
    ctx = lax.axis_index("ctx")
    y, z = ctx // 4, lax.rem(ctx, 4)
    shard_index = lax.axis_index("dp") * 16 + ctx

    blocks = jnp.arange(32, dtype=jnp.int32)
    hits = group_place[None, :] == blocks[:, None]
    slots = jnp.sum(jnp.where(hits, blocks[None, :], 0), axis=1)
    four = jnp.arange(4, dtype=jnp.int32)
    rows_of = jnp.concatenate([y * 4 + four, four * 4 + z])
    held_slots = (rows_of[:, None] * 2 + jnp.arange(2, dtype=jnp.int32)[None, :]).reshape(16)
    chosen = held_slots[:, None] == blocks[None, :]
    places = jnp.sum(jnp.where(chosen, group_place[None, :], 0), axis=1)
    own_slots = ctx * 2 + jnp.arange(2, dtype=jnp.int32)
    own_blocks = jnp.sum(
        jnp.where(own_slots[:, None] == blocks[None, :], group_place[None, :], 0), axis=1
    )
    own_places = (own_blocks[:, None] * 128 + jnp.arange(128, dtype=jnp.int32)[None, :]).reshape(256)
    own_tables = rotary_tables(own_places)
    all_tables = rotary_tables(jnp.arange(4096, dtype=jnp.int32))

    vectors = jnp.concatenate(
        [
            jnp.stack([attend_gain, attend_shift, mixer_gain, mixer_shift], axis=1),
            jnp.pad(project_bias.reshape(1, 48), ((0, 63), (0, 0))),
            jnp.zeros((64, 76), BF),
        ],
        axis=1,
    )
    front_shard = jnp.concatenate(
        [project_weight.reshape(64, 1536), output_weight.T, vectors], axis=1
    )
    back_shard = jnp.concatenate([gate_weight, up_weight, down_weight.T], axis=1)
    front = gather_front(front_shard).reshape(D, 2176)
    gains = front[:, 2048:2052].astype(F32).T
    first_gain, first_shift = gains[0:1], gains[1:2]
    second_gain, second_shift = gains[2:3], gains[3:4]
    bias = (
        front.reshape(32, 64, 2176)[:, 0, 2052:2100]
        .reshape(32, 3, 8, 2)
        .transpose(1, 2, 0, 3)
        .astype(F32)
        .reshape(6, 1, 256)
    )
    output_t = front[:, 1536:2048]
    project_flat = front[:, :1536]

    tokens = inputs.reshape(512, D)
    quarters = inputs.reshape(4, 128, D)
    qkv, first_low = project_heads(tokens, first_gain, first_shift, front, bias, own_tables)
    spread = spread_heads(qkv).reshape(2, 16, 3, 256, 128)
    attended_heads, attended_full, logs = attend(slots, places, rows_of, spread)
    attended_low = (
        swap_rows(attended_heads, 2, "attended_back").transpose(0, 2, 1, 3).reshape(512, 512)
    )
    branch = nt(attended_low, output_t).astype(BF).reshape(4, 128, D)
    hidden, second_low, back = middle_forward(branch, quarters, second_gain, second_shift, back_shard)

    second_low = second_low.reshape(512, D)
    back = back.reshape(D, 3 * UNITS)
    gate_w, up_w, down_t = back[:, :UNITS], back[:, UNITS : 2 * UNITS], back[:, 2 * UNITS :]
    dy = cotangent.reshape(512, D)
    gate_value = jnp.dot(second_low, gate_w, preferred_element_type=F32)
    up_value = jnp.dot(second_low, up_w, preferred_element_type=F32)
    dmixed = jnp.dot(dy, down_t, preferred_element_type=F32)
    sigmoid = jax.nn.sigmoid(gate_value)
    mixed = (gate_value * sigmoid * up_value).astype(BF)
    dgate = (dmixed * up_value * sigmoid * (1.0 + gate_value * (1.0 - sigmoid))).astype(BF)
    dup = (dmixed * gate_value * sigmoid).astype(BF)
    mixer_part = nt(mixed, down_t).astype(BF).reshape(4, 128, D)
    second_part = (nt(dgate, gate_w) + nt(dup, up_w)).astype(BF).reshape(4, 128, D)

    def tn(left, right):
        return lax.dot_general(left, right, (((0,), (0,)), ((), ())), preferred_element_type=F32)

    def shards(grad):
        return grad.astype(BF).reshape(2, 4, 4, 64, grad.shape[1])

    dhidden, hidden_low, mixer_vectors, gate_grad, up_grad, down_grad = middle_backward(
        second_part,
        cotangent.reshape(4, 128, D),
        hidden,
        second_gain,
        [shards(tn(second_low, dgate)), shards(tn(second_low, dup)), shards(tn(dy, mixed))],
    )

    hidden_low = hidden_low.reshape(512, D)
    dattended = jnp.dot(hidden_low, output_t, preferred_element_type=F32).astype(BF)
    upstream = swap_rows(
        dattended.reshape(2, 256, 4, 128).transpose(0, 2, 1, 3), 5, "dattended_out"
    )
    output_grad = shards(tn(hidden_low, attended_low))
    dq, dkv = attend_back(
        slots, places, rows_of, spread, attended_full, logs, upstream, all_tables
    )
    dproject, outputs = collect_heads(dkv.reshape(2, 4, 4, 2, 256, 128), dq, mixer_part, hidden)
    ordered = jnp.concatenate([dproject[:, :, 2:], dproject[:, :, :2]], axis=2)
    dproject = ordered.transpose(0, 3, 2, 1, 4).reshape(512, 1536)
    first_part = nt(dproject, project_flat).astype(BF).reshape(4, 128, D)
    project_grad = shards(tn(first_low, dproject))
    bias_part = jnp.sum(dproject.astype(F32), axis=0)
    small = jnp.concatenate(
        [
            jnp.zeros((2, D), F32),
            mixer_vectors,
            jnp.pad(bias_part, (0, D - 1536))[None],
            jnp.zeros((3, D), F32),
        ]
    )
    input_grad, small, project_grad, output_grad = last_backward(
        first_part, quarters, dhidden, first_gain, small, [project_grad, output_grad]
    )
    own = lax.dynamic_slice(small, (0, shard_index * 64), (4, 64))
    bias_grad = lax.dynamic_slice(
        small[4, :1536].reshape(3, 8, 64), (0, 0, shard_index * 2), (3, 8, 2)
    )
    shape = inputs.shape
    return (
        outputs.reshape(shape),
        input_grad.reshape(shape),
        own[0],
        own[1],
        project_grad.reshape(64, 3, 512),
        bias_grad,
        output_grad.T,
        own[2],
        own[3],
        gate_grad,
        up_grad,
        down_grad.T,
    )


def solution(mesh):
    weight = ("dp", "ctx")
    rows = P(None, "dp", "ctx", None)
    vector = P(weight)
    matrix = P(weight, "tensor")
    turned = P("tensor", weight)
    project = P(weight, None, "tensor")
    bias = P(None, "tensor", weight)
    params = (vector, vector, project, bias, turned, vector, vector, matrix, matrix, turned)
    return jax.shard_map(
        body,
        mesh=mesh,
        in_specs=(rows, rows, P()) + params,
        out_specs=(rows, rows) + params,
        check_vma=False,
    )
```

time: 1690 us -> 660 us (0.39)
  waiting for transfers between devices: 867 us -> 0 us
  Pallas kernels: 0 us -> 472 us
  blocking collectives: 323 us -> 0 us
  matrix products: 309 us -> 86.9 us
  other arithmetic: 98.2 us -> 23.8 us
    pallas_call x0 -> x11, Pallas kernels: none -> 472 us  [the longest x1 71.9 us: middle_backward(): remote_call(kernel, 'middle_backward', 4, [ANY, ANY, IN_VMEM, IN_VMEM] +...]
    reduce_scatter x7 -> x0, waiting for transfers between devices: 341 us -> none  [the longest x1 87.3 us: body(): lax.psum_scatter(totals[8].astype(jnp.bfloat16), ('dp', 'ctx'), scatter_d...]
    all_gather x9 -> x0, waiting for transfers between devices: 286 us -> none  [the longest x2 103 us: forward_pass(): key_piece = lax.all_gather(key_heads, 'ctx', axis=1, tiled=True)]
    unnamed x2 -> x0, blocking collectives: 262 us -> none
    psum x4 -> x0, waiting for transfers between devices: 236 us -> none  [the longest x1 92.4 us: forward_pass(): lax.psum(mixer_part.astype(jnp.bfloat16), 'tensor').astype(jnp.float32)]
    dot_general x42 -> x14, matrix products: 309 us -> 86.9 us  [the longest x5 31 us: nt(): lax.dot_general(left, right, (((1,), (1,)), ((), ())), preferred_element_...]
    all_gather x1 -> x0, blocking collectives: 61.5 us -> none  [gather_weights(): lax.all_gather(shards[3], ('dp', 'ctx'), axis=2, tiled=True)]
    reduce_sum x13 -> x4, other arithmetic: 51.8 us -> 3.7 us  [the longest x1 1.36 us: body(): places = jnp.sum(jnp.where(chosen, group_place[None, :], 0), axis=1)]
  transfers between devices with their start and end apart: 20 -> 0, of which waited for: 16 -> 0; matrix products, arithmetic and copies ran while one was open for 18% -> 0% of each run, Pallas kernels for 0% -> 0%
where the time goes in v1:
time: 660 us; the launch traced here: 649 us
  Pallas kernels  472 us (72%)
  matrix products  86.9 us (13%)
  local copies, waits for them, and re-layouts  64.9 us (10%)
  other arithmetic  23.8 us (4%)
    pallas_call x1, Pallas kernels, middle_backward(): remote_call(kernel, 'middle_backward', 4, [ANY, ANY, IN_VMEM, IN_VMEM] +...  71.9 us
    pallas_call x1, Pallas kernels, middle_forward(): remote_call(kernel, 'middle_forward', 3, [ANY, ANY, IN_VMEM, IN_VMEM, ANY...  69.7 us
    pallas_call x1, Pallas kernels, last_backward(): remote_call(kernel, 'last_backward', 7, [ANY, ANY, IN_VMEM, IN_VMEM, IN_V...  60.5 us
    pallas_call x1, Pallas kernels, attend_back(): pl.pallas_call(kernel, name='attend_back', grid_spec=grid_spec, out_shape...  58.2 us
    pallas_call x1, Pallas kernels, attend(): pl.pallas_call(kernel, name='attend', grid_spec=grid_spec, out_shape=[jax...  50.2 us
    pallas_call x1, Pallas kernels, collect_heads(): remote_call(kernel, 'collect_heads', 6, [ANY, ANY, ANY, IN_VMEM], [((2, 4...  49.3 us
    pallas_call x1, Pallas kernels, gather_front(): remote_call(kernel, 'gather_front', 0, [ANY], [((2, 4, 4, 64, width), BF,...  42.7 us
    pallas_call x1, Pallas kernels, spread_heads(): remote_call(kernel, 'spread_heads', 1, [ANY], [((2, 4, 4, 3, 256, 128), B...  35.8 us

profile of v1, /device:TPU:1, one launch (start us, length us, event | category | flops | bytes accessed | tf_op | source)
XLA Modules:
  0.0 648.9 jit_solution(18213324538872159172)
XLA Ops:
  14.6 9.3 %multiply_cosine_fusion = (f32[4096,8]{1,0:T(8,128)S(1)}, f32[4096,8]{1,0:T(8,128)}, f32[4096,8]{1,0:T(8,128)}) fusion(f32[4096]{0:T(1024)S(1)} %iota_convert_fusion, f32[8]{0:T(128)S(1)} %multiply_power_fusion), kind=kLoop, calls=%fused_computation.24 | loop fusion | flops 65536 | bytes 409632 | tf_op jit(solution)/shard_map/cos | solution.py:992
  25.4 7.6 %concatenate.55 = f32[4096,128]{1,0:T(8,128)} concatenate(f32[4096,8]{1,0:T(8,128)S(1)} %get-tuple-element.137, f32[4096,8]{1,0:T(8,128)S(1)} %get-tuple-element.137, f32[4096,48]{1,0:T(8,128)} %broadcast_in_dim.85, f32[4096,8]{1,0:T(8,128)S(1)} %get-tuple-element.137, f32[4096,8]{1,0:T(8,128)S(1)} %get-tuple-element.137, f32[4096,48]{1,0:T(8,128)} %broadcast_in_dim.85), dimensions={1} | concatenate | bytes 4194304 | tf_op jit(solution)/shard_map/concatenate | solution.py:1001
  34.6 8.8 %concatenate.56 = f32[4096,128]{1,0:T(8,128)} concatenate(f32[4096,8]{1,0:T(8,128)} %get-tuple-element.138, f32[4096,8]{1,0:T(8,128)} %broadcast_in_dim.86, f32[4096,48]{1,0:T(8,128)S(1)} %broadcast.80, f32[4096,8]{1,0:T(8,128)} %get-tuple-element.138, f32[4096,8]{1,0:T(8,128)} %broadcast_in_dim.86, f32[4096,48]{1,0:T(8,128)S(1)} %broadcast.80), dimensions={1} | concatenate | bytes 4194304 | tf_op jit(solution)/shard_map/concatenate | solution.py:1001
  43.5 8.5 %concatenate.57 = f32[4096,128]{1,0:T(8,128)} concatenate(f32[4096,8]{1,0:T(8,128)} %broadcast_in_dim.86, f32[4096,8]{1,0:T(8,128)} %get-tuple-element.139, f32[4096,48]{1,0:T(8,128)S(1)} %broadcast.80, f32[4096,8]{1,0:T(8,128)} %broadcast_in_dim.86, f32[4096,8]{1,0:T(8,128)} %get-tuple-element.139, f32[4096,48]{1,0:T(8,128)S(1)} %broadcast.80), dimensions={1} | concatenate | bytes 4194304 | tf_op jit(solution)/shard_map/concatenate | solution.py:1001
  51.9 5.9 pad_maximum_fusion.t_ref
  57.9 42.7 %gather_front.1 = bf16[2,4,4,64,2176]{4,3,2,1,0:T(8,128)(2,1)} custom-call(bf16[64,2176]{1,0:T(8,128)(2,1)} %concatenate.50.src), custom_call_target="tpu_custom_call" | custom-call | tf_op jit(solution)/shard_map/gather_front/pallas_call | solution.py:366
  104.7 21.2 %project_heads.1 = (bf16[2,4,3,256,128]{4,3,2,1,0:T(8,128)(2,1)}, bf16[512,2048]{1,0:T(8,128)(2,1)}) custom-call(bf16[512,2048]{1,0:T(8,128)(2,1)} %bitcast.115, f32[1,2048]{1,0:T(1,128)} %get-tuple-element.136.gain_ref.gain, f32[1,2048]{1,0:T(1,128)} %get-tuple-element.135.shift_ref, bf16[2048,2176]{1,0:T(8,128)(2,1)} %bitcast.110, ...), custom_call_target="tpu_custom_call" | custom-call | tf_op jit(solution)/shard_map/project_heads/pallas_call | solution.py:756
  126.0 35.8 %spread_heads.1 = bf16[2,4,4,3,256,128]{5,4,3,2,1,0:T(8,128)(2,1)} custom-call(bf16[2,4,3,256,128]{4,3,2,1,0:T(8,128)(2,1)} %get-tuple-element.34.src), custom_call_target="tpu_custom_call" | custom-call | tf_op jit(solution)/shard_map/spread_heads/pallas_call | solution.py:401
  161.8 50.2 %attend.1 = (bf16[2,4,256,128]{3,2,1,0:T(8,128)(2,1)}, f32[2,4,256,128]{3,2,1,0:T(8,128)}, f32[2,4,2,256]{3,2,1,0:T(2,128)}) custom-call(s32[32]{0:T(128)} %select_reduce_fusion.slots, s32[16]{0:T(128)} %select_reduce_fusion.1.places, s32[8]{0:T(128)} %get-tuple-element.129.rows_of, bf16[2,16,3,256,128]{4,3,2,1,0:T(8,128)(2,1)} %bitcast.102, ...), custom_call_target="tpu_custom_call" | custom-call | tf_op jit(solution)/shard_map/attend/pallas_call | solution.py:866
  212.0 6.1 attended_back.1
  223.7 69.7 %middle_forward.1 = (f32[128,2048]{1,0:T(8,128)}, bf16[4,128,2048]{2,1,0:T(8,128)(2,1)}, bf16[2,4,4,64,4224]{4,3,2,1,0:T(8,128)(2,1)}) custom-call(bf16[4,128,2048]{2,1,0:T(8,128)(2,1)} %bitcast.129, bf16[4,128,2048]{2,1,0:T(8,128)(2,1)} %bitcast.116, f32[1,2048]{1,0:T(1,128)} %get-tuple-element.134.gain, f32[1,2048]{1,0:T(1,128)} %get-tuple-element.133.shift, ...), custom_call_target="tpu_custom_call" | custom-call | tf_op jit(solution)/shard_map/middle_forward/pallas_call | solution.py:456
  293.4 8.2 %fusion.5 = f32[512,1408]{0,1:T(8,128)} fusion(bf16[512,2048]{1,0:T(8,128)(2,1)} %bitcast.165, bf16[2048,4224]{1,0:T(8,128)(2,1)} %bitcast.157), kind=kOutput, calls=%fused_computation.10 | convolution fusion | flops 2952790016 | bytes 10747904 | tf_op jit(solution)/shard_map/dot_general | solution.py:1080
  301.6 7.6 %fusion.15 = f32[512,1408]{0,1:T(8,128)} fusion(bf16[512,2048]{1,0:T(8,128)(2,1)S(1)} %bitcast.126, bf16[2048,4224]{1,0:T(8,128)(2,1)} %bitcast.158), kind=kOutput, calls=%fused_computation.21 | convolution fusion | flops 2952790016 | bytes 10747904 | tf_op jit(solution)/shard_map/dot_general | solution.py:1082
  309.2 11.1 %multiply_convert_fusion = (bf16[512,1408]{0,1:T(8,128)(2,1)}, bf16[512,1408]{0,1:T(8,128)(2,1)}, bf16[512,1408]{0,1:T(8,128)(2,1)}) fusion(f32[512,1408]{0,1:T(8,128)} %fusion.5, f32[512,1408]{0,1:T(8,128)} %fusion.15, bf16[512,2048]{1,0:T(8,128)(2,1)S(1)} %bitcast.166, bf16[2048,4224]{1,0:T(8,128)(2,1)} %bitcast.159), kind=kOutput, calls=%fused_computation.29 | convolution fusion | flops 2964324352 | bytes 17956864 | tf_op jit(solution)/shard_map/dot_general | solution.py:1081
  320.3 8.1 %fusion.23 = bf16[512,2048]{1,0:T(8,128)(2,1)} fusion(bf16[512,1408]{0,1:T(8,128)(2,1)} %get-tuple-element.130, bf16[2048,4224]{1,0:T(8,128)(2,1)} %bitcast.160), kind=kOutput, calls=%fused_computation.28 | convolution fusion | flops 2953838592 | bytes 9306112 | tf_op jit(solution)/shard_map/dot_general | solution.py:794
  333.5 6.3 add_convert_fusion
  355.3 8.5 %copy.160 = bf16[2048,1408]{1,0:T(8,128)(2,1)} copy(bf16[2048,1408]{0,1:T(8,128)(2,1)} %fusion) | data formatting | bytes 11534336 | tf_op jit(solution)/shard_map/convert_element_type | solution.py:1094
  363.8 71.9 %middle_backward.1 = (f32[128,2048]{1,0:T(8,128)}, bf16[4,128,2048]{2,1,0:T(8,128)(2,1)}, f32[2,2048]{1,0:T(2,128)}, f32[64,1408]{1,0:T(8,128)}, f32[64,1408]{1,0:T(8,128)}, /*index=5*/f32[64,1408]{1,0:T(8,128)}) custom-call(bf16[4,128,2048]{2,1,0:T(8,128)(2,1)} %bitcast.128, bf16[4,128,2048]{2,1,0:T(8,128)(2,1)} %bitcast.125, ...), custom_call_target="tpu_custom_call" | custom-call | tf_op jit(solution)/shard_map/middle_backward/pallas_call | solution.py:523
  443.0 6.3 dattended_out.1.up_ref
  449.3 58.2 %attend_back.1 = (bf16[2,4,256,128]{3,2,1,0:T(8,128)(2,1)}, bf16[2,16,2,256,128]{4,3,2,1,0:T(8,128)(2,1)}) custom-call(s32[32]{0:T(128)} %select_reduce_fusion.slots, s32[16]{0:T(128)} %select_reduce_fusion.1.places, s32[8]{0:T(128)} %get-tuple-element.129.rows_of, bf16[2,16,3,256,128]{4,3,2,1,0:T(8,128)(2,1)} %bitcast.105, ...), custom_call_target="tpu_custom_call" | custom-call | tf_op jit(solution)/shard_map/attend_back/pallas_call | solution.py:977
  507.5 49.3 %collect_heads.1 = (bf16[2,4,3,256,128]{4,3,2,1,0:T(8,128)(2,1)}, bf16[4,128,2048]{2,1,0:T(8,128)(2,1)}) custom-call(bf16[2,4,4,2,256,128]{5,4,3,2,1,0:T(8,128)(2,1)} %bitcast.124, bf16[2,4,256,128]{3,2,1,0:T(8,128)(2,1)} %get-tuple-element.43.dq, bf16[4,128,2048]{2,1,0:T(8,128)(2,1)} %bitcast.135, f32[128,2048]{1,0:T(8,128)} %get-tuple-element.40.hidden), custom_call_target="tpu_custom_call" | custom-call | tf_op jit(solution)/shard_map/collect_heads/pallas_call | solution.py:610
  561.5 7.4 %fusion.20 = bf16[512,2048]{1,0:T(8,128)(2,1)} fusion(bf16[512,1536]{1,0:T(8,128)(2,1)S(1)} %reshape.199, bf16[2048,2176]{1,0:T(8,128)(2,1)} %bitcast.113), kind=kOutput, calls=%fused_computation.25 | convolution fusion | flops 3222274048 | bytes 9961472 | tf_op jit(solution)/shard_map/dot_general | solution.py:794
  569.6 7.3 %convolution_convert_fusion = bf16[2048,1536]{1,0:T(8,128)(2,1)} fusion(bf16[512,2048]{1,0:T(8,128)(2,1)} %get-tuple-element.48, bf16[512,1536]{1,0:T(8,128)(2,1)S(1)} %reshape.199), kind=kOutput, calls=%fused_computation | convolution fusion | flops 3224371200 | bytes 9961472 | tf_op jit(solution)/shard_map/dot_general | solution.py:1091
  576.9 60.5 %last_backward.1 = (bf16[4,128,2048]{2,1,0:T(8,128)(2,1)}, f32[8,2048]{1,0:T(8,128)}, f32[64,1536]{1,0:T(8,128)}, f32[64,512]{1,0:T(8,128)}) custom-call(bf16[4,128,2048]{2,1,0:T(8,128)(2,1)} %bitcast.136, bf16[4,128,2048]{2,1,0:T(8,128)(2,1)} %bitcast.117, f32[128,2048]{1,0:T(8,128)} %get-tuple-element.46.dhidden, ...), custom_call_target="tpu_custom_call" | custom-call | tf_op jit(solution)/shard_map/last_backward/pallas_call | solution.py:707
  (122 shorter events, 71.2 us)
Async XLA Ops:
  11.7 2.1 copy-start.6
  11.7 2.1 copy-start.7
  11.7 2.1 copy-start.8
  293.4 8.2 %copy-start = (bf16[2,1,256,2048]{3,2,1,0:T(8,128)(2,1)S(1)}, bf16[2,1,256,2048]{3,2,1,0:T(8,128)(2,1)}, u32[]{:S(2)}) copy-start(bf16[2,1,256,2048]{3,2,1,0:T(8,128)(2,1)} %param.14) | copy-start | bytes 6291460
  301.6 7.6 %copy-start.11 = (bf16[4,128,2048]{2,1,0:T(8,128)(2,1)S(1)}, bf16[4,128,2048]{2,1,0:T(8,128)(2,1)}, u32[]{:S(2)}) copy-start(bf16[4,128,2048]{2,1,0:T(8,128)(2,1)} %get-tuple-element.39) | copy-start | bytes 6291460
  309.2 19.2 %slice-start = ((s8[17301504]{0:T(1024)(128)(4,1)}), s8[524288]{0:T(1024)(128)(4,1)S(1)}, s32[]{:S(2)}) async-start(s8[17301504]{0:T(1024)(128)(4,1)} %bitcast.161), calls=%async_computation | async-start | bytes 1048576
  309.2 19.2 %slice-start.1 = ((s8[17301504]{0:T(1024)(128)(4,1)}), s8[4194304]{0:T(1024)(128)(4,1)S(1)}, s32[]{:S(2)}) async-start(s8[17301504]{0:T(1024)(128)(4,1)} %bitcast.161), calls=%async_computation.1 | async-start | bytes 8388608
  309.2 19.2 %slice-start.2 = ((s8[17301504]{0:T(1024)(128)(4,1)}), s8[4194304]{0:T(1024)(128)(4,1)S(1)}, s32[]{:S(2)}) async-start(s8[17301504]{0:T(1024)(128)(4,1)} %bitcast.161), calls=%async_computation.2 | async-start | bytes 8388608
  309.2 19.2 %slice-start.3 = ((s8[17301504]{0:T(1024)(128)(4,1)}), s8[4194304]{0:T(1024)(128)(4,1)S(1)}, s32[]{:S(2)}) async-start(s8[17301504]{0:T(1024)(128)(4,1)} %bitcast.161), calls=%async_computation.3 | async-start | bytes 8388608
  320.3 8.1 %slice-start.4 = ((s8[17301504]{0:T(1024)(128)(4,1)}), s8[4194304]{0:T(1024)(128)(4,1)S(1)}, s32[]{:S(2)}) async-start(s8[17301504]{0:T(1024)(128)(4,1)} %bitcast.161), calls=%async_computation.4 | async-start | bytes 8388608
  320.3 8.1 %copy-start.15 = (bf16[512,1408]{0,1:T(8,128)(2,1)S(1)}, bf16[512,1408]{0,1:T(8,128)(2,1)}, u32[]{:S(2)}) copy-start(bf16[512,1408]{0,1:T(8,128)(2,1)} %get-tuple-element.131) | copy-start | bytes 4325380
  328.4 5.1 copy-start.14
  345.0 5.3 copy-start.13
  435.7 3.6 copy-start.12
  561.5 7.5 %copy-start.10 = (f32[2,2048]{1,0:T(2,128)S(1)}, f32[2,2048]{1,0:T(2,128)}, u32[]{:S(2)}) copy-start(f32[2,2048]{1,0:T(2,128)} %get-tuple-element.47) | copy-start | bytes 49156
  576.9 65.2 %copy-start.1 = (bf16[4,128,2048]{2,1,0:T(8,128)(2,1)S(1)}, bf16[4,128,2048]{2,1,0:T(8,128)(2,1)}, u32[]{:S(2)}) copy-start(bf16[4,128,2048]{2,1,0:T(8,128)(2,1)} %get-tuple-element.44) | copy-start | bytes 6291460
  642.1 2.3 copy-start.2
  644.5 1.3 copy-start.9
  644.5 2.0 copy-start.5
  644.5 2.7 copy-start.4
  644.5 3.5 copy-start.3

commit v2 on v1

v2 whole, which is shorter than its diff:
```python
import functools

import jax
import jax.numpy as jnp
import numpy as np
from jax import lax
from jax.experimental import pallas as pl
from jax.experimental.pallas import tpu as pltpu
from jax.sharding import PartitionSpec as P

MESH = pl.DeviceIdType.MESH
D = 2048
UNITS = 1408
HEAD_DIM = 64
ROT = 16
EPSILON = 1e-05
LOG2E = 1.4426950408889634
LOW = -1e30
TILE = 512
VMEM_LIMIT = 58 * 2**20
STEPS = (1, 3, 2)
BF = jnp.bfloat16
F32 = jnp.float32


def here():
    ctx = lax.axis_index("ctx")
    return (lax.axis_index("dp"), ctx // 4, lax.rem(ctx, 4), lax.axis_index("tensor"))


def at(c, y, z, x):
    return (c, lax.rem(y, 4) * 4 + lax.rem(z, 4), lax.rem(x, 4))


def up(i, d):
    return lax.rem(i + d, 4)


def down(i, d):
    return lax.rem(i + 4 - d, 4)


class Net:
    def __init__(self, send_sems, recv_sems):
        self.send_sems, self.recv_sems = send_sems, recv_sems
        self.sent = []

    def send(self, src, dst, device):
        n = len(self.sent)
        copy = pltpu.make_async_remote_copy(
            src_ref=src,
            dst_ref=dst,
            send_sem=self.send_sems.at[n],
            recv_sem=self.recv_sems.at[n],
            device_id=device,
            device_id_type=MESH,
        )
        copy.start()
        self.sent.append(copy)
        return copy

    def finish(self):
        for copy in self.sent:
            copy.wait_send()


class Local:
    def __init__(self, sems):
        self.sems, self.n = sems, 0

    def copy(self, src, dst):
        copy = pltpu.make_async_copy(src, dst, self.sems.at[self.n])
        copy.start()
        self.n += 1
        return copy


def greet(peers):
    barrier = pltpu.get_barrier_semaphore()
    for peer in peers:
        pl.semaphore_signal(barrier, inc=1, device_id=peer, device_id_type=MESH)
    pl.semaphore_wait(barrier, len(peers))


def y_peers(c, y, z, x):
    return [at(c, y + d, z, x) for d in (1, 2, 3)]


def z_peers(c, y, z, x):
    return [at(c, y, z + d, x) for d in (1, 2, 3)]


def x_peers(c, y, z, x):
    return [at(c, y, z, x + d) for d in (1, 2, 3)]


def core_peer(c, y, z, x):
    return [at(1 - c, y, z, x)]


class RingSum:
    def __init__(self, net, device, mine, spare, add):
        self.net, self.device, self.mine, self.spare, self.add = net, device, mine, spare, add

    def start(self):
        send, mine, spare = self.net.send, self.mine, self.spare
        ahead, back = self.device(1), self.device(3)
        self.far_ahead = send(mine(2, 0), spare.at[0], ahead)
        self.far_back = send(mine(2, 1), spare.at[1], back)
        self.near = [send(mine(1, 1), spare.at[3], ahead), send(mine(3, 0), spare.at[2], back)]

    def middle(self):
        send, spare = self.net.send, self.spare
        self.far_ahead.wait_recv()
        self.add(spare.at[0], self.mine(1, 0))
        self.near.append(send(spare.at[0], spare.at[4], self.device(1)))
        self.far_back.wait_recv()
        self.add(spare.at[1], self.mine(3, 1))
        self.near.append(send(spare.at[1], spare.at[5], self.device(3)))

    def arrive(self):
        for copy in self.near:
            copy.wait_recv()

    def terms(self, half):
        return [self.spare.at[4 if half == 0 else 3], self.spare.at[2 if half == 0 else 5]]


RING_SUM = 6


class RingGather:
    def __init__(self, net, device, out):
        self.net, self.device, self.out = net, device, out

    def start(self, block):
        self.ahead = self.net.send(block, self.out(0), self.device(1))
        self.back = self.net.send(block, self.out(0), self.device(3))

    def from_back(self):
        self.ahead.wait_recv()
        piece = self.out(3, 0)
        self.far_ahead = self.net.send(piece, piece, self.device(1))

    def from_ahead(self):
        self.back.wait_recv()
        piece = self.out(1, 1)
        self.far_back = self.net.send(piece, piece, self.device(3))

    def arrive(self):
        self.far_ahead.wait_recv()
        self.far_back.wait_recv()


RING_GATHER = 4


class Gather:
    def __init__(self, net, local, src, out, me):
        self.net, self.local, self.src, self.out, self.me = net, local, src, out, me
        self.core = []
        c, y, z, x = me
        along_y = lambda d: at(c, y + d, z, x)
        along_z = lambda d: at(c, y, z + d, x)

        def rows(first, half):
            return pl.ds(first, 32) if half is None else pl.ds(first + 16 * half, 16)

        self.one = (
            RingGather(net, along_y, lambda d, half=None: out.at[c, up(y, d), z, rows(0, half)]),
            RingGather(net, along_z, lambda d, half=None: out.at[c, y, up(z, d), rows(32, half)]),
        )
        self.two = {}
        for k in range(4):
            self.two[0, k] = RingGather(
                net, along_z, lambda d, half=None, k=k: out.at[c, up(y, k), up(z, d), rows(0, half)]
            )
            self.two[1, k] = RingGather(
                net, along_y, lambda d, half=None, k=k: out.at[c, up(y, d), up(z, k), rows(32, half)]
            )

    def hand_over(self, piece):
        c, y, z, x = self.me
        self.core.append(self.net.send(piece, piece, at(1 - c, y, z, x)))

    def start(self):
        c, y, z, x = self.me
        src = self.src
        self.own = self.local.copy(src, self.out.at[c, y, z])
        halves = (src.at[pl.ds(0, 32)], src.at[pl.ds(32, 32)])
        for way in range(2):
            self.one[way].start(halves[way])
        for way in range(2):
            self.two[way, 0].start(halves[way])
        self.core.append(self.net.send(src, self.out.at[c, y, z], at(1 - c, y, z, x)))

    def near(self):
        for way in range(2):
            self.one[way].from_back()
            self.two[way, 3].start(self.one[way].out(3))
        for way in range(2):
            self.one[way].from_ahead()
            self.two[way, 1].start(self.one[way].out(1))
        for k in (3, 1):
            for way in range(2):
                self.hand_over(self.one[way].out(k))
        self.pass_on(0)
        for way in range(2):
            self.one[way].arrive()
            self.two[way, 2].start(self.one[way].out(2))
            self.hand_over(self.one[way].out(2))

    def pass_on(self, k):
        for way in range(2):
            self.two[way, k].from_back()
            self.two[way, k].from_ahead()
            self.hand_over(self.two[way, k].out(3))
            self.hand_over(self.two[way, k].out(1))

    def far(self):
        for k in (3, 1, 2):
            self.pass_on(k)
        for k in (0, 3, 1, 2):
            for way in range(2):
                self.two[way, k].arrive()
                self.hand_over(self.two[way, k].out(2))

    def finish(self):
        for copy in self.core:
            copy.wait_recv()
        self.own.wait()


GATHER_COPIES = 10 * RING_GATHER + 31


def scatter_scratch(width):
    return [
        pltpu.VMEM((4, 4, 64, width), BF),
        pltpu.VMEM((4, 4, 64, width), BF),
        pltpu.VMEM((6, 4, 16, width), BF),
        pltpu.VMEM((6, 4, 16, width), BF),
        pltpu.VMEM((4, 32, width), BF),
        pltpu.VMEM((4, 32, width), BF),
        pltpu.VMEM((6, 16, width), BF),
        pltpu.VMEM((6, 16, width), BF),
    ]


SCATTER_COPIES = 1 + 4 * RING_SUM


def add_blocks(total, term):
    if len(total.shape) == 2:
        total[...] = (total[...].astype(F32) + term[...].astype(F32)).astype(BF)
        return

    def one(i, carry):
        total[i] = (total[i].astype(F32) + term[i].astype(F32)).astype(BF)
        return carry

    lax.fori_loop(0, total.shape[0], one, 0)


class Scatter:
    def __init__(self, net, local, grads, out, scratch, me):
        self.net, self.local, self.grads, self.out, self.me = net, local, grads, out, me
        (held, self.other, one_a, one_b, self.sum_a, self.sum_b, two_a, two_b) = scratch
        self.held = held
        c, y, z, x = me
        along_y = lambda d: at(c, y + d, z, x)
        along_z = lambda d: at(c, y, z + d, x)
        self.one_a = RingSum(
            net, along_z, lambda d, half: held.at[:, up(z, d), pl.ds(16 * half, 16)], one_a, add_blocks
        )
        self.one_b = RingSum(
            net, along_y, lambda d, half: held.at[up(y, d), :, pl.ds(32 + 16 * half, 16)], one_b, add_blocks
        )
        self.two_a = RingSum(
            net, along_y, lambda d, half: self.sum_a.at[up(y, d), pl.ds(16 * half, 16)], two_a, add_blocks
        )
        self.two_b = RingSum(
            net, along_z, lambda d, half: self.sum_b.at[up(z, d), pl.ds(16 * half, 16)], two_b, add_blocks
        )

    def start(self):
        c, y, z, x = self.me
        self.own = self.local.copy(self.grads.at[c], self.held)
        self.zero = self.net.send(self.grads.at[1 - c], self.other, at(1 - c, y, z, x))

    def first(self):
        self.own.wait()
        self.zero.wait_recv()
        held, other = self.held, self.other

        def add(i, carry):
            for q in range(4):
                rows = pl.ds(q * 16, 16)
                held[i // 4, lax.rem(i, 4), rows, :] = (
                    held[i // 4, lax.rem(i, 4), rows, :].astype(F32)
                    + other[i // 4, lax.rem(i, 4), rows, :].astype(F32)
                ).astype(BF)
            return carry

        lax.fori_loop(0, 16, add, 0)
        self.one_a.start()
        self.one_b.start()

    def first_middle(self):
        self.one_a.middle()
        self.one_b.middle()

    def second(self):
        for one, two, total in ((self.one_a, self.two_a, self.sum_a), (self.one_b, self.two_b, self.sum_b)):
            one.arrive()
            for half in range(2):
                own, terms = one.mine(0, half), one.terms(half)

                def add(i, carry, half=half, own=own, terms=terms, total=total):
                    value = own[i].astype(F32)
                    for term in terms:
                        value += term[i].astype(F32)
                    total[i, pl.ds(16 * half, 16), :] = value.astype(BF)
                    return carry

                lax.fori_loop(0, 4, add, 0)
            two.start()

    def second_middle(self):
        self.two_a.middle()
        self.two_b.middle()

    def third(self):
        for first, two in ((0, self.two_a), (32, self.two_b)):
            two.arrive()
            for half in range(2):
                value = two.mine(0, half)[...].astype(F32)
                for term in two.terms(half):
                    value += term[...].astype(F32)
                self.out[pl.ds(first + 16 * half, 16), :] = value


class SumX:
    def __init__(self, net, local, parts, held, spare, me):
        c, y, z, x = me
        self.local, self.parts, self.held, self.x, self.net = local, parts, held, x, net
        self.along = lambda d: at(c, y, z, x + d)
        self.ring = RingSum(
            net, self.along, lambda d, half: held.at[up(x, d), pl.ds(64 * half, 64)], spare, self.add
        )

    def add(self, total, term):
        def one(i, carry):
            rows = pl.ds(pl.multiple_of(i * 16, 16), 16)
            total[rows, :] = (total[rows, :].astype(F32) + term[rows, :].astype(F32)).astype(BF)
            return carry

        lax.fori_loop(0, 4, one, 0)

    def load(self):
        self.loads = [self.local.copy(self.parts.at[up(self.x, d)], self.held.at[up(self.x, d)]) for d in (2, 1, 3, 0)]

    def start(self):
        for copy in self.loads:
            copy.wait()
        self.ring.start()

    def middle(self):
        self.ring.middle()

    def totals(self, step):
        self.ring.arrive()
        for half in range(2):
            terms = self.ring.terms(half)

            def loop(i, carry, half=half, terms=terms):
                rows = pl.ds(pl.multiple_of(i * 16, 16), 16)
                own = pl.ds(pl.multiple_of(64 * half + i * 16, 16), 16)
                value = self.held[self.x, own, :].astype(F32)
                for term in terms:
                    value += term[rows, :].astype(F32)
                step(own, value)
                return carry

            lax.fori_loop(0, 4, loop, 0)

    def gather(self, block, out):
        x = self.x

        def piece(d, half=None):
            whole = out.at[up(x, d)]
            return whole if half is None else out.at[up(x, d), pl.ds(64 * half, 64)]

        self.back = RingGather(self.net, self.along, piece)
        self.mine = self.local.copy(block, out.at[x])
        self.back.start(block)

    def gather_middle(self):
        self.back.from_back()
        self.back.from_ahead()

    def finish(self):
        self.mine.wait()
        self.back.arrive()


SUM_COPIES = RING_SUM + RING_GATHER
SUM_LOCALS = 5


def sum_scratch():
    return [pltpu.VMEM((4, 128, D), BF), pltpu.VMEM((6, 64, D), BF)]


def normed(values):
    centre = jnp.mean(values, axis=-1, keepdims=True)
    spread = values - centre
    inverse = lax.rsqrt(jnp.mean(spread * spread, axis=-1, keepdims=True) + EPSILON)
    return spread * inverse, inverse


def norm_pullback(upstream, norm, inverse, gain):
    scaled = upstream * gain
    first = jnp.mean(scaled, axis=-1, keepdims=True)
    second = jnp.mean(scaled * norm, axis=-1, keepdims=True)
    return inverse * (scaled - first - norm * second)


ANY = pl.BlockSpec(memory_space=pl.ANY)
IN_VMEM = pl.BlockSpec(memory_space=pltpu.VMEM)


def remote_call(body, name, cid, ins, outs, scratch, copies, locals_):
    return pl.pallas_call(
        body,
        name=name,
        in_specs=ins,
        out_specs=[spec for _, _, spec in outs],
        out_shape=[jax.ShapeDtypeStruct(shape, dtype) for shape, dtype, _ in outs],
        scratch_shapes=scratch
        + [
            pltpu.SemaphoreType.DMA((copies,)),
            pltpu.SemaphoreType.DMA((copies,)),
            pltpu.SemaphoreType.DMA((locals_,)),
        ],
        compiler_params=pltpu.CompilerParams(
            collective_id=cid, has_side_effects=True, vmem_limit_bytes=VMEM_LIMIT
        ),
    )


def gather_front(shard):
    def kernel(src, out, ss, rs, ls):
        me = here()
        greet(y_peers(*me) + z_peers(*me) + core_peer(*me))
        net, local = Net(ss, rs), Local(ls)
        gather = Gather(net, local, src, out, me)
        gather.start()
        gather.near()
        gather.far()
        gather.finish()
        net.finish()

    width = shard.shape[1]
    return remote_call(
        kernel, "gather_front", 0, [ANY], [((2, 4, 4, 64, width), BF, ANY)], [], GATHER_COPIES, 1
    )(shard)[0]


def spread_heads(qkv):
    def kernel(src, out, ss, rs, ls):
        me = here()
        c, y, z, x = me
        greet(y_peers(*me) + z_peers(*me))
        net, local = Net(ss, rs), Local(ls)
        kv = pl.ds(0, 2)
        owns = [local.copy(src.at[0, z], out.at[0, y, z]), local.copy(src.at[1, y], out.at[1, y, z])]
        first, second = {}, {}
        along_y = lambda d: at(c, y + d, z, x)
        along_z = lambda d: at(c, y, z + d, x)

        def part(half):
            return kv if half is None else half

        for k in range(4):
            second[0, k] = RingGather(
                net, along_y, lambda d, half=None, k=k: out.at[0, up(y, d), up(z, k), part(half)]
            )
            second[1, k] = RingGather(
                net, along_z, lambda d, half=None, k=k: out.at[1, up(y, k), up(z, d), part(half)]
            )
        for d in STEPS:
            first[0, d] = net.send(src.at[0, up(z, d)], out.at[0, y, z], along_z(d))
            first[1, d] = net.send(src.at[1, up(y, d)], out.at[1, y, z], along_y(d))
        second[0, 0].start(src.at[0, z, kv])
        second[1, 0].start(src.at[1, y, kv])
        for d in STEPS:
            for m in range(2):
                first[m, d].wait_recv()
                ring = second[m, 4 - d]
                ring.start(ring.out(0))
        for k in (0, 3, 1, 2):
            for m in range(2):
                second[m, k].from_back()
                second[m, k].from_ahead()
        for ring in second.values():
            ring.arrive()
        for copy in owns:
            copy.wait()
        net.finish()

    return remote_call(
        kernel, "spread_heads", 1, [ANY], [((2, 4, 4, 3, 256, 128), BF, ANY)], [], 6 + 8 * RING_GATHER, 2
    )(qkv)[0]


def swap_rows(blocks, cid, name):
    def kernel(src, out, ss, rs, ls):
        me = here()
        c, y, z, x = me
        greet(y_peers(*me) + z_peers(*me))
        net, local = Net(ss, rs), Local(ls)
        owns = [local.copy(src.at[0, z], out.at[0, z]), local.copy(src.at[1, y], out.at[1, y])]
        copies = []
        for d in STEPS:
            copies.append(net.send(src.at[0, up(z, d)], out.at[0, z], at(c, y, z + d, x)))
            copies.append(net.send(src.at[1, up(y, d)], out.at[1, y], at(c, y + d, z, x)))
        for copy in copies:
            copy.wait_recv()
        for copy in owns:
            copy.wait()
        net.finish()

    return remote_call(kernel, name, cid, [ANY], [((2, 4, 256, 128), BF, ANY)], [], 6, 2)(blocks)[0]


def middle_forward(parts, inputs, gain, shift, shard):
    width = shard.shape[1]

    def kernel(parts, inputs, gain, shift, shard, hidden, second, weights, held, spare, base, low, ss, rs, ls):
        me = here()
        c, y, z, x = me
        net, local = Net(ss, rs), Local(ls)
        sums = SumX(net, local, parts, held, spare, me)
        sums.load()
        residual = local.copy(inputs.at[x], base)
        greet(y_peers(*me) + z_peers(*me) + core_peer(*me) + x_peers(*me))
        gather = Gather(net, local, shard, weights, me)
        gather.start()
        sums.start()
        gather.near()
        sums.middle()
        residual.wait()

        def step(rows, total):
            value = base[rows, :].astype(F32) + total
            hidden[rows, :] = value
            norm, _ = normed(value)
            low[rows, :] = (norm * gain[...] + shift[...]).astype(BF)

        sums.totals(step)
        sums.gather(low, second)
        gather.far()
        sums.gather_middle()
        gather.finish()
        sums.finish()
        net.finish()

    return remote_call(
        kernel,
        "middle_forward",
        3,
        [ANY, ANY, IN_VMEM, IN_VMEM, ANY],
        [
            ((128, D), F32, IN_VMEM),
            ((4, 128, D), BF, ANY),
            ((2, 4, 4, 64, width), BF, ANY),
        ],
        sum_scratch() + [pltpu.VMEM((128, D), BF), pltpu.VMEM((128, D), BF)],
        GATHER_COPIES + SUM_COPIES,
        SUM_LOCALS + 2,
    )(parts, inputs, gain, shift, shard)


def middle_backward(parts, cotangent, hidden, gain, grads):
    widths = [g.shape[-1] for g in grads]
    count = len(grads)

    def kernel(parts, cotangent, hidden, gain, *rest):
        grad_refs = rest[:count]
        dhidden, hidden_low, vectors = rest[count : count + 3]
        outs = rest[count + 3 : 2 * count + 3]
        held, spare, base, low = rest[2 * count + 3 : 2 * count + 7]
        scratch = rest[2 * count + 7 : -3]
        ss, rs, ls = rest[-3:]
        me = here()
        c, y, z, x = me
        net, local = Net(ss, rs), Local(ls)
        sums = SumX(net, local, parts, held, spare, me)
        sums.load()
        upstream = local.copy(cotangent.at[x], base)
        greet(y_peers(*me) + z_peers(*me) + core_peer(*me) + x_peers(*me))
        scatters = [
            Scatter(net, local, grad_refs[k], outs[k], scratch[8 * k : 8 * k + 8], me)
            for k in range(count)
        ]
        for scatter in scatters:
            scatter.start()
        sums.start()
        for scatter in scatters:
            scatter.first()
        sums.middle()
        for scatter in scatters:
            scatter.first_middle()
        upstream.wait()
        vectors[...] = jnp.zeros_like(vectors)

        def step(rows, dsecond):
            norm, inverse = normed(hidden[rows, :])
            value = base[rows, :].astype(F32) + norm_pullback(dsecond, norm, inverse, gain[...])
            dhidden[rows, :] = value
            low[rows, :] = value.astype(BF)
            vectors[0:1, :] += jnp.sum(dsecond * norm, axis=0, keepdims=True)
            vectors[1:2, :] += jnp.sum(dsecond, axis=0, keepdims=True)

        sums.totals(step)
        sums.gather(low, hidden_low)
        scatters[0].second()
        sums.gather_middle()
        for scatter in scatters[1:]:
            scatter.second()
        for scatter in scatters:
            scatter.second_middle()
        for scatter in scatters:
            scatter.third()
        sums.finish()
        net.finish()

    scratch = sum_scratch() + [pltpu.VMEM((128, D), BF), pltpu.VMEM((128, D), BF)]
    for width in widths:
        scratch += scatter_scratch(width)
    return remote_call(
        kernel,
        "middle_backward",
        4,
        [ANY, ANY, IN_VMEM, IN_VMEM] + [ANY] * count,
        [((128, D), F32, IN_VMEM), ((4, 128, D), BF, ANY), ((2, D), F32, IN_VMEM)]
        + [((64, width), F32, IN_VMEM) for width in widths],
        scratch,
        SUM_COPIES + SCATTER_COPIES * count,
        SUM_LOCALS + 1 + count,
    )(parts, cotangent, hidden, gain, *grads)


def collect_heads(dkv, dq, parts, hidden):
    def kernel(dkv, dq, parts, hidden, dproject, outputs, mine, got, summed, held, spare, low, ss, rs, ls):
        me = here()
        c, y, z, x = me
        net, local = Net(ss, rs), Local(ls)
        order = (1, 3, 2, 0)
        loads = [local.copy(dkv.at[m], mine.at[m]) for m in range(2)]
        sums = SumX(net, local, parts, held, spare, me)
        sums.load()
        greet(y_peers(*me) + z_peers(*me) + x_peers(*me))
        kv = pl.ds(0, 2)
        along_y = lambda d: at(c, y + d, z, x)
        along_z = lambda d: at(c, y, z + d, x)

        def add(total, term):
            def one(i, carry):
                rows = pl.ds(pl.multiple_of(i * 64, 64), 64)
                total[rows, :] = (total[rows, :].astype(F32) + term[rows, :].astype(F32)).astype(BF)
                return carry

            lax.fori_loop(0, 4, one, 0)

        rings = {}
        for k in order:
            rings[0, k] = RingSum(
                net, along_y, lambda d, half, k=k: mine.at[0, up(y, d), up(z, k), half], got.at[0, k], add
            )
            rings[1, k] = RingSum(
                net, along_z, lambda d, half, k=k: mine.at[1, up(y, k), up(z, d), half], got.at[1, k], add
            )
        for copy in loads:
            copy.wait()
        for ring in rings.values():
            ring.start()
        sums.start()
        lates = [
            local.copy(dq.at[0, z], dproject.at[0, z, 2]),
            local.copy(dq.at[1, y], dproject.at[1, y, 2]),
        ]
        two = []
        for d in STEPS:
            two.append(net.send(dq.at[0, up(z, d)], dproject.at[0, z, 2], along_z(d)))
            two.append(net.send(dq.at[1, up(y, d)], dproject.at[1, y, 2], along_y(d)))
        for ring in rings.values():
            ring.middle()
        sums.middle()
        for k in order:
            for m, spot in ((0, z), (1, y)):
                ring = rings[m, k]
                ring.arrive()
                for half in range(2):
                    own, terms = ring.mine(0, half), ring.terms(half)

                    def total(i, carry, m=m, k=k, half=half, own=own, terms=terms):
                        rows = pl.ds(pl.multiple_of(i * 64, 64), 64)
                        value = own[rows, :].astype(F32)
                        for term in terms:
                            value += term[rows, :].astype(F32)
                        summed[m, k, half, rows, :] = value.astype(BF)
                        return carry

                    lax.fori_loop(0, 4, total, 0)
            if k:
                two.append(net.send(summed.at[0, k], dproject.at[0, z, kv], along_z(k)))
                two.append(net.send(summed.at[1, k], dproject.at[1, y, kv], along_y(k)))
            else:
                lates.append(local.copy(summed.at[0, 0], dproject.at[0, z, kv]))
                lates.append(local.copy(summed.at[1, 0], dproject.at[1, y, kv]))

        def step(rows, total):
            low[rows, :] = (hidden[rows, :] + total).astype(BF)

        sums.totals(step)
        sums.gather(low, outputs)
        sums.gather_middle()
        for copy in two:
            copy.wait_recv()
        for copy in lates:
            copy.wait()
        sums.finish()
        net.finish()

    return remote_call(
        kernel,
        "collect_heads",
        6,
        [ANY, ANY, ANY, IN_VMEM],
        [((2, 4, 3, 256, 128), BF, ANY), ((4, 128, D), BF, ANY)],
        [
            pltpu.VMEM((2, 4, 4, 2, 256, 128), BF),
            pltpu.VMEM((2, 4, 6, 256, 128), BF),
            pltpu.VMEM((2, 4, 2, 256, 128), BF),
        ]
        + sum_scratch()
        + [pltpu.VMEM((128, D), BF)],
        8 * RING_SUM + 6 + 6 + SUM_COPIES,
        2 + 4 + SUM_LOCALS,
    )(dkv, dq, parts, hidden)


def last_backward(parts, inputs, dhidden, gain, vectors, grads):
    widths = [g.shape[-1] for g in grads]
    count = len(grads)

    def kernel(parts, inputs, dhidden, gain, vectors, *rest):
        grad_refs = rest[:count]
        input_grad, sums_out = rest[count : count + 2]
        outs = rest[count + 2 : 2 * count + 2]
        held, spare, base, low, small, got = rest[2 * count + 2 : 2 * count + 8]
        scratch = rest[2 * count + 8 : -3]
        ss, rs, ls = rest[-3:]
        me = here()
        c, y, z, x = me
        net, local = Net(ss, rs), Local(ls)
        sums = SumX(net, local, parts, held, spare, me)
        sums.load()
        residual = local.copy(inputs.at[x], base)
        greet(y_peers(*me) + z_peers(*me) + core_peer(*me) + x_peers(*me))
        scatters = [
            Scatter(net, local, grad_refs[k], outs[k], scratch[8 * k : 8 * k + 8], me)
            for k in range(count)
        ]
        for scatter in scatters:
            scatter.start()
        sums.start()
        for scatter in scatters:
            scatter.first()
        sums.middle()
        for scatter in scatters:
            scatter.first_middle()
        residual.wait()
        small[0, ...] = vectors[...]

        def step(rows, dfirst):
            norm, inverse = normed(base[rows, :].astype(F32))
            value = dhidden[rows, :] + norm_pullback(dfirst, norm, inverse, gain[...])
            low[rows, :] = value.astype(BF)
            small[0, 0:1, :] += jnp.sum(dfirst * norm, axis=0, keepdims=True)
            small[0, 1:2, :] += jnp.sum(dfirst, axis=0, keepdims=True)

        sums.totals(step)
        copies = [
            net.send(small.at[0], got.at[0, d - 1], at(c, y, z, x + d)) for d in STEPS
        ]
        sums.gather(low, input_grad)
        for scatter in scatters:
            scatter.second()
        sums.gather_middle()
        for copy in copies:
            copy.wait_recv()
        small[1, ...] = small[0, ...]
        for n in range(3):
            small[1, 0:4, :] += got[0, n, 0:4, :]
        copies = [
            net.send(small.at[1], got.at[1, d - 1], at(c, y + d, z, x)) for d in STEPS
        ]
        for copy in copies:
            copy.wait_recv()
        small[2, ...] = small[1, ...] + got[1, 0] + got[1, 1] + got[1, 2]
        copies = [
            net.send(small.at[2], got.at[2, d - 1], at(c, y, z + d, x)) for d in STEPS
        ]
        for copy in copies:
            copy.wait_recv()
        small[3, ...] = small[2, ...] + got[2, 0] + got[2, 1] + got[2, 2]
        copy = net.send(small.at[3], got.at[3, 0], at(1 - c, y, z, x))
        for scatter in scatters:
            scatter.second_middle()
        for scatter in scatters:
            scatter.third()
        copy.wait_recv()
        sums_out[...] = small[3, ...] + got[3, 0]
        sums.finish()
        net.finish()

    scratch = sum_scratch() + [
        pltpu.VMEM((128, D), BF),
        pltpu.VMEM((128, D), BF),
        pltpu.VMEM((4, 8, D), F32),
        pltpu.VMEM((4, 3, 8, D), F32),
    ]
    for width in widths:
        scratch += scatter_scratch(width)
    return remote_call(
        kernel,
        "last_backward",
        7,
        [ANY, ANY, IN_VMEM, IN_VMEM, IN_VMEM] + [ANY] * count,
        [((4, 128, D), BF, ANY), ((8, D), F32, IN_VMEM)]
        + [((64, width), F32, IN_VMEM) for width in widths],
        scratch,
        SUM_COPIES + 10 + SCATTER_COPIES * count,
        SUM_LOCALS + 1 + count,
    )(parts, inputs, dhidden, gain, vectors, *grads)


def turn(values, cosine, sine):
    lane = lax.rem(lax.broadcasted_iota(jnp.int32, values.shape, 1), HEAD_DIM)
    swapped = jnp.where(lane < ROT // 2, -pltpu.roll(values, 120, 1), pltpu.roll(values, 8, 1))
    return values * cosine + swapped * sine


def project_heads(tokens, gain, shift, front, bias, tables):
    def kernel(x_ref, gain_ref, shift_ref, w_hbm, b_ref, t_ref, out_ref, low_ref, weights, sems):
        loads = []
        for t in range(3):
            columns = pl.ds(t * 512, 512)
            loads.append(pltpu.make_async_copy(w_hbm.at[:, columns], weights.at[t], sems.at[t]))
            loads[t].start()

        def step(i, carry):
            rows = pl.ds(pl.multiple_of(i * 32, 32), 32)
            norm, _ = normed(x_ref[rows, :].astype(F32))
            low_ref[rows, :] = (norm * gain_ref[...] + shift_ref[...]).astype(BF)
            return carry

        lax.fori_loop(0, 16, step, 0)
        for t in (1, 2, 0):
            loads[t].wait()
            for m in range(2):
                acc = jnp.dot(
                    low_ref[m * 256 : m * 256 + 256, :], weights[t], preferred_element_type=F32
                )
                acc = acc + b_ref[:, t * 512 : t * 512 + 512]
                for h in range(4):
                    part = acc[:, h * 128 : h * 128 + 128]
                    if t < 2:
                        part = turn(part, t_ref[0], t_ref[1])
                    out_ref[m, h, (t + 2) % 3] = part.astype(BF)

    return pl.pallas_call(
        kernel,
        name="project_heads",
        in_specs=[IN_VMEM, IN_VMEM, IN_VMEM, ANY, IN_VMEM, IN_VMEM],
        out_specs=[IN_VMEM, IN_VMEM],
        out_shape=[
            jax.ShapeDtypeStruct((2, 4, 3, 256, 128), BF),
            jax.ShapeDtypeStruct((512, D), BF),
        ],
        scratch_shapes=[pltpu.VMEM((3, D, 512), BF), pltpu.SemaphoreType.DMA((3,))],
        compiler_params=pltpu.CompilerParams(vmem_limit_bytes=VMEM_LIMIT),
    )(tokens, gain, shift, front, bias, tables)


def two_heads(block):
    lane = lax.broadcasted_iota(jnp.int32, (128, 128), 1)
    value = block.astype(F32)
    return jnp.concatenate(
        [jnp.where(lane < HEAD_DIM, value, 0.0), jnp.where(lane >= HEAD_DIM, value, 0.0)], axis=0
    )


def two_heads_t(block):
    feature = lax.broadcasted_iota(jnp.int32, (128, 128), 0)
    value = block.astype(F32).T
    return jnp.concatenate(
        [jnp.where(feature < HEAD_DIM, value, 0.0), jnp.where(feature >= HEAD_DIM, value, 0.0)], axis=1
    )


def one_block(stacked):
    feature = lax.broadcasted_iota(jnp.int32, (128, 128), 0)
    return jnp.where(feature < HEAD_DIM, stacked[:, :128], stacked[:, 128:]).T


def nt(left, right):
    return lax.dot_general(left, right, (((1,), (1,)), ((), ())), preferred_element_type=F32)


def unit_of(places, m, n):
    pair, rest = n // 9, lax.rem(n, 9)
    ahead = places[m * 8 + pair * 2] // (TILE // 128) + 1
    late = rest >= ahead
    block = pair * 2 + jnp.where(late, 1, 0)
    tile = rest - jnp.where(late, ahead, 0)
    return block, tile, places[m * 8 + block] * 128 - tile * TILE


def key_minus_query():
    return lax.broadcasted_iota(jnp.int32, (TILE, 256), 0) - lax.rem(
        lax.broadcasted_iota(jnp.int32, (TILE, 256), 1), 128
    )


def tile_of(t):
    return pl.ds(pl.multiple_of(t * TILE, TILE), TILE)


def lay_blocks(slots, lay):
    def some(n, carry):
        for k in range(4):
            b = n * 4 + k
            slot = slots[b]
            rows = pl.ds(pl.multiple_of(lax.rem(slot, 2) * 128, 128), 128)
            lay(slot // 2, rows, pl.ds(pl.multiple_of(b * 128, 128), 128))
        return carry

    lax.fori_loop(0, 8, some, 0)


UNITS_EACH = 36


def attend(slots, places, rows_of, spread):
    def kernel(
        slots, places, rows_of, k_ref, v_ref, q_ref, o_ref, full_ref, log_ref,
        keys, values_t, queries, scores_0, scores_1, weights_0, weights_1, results, sums,
    ):
        scores, weights = (scores_0, scores_1), (weights_0, weights_1)
        m = pl.program_id(0)

        def lay(slot, rows, to):
            keys[to, :] = k_ref[0, slot, 0, rows, :]
            values_t[:, to] = v_ref[0, slot, 0, rows, :].T

        lay_blocks(slots, lay)
        for b in range(8):
            row = rows_of[m * 4 + b // 2]
            block = q_ref[0, row, 0, (b % 2) * 128 : (b % 2) * 128 + 128, :]
            queries[b] = (two_heads_t(block) * 0.125).astype(BF)
        offset = key_minus_query()

        def multiply(n, odd):
            block, tile, _ = unit_of(places, m, n)
            scores[odd][...] = jnp.dot(
                keys[tile_of(tile), :], queries[block], preferred_element_type=F32
            )

        def soften(n, odd, top, total):
            block, tile, limit = unit_of(places, m, n)
            value = jnp.where(offset <= limit, scores[odd][...] * LOG2E, LOW)
            first = tile == 0
            top = jnp.where(first, LOW, top)
            new_top = jnp.maximum(top, jnp.max(value, axis=0, keepdims=True))
            exps = jnp.exp2(value - new_top)
            shrink = jnp.exp2(top - new_top)
            total = total * shrink + jnp.sum(exps, axis=0, keepdims=True)
            weights[odd][...] = exps.astype(BF)
            sums[block, 0:1, :] = new_top
            sums[block, 1:2, :] = total
            return new_top, total, shrink

        def gather(n, odd, shrink, acc):
            block, tile, _ = unit_of(places, m, n)
            acc = acc * shrink + jnp.dot(
                values_t[:, tile_of(tile)], weights[odd][...], preferred_element_type=F32
            )
            results[block] = acc
            return acc

        row = jnp.zeros((1, 256), F32)
        multiply(0, 0)
        multiply(1, 1)
        top, total, shrink = soften(0, 0, row, row)

        def step(k, carry):
            top, total, shrink, acc = carry
            for n, odd in ((2 * k + 1, 1), (2 * k + 2, 0)):
                multiply(n + 1, 1 - odd)
                acc = gather(n - 1, 1 - odd, shrink, acc)
                top, total, shrink = soften(n, odd, top, total)
            return top, total, shrink, acc

        carry = (top, total, shrink, jnp.zeros((128, 256), F32))
        top, total, shrink, acc = lax.fori_loop(0, UNITS_EACH // 2 - 1, step, carry)
        last = UNITS_EACH - 1
        acc = gather(last - 1, 0, shrink, acc)
        _, _, shrink = soften(last, 1, top, total)
        gather(last, 1, shrink, acc)
        for b in range(8):
            rows = slice((b % 2) * 128, (b % 2) * 128 + 128)
            total = sums[b, 1:2, :]
            result = one_block(results[b] / total)
            full_ref[0, b // 2, rows, :] = result
            o_ref[0, b // 2, rows, :] = result.astype(BF)
            log_ref[0, b : b + 1, :] = sums[b, 0:1, :] + jnp.log2(total)

    grid_spec = pltpu.PrefetchScalarGridSpec(
        num_scalar_prefetch=3,
        grid=(2,),
        in_specs=[
            pl.BlockSpec((1, 16, 1, 256, 128), lambda m, s, p, r: (m, 0, 0, 0, 0)),
            pl.BlockSpec((1, 16, 1, 256, 128), lambda m, s, p, r: (m, 0, 1, 0, 0)),
            pl.BlockSpec((1, 16, 1, 256, 128), lambda m, s, p, r: (m, 0, 2, 0, 0)),
        ],
        out_specs=[
            pl.BlockSpec((1, 4, 256, 128), lambda m, s, p, r: (m, 0, 0, 0)),
            pl.BlockSpec((1, 4, 256, 128), lambda m, s, p, r: (m, 0, 0, 0)),
            pl.BlockSpec((1, 8, 256), lambda m, s, p, r: (m, 0, 0)),
        ],
        scratch_shapes=[
            pltpu.VMEM((4096, 128), BF),
            pltpu.VMEM((128, 4096), BF),
            pltpu.VMEM((8, 128, 256), BF),
            pltpu.VMEM((TILE, 256), F32),
            pltpu.VMEM((TILE, 256), F32),
            pltpu.VMEM((TILE, 256), BF),
            pltpu.VMEM((TILE, 256), BF),
            pltpu.VMEM((8, 128, 256), F32),
            pltpu.VMEM((8, 8, 256), F32),
        ],
    )
    return pl.pallas_call(
        kernel,
        name="attend",
        grid_spec=grid_spec,
        out_shape=[
            jax.ShapeDtypeStruct((2, 4, 256, 128), BF),
            jax.ShapeDtypeStruct((2, 4, 256, 128), F32),
            jax.ShapeDtypeStruct((2, 8, 256), F32),
        ],
        compiler_params=pltpu.CompilerParams(vmem_limit_bytes=VMEM_LIMIT),
    )(slots, places, rows_of, spread, spread, spread)


def attend_back(slots, places, rows_of, spread, full, logs, upstream, tables):
    base, steps = tables

    def kernel(
        slots, places, rows_of, k_ref, v_ref, q_ref, full_ref, log_ref, up_ref, base_ref, steps_ref,
        dq_ref, dkv_ref,
        keys, keys_t, values, dkeys, dvalues, queries, queries_t, grads, grads_t, delta,
        scores_0, scores_1, dprobs_0, dprobs_1, probs_0, probs_1, dscores_0, dscores_1, results,
    ):
        scores, dprobs = (scores_0, scores_1), (dprobs_0, dprobs_1)
        probs_low, dscores = (probs_0, probs_1), (dscores_0, dscores_1)
        m = pl.program_id(0)

        def lay(slot, rows, to):
            block = k_ref[0, slot, 0, rows, :]
            keys[to, :] = block
            keys_t[:, to] = block.T
            values[to, :] = v_ref[0, slot, 0, rows, :]
            dkeys[to, :] = jnp.zeros((128, 128), F32)
            dvalues[to, :] = jnp.zeros((128, 128), F32)

        lay_blocks(slots, lay)
        for b in range(8):
            rows = slice((b % 2) * 128, (b % 2) * 128 + 128)
            block = q_ref[0, rows_of[m * 4 + b // 2], 0, rows, :]
            queries[b] = (two_heads(block) * 0.125).astype(BF)
            queries_t[b] = (two_heads_t(block) * 0.125).astype(BF)
            ups = up_ref[0, b // 2, rows, :]
            grads[b] = two_heads(ups).astype(BF)
            grads_t[b] = two_heads_t(ups).astype(BF)
            product = (ups.astype(F32) * full_ref[0, b // 2, rows, :]).T
            delta[b, 0:1, :128] = jnp.sum(product[:HEAD_DIM], axis=0, keepdims=True)
            delta[b, 0:1, 128:] = jnp.sum(product[HEAD_DIM:], axis=0, keepdims=True)
        offset = key_minus_query()

        def multiply(n, odd):
            block, tile, _ = unit_of(places, m, n)
            scores[odd][...] = jnp.dot(
                keys[tile_of(tile), :], queries_t[block], preferred_element_type=F32
            )
            dprobs[odd][...] = jnp.dot(
                values[tile_of(tile), :], grads_t[block], preferred_element_type=F32
            )

        def soften(n, odd):
            block, _, limit = unit_of(places, m, n)
            value = jnp.exp2(scores[odd][...] * LOG2E - log_ref[0, pl.ds(block, 1), :])
            value = jnp.where(offset <= limit, value, 0.0)
            probs_low[odd][...] = value.astype(BF)
            dscores[odd][...] = (
                value * (dprobs[odd][...] - delta[block, 0:1, :])
            ).astype(BF)

        def gather(n, odd, acc):
            block, tile, _ = unit_of(places, m, n)
            span = tile_of(tile)
            dvalues[span, :] += jnp.dot(probs_low[odd][...], grads[block], preferred_element_type=F32)
            dkeys[span, :] += jnp.dot(dscores[odd][...], queries[block], preferred_element_type=F32)
            acc = jnp.where(tile == 0, 0.0, acc) + jnp.dot(
                keys_t[:, span], dscores[odd][...], preferred_element_type=F32
            )
            results[block] = acc
            return acc

        multiply(0, 0)
        multiply(1, 1)
        soften(0, 0)

        def step(k, acc):
            for n, odd in ((2 * k + 1, 1), (2 * k + 2, 0)):
                multiply(n + 1, 1 - odd)
                acc = gather(n - 1, 1 - odd, acc)
                soften(n, odd)
            return acc

        last = UNITS_EACH - 1
        acc = lax.fori_loop(0, UNITS_EACH // 2 - 1, step, jnp.zeros((128, 256), F32))
        acc = gather(last - 1, 0, acc)
        soften(last, 1)
        gather(last, 1, acc)

        def turned_back(values, place):
            cosine, sine = base_ref[0], base_ref[1]
            far_cosine, far_sine = steps_ref[0, pl.ds(place, 1), :], steps_ref[1, pl.ds(place, 1), :]
            return turn(
                values,
                far_cosine * cosine - far_sine * sine,
                -(far_sine * cosine + far_cosine * sine),
            )

        for b in range(8):
            rows = slice((b % 2) * 128, (b % 2) * 128 + 128)
            dquery = one_block(results[b]) * 0.125
            dq_ref[0, b // 2, rows, :] = turned_back(dquery, places[m * 8 + b]).astype(BF)

        def flush(n, carry):
            for k in range(2):
                b = n * 2 + k
                slot = slots[b]
                rows = pl.ds(pl.multiple_of(lax.rem(slot, 2) * 128, 128), 128)
                to = pl.ds(pl.multiple_of(b * 128, 128), 128)
                dkv_ref[0, slot // 2, 0, rows, :] = turned_back(dkeys[to, :], b).astype(BF)
                dkv_ref[0, slot // 2, 1, rows, :] = dvalues[to, :].astype(BF)
            return carry

        lax.fori_loop(0, 16, flush, 0)

    grid_spec = pltpu.PrefetchScalarGridSpec(
        num_scalar_prefetch=3,
        grid=(2,),
        in_specs=[
            pl.BlockSpec((1, 16, 1, 256, 128), lambda m, s, p, r: (m, 0, 0, 0, 0)),
            pl.BlockSpec((1, 16, 1, 256, 128), lambda m, s, p, r: (m, 0, 1, 0, 0)),
            pl.BlockSpec((1, 16, 1, 256, 128), lambda m, s, p, r: (m, 0, 2, 0, 0)),
            pl.BlockSpec((1, 4, 256, 128), lambda m, s, p, r: (m, 0, 0, 0)),
            pl.BlockSpec((1, 8, 256), lambda m, s, p, r: (m, 0, 0)),
            pl.BlockSpec((1, 4, 256, 128), lambda m, s, p, r: (m, 0, 0, 0)),
            pl.BlockSpec((2, 128, 128), lambda m, s, p, r: (0, 0, 0)),
            pl.BlockSpec((2, 32, 128), lambda m, s, p, r: (0, 0, 0)),
        ],
        out_specs=[
            pl.BlockSpec((1, 4, 256, 128), lambda m, s, p, r: (m, 0, 0, 0)),
            pl.BlockSpec((1, 16, 2, 256, 128), lambda m, s, p, r: (m, 0, 0, 0, 0)),
        ],
        scratch_shapes=[
            pltpu.VMEM((4096, 128), BF),
            pltpu.VMEM((128, 4096), BF),
            pltpu.VMEM((4096, 128), BF),
            pltpu.VMEM((4096, 128), F32),
            pltpu.VMEM((4096, 128), F32),
            pltpu.VMEM((8, 256, 128), BF),
            pltpu.VMEM((8, 128, 256), BF),
            pltpu.VMEM((8, 256, 128), BF),
            pltpu.VMEM((8, 128, 256), BF),
            pltpu.VMEM((8, 8, 256), F32),
            pltpu.VMEM((TILE, 256), F32),
            pltpu.VMEM((TILE, 256), F32),
            pltpu.VMEM((TILE, 256), F32),
            pltpu.VMEM((TILE, 256), F32),
            pltpu.VMEM((TILE, 256), BF),
            pltpu.VMEM((TILE, 256), BF),
            pltpu.VMEM((TILE, 256), BF),
            pltpu.VMEM((TILE, 256), BF),
            pltpu.VMEM((8, 128, 256), F32),
        ],
    )
    return pl.pallas_call(
        kernel,
        name="attend_back",
        grid_spec=grid_spec,
        out_shape=[
            jax.ShapeDtypeStruct((2, 4, 256, 128), BF),
            jax.ShapeDtypeStruct((2, 16, 2, 256, 128), BF),
        ],
        compiler_params=pltpu.CompilerParams(vmem_limit_bytes=VMEM_LIMIT),
    )(slots, places, rows_of, spread, spread, spread, full, logs, upstream, base, steps)


def tn(left, right):
    return lax.dot_general(left, right, (((0,), (0,)), ((), ())), preferred_element_type=F32)


def feed_forward(second_low, dy, weights):
    def kernel(
        low_hbm, dy_hbm, w_hbm, branch, dsecond, gate_out, up_out, down_out,
        low, dys, gate_w, up_w, down_w, gate, up, dmixed, mixed, dgate, dup, chunks, sems, chunk_sems,
    ):
        def load(n, src, dst):
            copy = pltpu.make_async_copy(src, dst, sems.at[n])
            copy.start()
            return copy

        def columns(k):
            return w_hbm.at[:, pl.ds(k * UNITS, UNITS)]

        loads = [
            load(0, low_hbm, low),
            load(1, columns(0), gate_w),
            load(2, columns(1), up_w),
            load(3, dy_hbm, dys),
            load(4, columns(2), down_w),
        ]
        loads[0].wait()
        loads[1].wait()
        gate[...] = jnp.dot(low[...], gate_w[...], preferred_element_type=F32)
        loads[2].wait()
        up[...] = jnp.dot(low[...], up_w[...], preferred_element_type=F32)
        loads[3].wait()
        loads[4].wait()
        dmixed[...] = jnp.dot(dys[...], down_w[...], preferred_element_type=F32)

        def step(i, carry):
            rows = pl.ds(pl.multiple_of(i * 16, 16), 16)
            g, u, d = gate[rows, :], up[rows, :], dmixed[rows, :]
            s = jax.nn.sigmoid(g)
            silu = g * s
            mixed[rows, :] = (silu * u).astype(BF)
            dgate[rows, :] = (d * u * s * (1.0 + g * (1.0 - s))).astype(BF)
            dup[rows, :] = (d * silu).astype(BF)
            return carry

        lax.fori_loop(0, 32, step, 0)
        dsecond[...] = (nt(dgate[...], gate_w[...]) + nt(dup[...], up_w[...])).astype(BF)
        busy = {}
        n = 0
        for left, right, out in ((low, dgate, gate_out), (low, dup, up_out), (dys, mixed, down_out)):
            for k in range(4):
                rows = pl.ds(k * 512, 512)
                slot = n % 2
                if slot in busy:
                    busy[slot].wait()
                chunks[slot] = tn(left[:, rows], right[...]).astype(BF)
                busy[slot] = pltpu.make_async_copy(chunks.at[slot], out.at[rows, :], chunk_sems.at[slot])
                busy[slot].start()
                n += 1
        branch[...] = nt(mixed[...], down_w[...]).astype(BF)
        busy[0].wait()
        busy[1].wait()

    return pl.pallas_call(
        kernel,
        name="feed_forward",
        in_specs=[ANY, ANY, ANY],
        out_specs=[IN_VMEM, IN_VMEM, ANY, ANY, ANY],
        out_shape=[jax.ShapeDtypeStruct((512, D), BF)] * 2 + [jax.ShapeDtypeStruct((D, UNITS), BF)] * 3,
        scratch_shapes=[pltpu.VMEM((512, D), BF)] * 2
        + [pltpu.VMEM((D, UNITS), BF)] * 3
        + [pltpu.VMEM((512, UNITS), F32)] * 3
        + [pltpu.VMEM((512, UNITS), BF)] * 3
        + [
            pltpu.VMEM((2, 512, UNITS), BF),
            pltpu.SemaphoreType.DMA((5,)),
            pltpu.SemaphoreType.DMA((2,)),
        ],
        compiler_params=pltpu.CompilerParams(vmem_limit_bytes=VMEM_LIMIT),
    )(second_low, dy, weights)


def project_back(dproject, first_low, front):
    def kernel(dp_ref, low_ref, w_hbm, dfirst, grad_out, bias_out, wide, weights, chunks, sems, chunk_sems):
        load = pltpu.make_async_copy(w_hbm.at[:, pl.ds(0, 1536)], weights, sems.at[0])
        load.start()
        for m in range(2):
            for t in range(3):
                for h in range(4):
                    to = t * 512 + h * 128
                    wide[m * 256 : m * 256 + 256, to : to + 128] = dp_ref[m, h, (t + 2) % 3]
        bias_out[...] = jnp.sum(wide[...].astype(F32), axis=0, keepdims=True)
        busy = {}
        for k in range(4):
            rows = pl.ds(k * 512, 512)
            slot = k % 2
            if slot in busy:
                busy[slot].wait()
            chunks[slot] = tn(low_ref[:, rows], wide[...]).astype(BF)
            busy[slot] = pltpu.make_async_copy(chunks.at[slot], grad_out.at[rows, :], chunk_sems.at[slot])
            busy[slot].start()
        load.wait()
        dfirst[...] = nt(wide[...], weights[...]).astype(BF)
        busy[0].wait()
        busy[1].wait()

    return pl.pallas_call(
        kernel,
        name="project_back",
        in_specs=[IN_VMEM, IN_VMEM, ANY],
        out_specs=[IN_VMEM, ANY, IN_VMEM],
        out_shape=[
            jax.ShapeDtypeStruct((512, D), BF),
            jax.ShapeDtypeStruct((D, 1536), BF),
            jax.ShapeDtypeStruct((1, 1536), F32),
        ],
        scratch_shapes=[
            pltpu.VMEM((512, 1536), BF),
            pltpu.VMEM((D, 1536), BF),
            pltpu.VMEM((2, 512, 1536), BF),
            pltpu.SemaphoreType.DMA((1,)),
            pltpu.SemaphoreType.DMA((2,)),
        ],
        compiler_params=pltpu.CompilerParams(vmem_limit_bytes=VMEM_LIMIT),
    )(dproject, first_low, front)


def rotary_tables(places):
    lane = np.arange(128) % HEAD_DIM
    power = 10000.0 ** (-jnp.arange(0, ROT, 2, dtype=F32) / ROT)
    hot = (lane[None, :] % (ROT // 2) == np.arange(ROT // 2)[:, None]) & (lane[None, :] < ROT)
    frequency = jnp.sum(jnp.where(hot, power[:, None], 0.0), axis=0)
    angles = places.astype(F32)[:, None] * frequency[None, :]
    return jnp.stack([jnp.cos(angles), jnp.sin(angles)])


def angle_tables():
    near = jnp.arange(128, dtype=jnp.int32)
    return rotary_tables(near), rotary_tables(near[:32] * 128)


def body(
    inputs,
    cotangent,
    group_place,
    attend_gain,
    attend_shift,
    project_weight,
    project_bias,
    output_weight,
    mixer_gain,
    mixer_shift,
    gate_weight,
    up_weight,
    down_weight,
):
    ctx = lax.axis_index("ctx")
    y, z = ctx // 4, lax.rem(ctx, 4)
    shard_index = lax.axis_index("dp") * 16 + ctx

    blocks = jnp.arange(32, dtype=jnp.int32)
    hits = group_place[None, :] == blocks[:, None]
    slots = jnp.sum(jnp.where(hits, blocks[None, :], 0), axis=1)
    four = jnp.arange(4, dtype=jnp.int32)
    rows_of = jnp.concatenate([y * 4 + four, four * 4 + z])
    held_slots = (rows_of[:, None] * 2 + jnp.arange(2, dtype=jnp.int32)[None, :]).reshape(16)
    chosen = held_slots[:, None] == blocks[None, :]
    places = jnp.sum(jnp.where(chosen, group_place[None, :], 0), axis=1)
    own_slots = ctx * 2 + jnp.arange(2, dtype=jnp.int32)
    own_blocks = jnp.sum(
        jnp.where(own_slots[:, None] == blocks[None, :], group_place[None, :], 0), axis=1
    )
    own_places = (own_blocks[:, None] * 128 + jnp.arange(128, dtype=jnp.int32)[None, :]).reshape(256)
    own_tables = rotary_tables(own_places)
    all_tables = angle_tables()

    vectors = jnp.concatenate(
        [
            jnp.stack([attend_gain, attend_shift, mixer_gain, mixer_shift], axis=1),
            jnp.pad(project_bias.reshape(1, 48), ((0, 63), (0, 0))),
            jnp.zeros((64, 76), BF),
        ],
        axis=1,
    )
    front_shard = jnp.concatenate(
        [project_weight.reshape(64, 1536), output_weight.T, vectors], axis=1
    )
    back_shard = jnp.concatenate([gate_weight, up_weight, down_weight.T], axis=1)
    front = gather_front(front_shard).reshape(D, 2176)
    gains = front[:, 2048:2052].astype(F32).T
    first_gain, first_shift = gains[0:1], gains[1:2]
    second_gain, second_shift = gains[2:3], gains[3:4]
    bias = (
        front.reshape(32, 64, 2176)[:, 0, 2052:2100]
        .reshape(32, 3, 8, 2)
        .transpose(1, 2, 0, 3)
        .astype(F32)
        .reshape(1, 1536)
    )
    output_t = front[:, 1536:2048]

    tokens = inputs.reshape(512, D)
    quarters = inputs.reshape(4, 128, D)
    qkv, first_low = project_heads(tokens, first_gain, first_shift, front, bias, own_tables)
    spread = spread_heads(qkv).reshape(2, 16, 3, 256, 128)
    attended_heads, attended_full, logs = attend(slots, places, rows_of, spread)
    attended_low = (
        swap_rows(attended_heads, 2, "attended_back").transpose(0, 2, 1, 3).reshape(512, 512)
    )
    branch = nt(attended_low, output_t).astype(BF).reshape(4, 128, D)
    hidden, second_low, back = middle_forward(branch, quarters, second_gain, second_shift, back_shard)

    mixer_part, second_part, gate_grad, up_grad, down_grad = feed_forward(
        second_low.reshape(512, D), cotangent.reshape(512, D), back.reshape(D, 3 * UNITS)
    )

    def shards(grad):
        return grad.reshape(2, 4, 4, 64, grad.shape[1])

    dhidden, hidden_low, mixer_vectors, gate_grad, up_grad, down_grad = middle_backward(
        second_part.reshape(4, 128, D),
        cotangent.reshape(4, 128, D),
        hidden,
        second_gain,
        [shards(gate_grad), shards(up_grad), shards(down_grad)],
    )

    hidden_low = hidden_low.reshape(512, D)
    dattended = jnp.dot(hidden_low, output_t, preferred_element_type=F32).astype(BF)
    upstream = swap_rows(
        dattended.reshape(2, 256, 4, 128).transpose(0, 2, 1, 3), 5, "dattended_out"
    )
    output_grad = shards(tn(hidden_low, attended_low).astype(BF))
    dq, dkv = attend_back(
        slots, places, rows_of, spread, attended_full, logs, upstream, all_tables
    )
    dproject, outputs = collect_heads(dkv.reshape(2, 4, 4, 2, 256, 128), dq, mixer_part.reshape(4, 128, D), hidden)
    first_part, project_grad, bias_part = project_back(dproject, first_low, front)
    small = jnp.concatenate(
        [
            jnp.zeros((2, D), F32),
            mixer_vectors,
            jnp.pad(bias_part, ((0, 0), (0, D - 1536))),
            jnp.zeros((3, D), F32),
        ]
    )
    input_grad, small, project_grad, output_grad = last_backward(
        first_part.reshape(4, 128, D),
        quarters,
        dhidden,
        first_gain,
        small,
        [shards(project_grad), output_grad],
    )
    own = lax.dynamic_slice(small, (0, shard_index * 64), (4, 64))
    bias_grad = lax.dynamic_slice(
        small[4, :1536].reshape(3, 8, 64), (0, 0, shard_index * 2), (3, 8, 2)
    )
    shape = inputs.shape
    return (
        outputs.reshape(shape),
        input_grad.reshape(shape),
        own[0],
        own[1],
        project_grad.reshape(64, 3, 512),
        bias_grad,
        output_grad.T,
        own[2],
        own[3],
        gate_grad,
        up_grad,
        down_grad.T,
    )


def solution(mesh):
    weight = ("dp", "ctx")
    rows = P(None, "dp", "ctx", None)
    vector = P(weight)
    matrix = P(weight, "tensor")
    turned = P("tensor", weight)
    project = P(weight, None, "tensor")
    bias = P(None, "tensor", weight)
    params = (vector, vector, project, bias, turned, vector, vector, matrix, matrix, turned)
    return jax.shard_map(
        body,
        mesh=mesh,
        in_specs=(rows, rows, P()) + params,
        out_specs=(rows, rows) + params,
        check_vma=False,
    )
```

time: 660 us -> 497 us (0.75); the launches traced: 649 us -> 494 us
  matrix products: 86.9 us -> 10.4 us
  local copies, waits for them, and re-layouts: 64.9 us -> 23.5 us
  Pallas kernels: 472 us -> 449 us
  other arithmetic: 23.8 us -> 10.1 us
    pallas_call x1 -> x3, Pallas kernels: 21.2 us -> 62.9 us  [the longest x1 40.1 us: feed_forward(): pl.pallas_call(kernel, name='feed_forward', in_specs=[ANY, ANY, ANY], out...]
    dot_general x3 -> x0, matrix products: 26.8 us -> none  [the longest x1 11.1 us: body(): up_value = jnp.dot(second_low, up_w, preferred_element_type=F32)]
    dot_general x5 -> x1, matrix products: 31 us -> 4.26 us  [nt(): lax.dot_general(left, right, (((1,), (1,)), ((), ())), preferred_element_...]
    pallas_call x1, Pallas kernels: 50.2 us -> 23.7 us  [attend(): pl.pallas_call(kernel, name='attend', grid_spec=grid_spec, out_shape=[jax...]
    concatenate x6 -> x0, local copies, waits for them, and re-layouts: 25.7 us -> none  [rotary_tables(): return jnp.stack([jnp.concatenate([t, t], axis=1) for t in tables])]
    dot_general x5 -> x1, matrix products: 25.4 us -> 2.64 us  [tn(): lax.dot_general(left, right, (((0,), (0,)), ((), ())), preferred_element_...]
    pallas_call x1, Pallas kernels: 58.2 us -> 43 us  [attend_back(): pl.pallas_call(kernel, name='attend_back', grid_spec=grid_spec, out_shape...]
    cos x2 -> x3, other arithmetic: 9.87 us -> 0.98 us  [rotary_tables(): return jnp.stack([jnp.cos(angles), jnp.sin(angles)])]
where the time goes in v2:
time: 497 us; the launch traced here: 494 us
  Pallas kernels  449 us (90%)
  local copies, waits for them, and re-layouts  23.5 us (5%)
  matrix products  10.4 us (2%)
  other arithmetic  10.1 us (2%)
    pallas_call x1, Pallas kernels, middle_forward(): remote_call(kernel, 'middle_forward', 3, [ANY, ANY, IN_VMEM, IN_VMEM, ANY...  68.7 us
    pallas_call x1, Pallas kernels, middle_backward(): remote_call(kernel, 'middle_backward', 4, [ANY, ANY, IN_VMEM, IN_VMEM] +...  66.8 us
    pallas_call x1, Pallas kernels, last_backward(): remote_call(kernel, 'last_backward', 7, [ANY, ANY, IN_VMEM, IN_VMEM, IN_V...  59.7 us
    pallas_call x1, Pallas kernels, collect_heads(): remote_call(kernel, 'collect_heads', 6, [ANY, ANY, ANY, IN_VMEM], [((2, 4...  44.1 us
    pallas_call x1, Pallas kernels, attend_back(): pl.pallas_call(kernel, name='attend_back', grid_spec=grid_spec, out_shape...  43 us
    pallas_call x1, Pallas kernels, feed_forward(): pl.pallas_call(kernel, name='feed_forward', in_specs=[ANY, ANY, ANY], out...  40.1 us
    pallas_call x1, Pallas kernels, gather_front(): remote_call(kernel, 'gather_front', 0, [ANY], [((2, 4, 4, 64, width), BF,...  35 us
    pallas_call x1, Pallas kernels, spread_heads(): remote_call(kernel, 'spread_heads', 1, [ANY], [((2, 4, 4, 3, 256, 128), B...  31.7 us

profile of v2, /device:TPU:1, one launch (start us, length us, event | category | flops | bytes accessed | tf_op | source)
XLA Modules:
  0.0 494.5 jit_solution(10695942802623484635)
XLA Ops:
  0.6 1.3 select_reduce_fusion.slots
  2.7 1.4 select_reduce_fusion.1.places
  8.9 1.7 concatenate.17.src
  10.6 35.0 %gather_front.1 = bf16[2,4,4,64,2176]{4,3,2,1,0:T(8,128)(2,1)} custom-call(bf16[64,2176]{1,0:T(8,128)(2,1)} %concatenate.17.src), custom_call_target="tpu_custom_call" | custom-call | tf_op jit(solution)/shard_map/gather_front/pallas_call | solution.py:465
  51.5 11.5 %project_heads.1 = (bf16[2,4,3,256,128]{4,3,2,1,0:T(8,128)(2,1)}, bf16[512,2048]{1,0:T(8,128)(2,1)}) custom-call(bf16[512,2048]{1,0:T(8,128)(2,1)} %bitcast.82, f32[1,2048]{1,0:T(1,128)} %get-tuple-element.113.gain_ref.gain, f32[1,2048]{1,0:T(1,128)} %get-tuple-element.112.shift_ref, bf16[2048,2176]{1,0:T(8,128)(2,1)} %bitcast.78, ...), custom_call_target="tpu_custom_call" | custom-call | tf_op jit(solution)/shard_map/project_heads/pallas_call | solution.py:885
  63.0 31.7 %spread_heads.1 = bf16[2,4,4,3,256,128]{5,4,3,2,1,0:T(8,128)(2,1)} custom-call(bf16[2,4,3,256,128]{4,3,2,1,0:T(8,128)(2,1)} %get-tuple-element.42.src), custom_call_target="tpu_custom_call" | custom-call | tf_op jit(solution)/shard_map/spread_heads/pallas_call | solution.py:512
  94.7 23.7 %attend.1 = (bf16[2,4,256,128]{3,2,1,0:T(8,128)(2,1)}, f32[2,4,256,128]{3,2,1,0:T(8,128)}, f32[2,8,256]{2,1,0:T(8,128)}) custom-call(s32[32]{0:T(128)} %select_reduce_fusion.slots, s32[16]{0:T(128)} %select_reduce_fusion.1.places, s32[8]{0:T(128)} %get-tuple-element.109.rows_of, bf16[2,16,3,256,128]{4,3,2,1,0:T(8,128)(2,1)} %bitcast.70, ...), custom_call_target="tpu_custom_call" | custom-call | tf_op jit(solution)/shard_map/attend/pallas_call | solution.py:1057
  118.4 6.4 %attended_back.1 = bf16[2,4,256,128]{3,2,1,0:T(8,128)(2,1)} custom-call(bf16[2,4,256,128]{3,2,1,0:T(8,128)(2,1)} %get-tuple-element.45.src), custom_call_target="tpu_custom_call" | custom-call | tf_op jit(solution)/shard_map/attended_back/pallas_call | solution.py:534
  124.8 1.4 copy.65
  126.3 4.3 convolution_convert_fusion.1
  131.5 68.7 %middle_forward.1 = (f32[128,2048]{1,0:T(8,128)}, bf16[4,128,2048]{2,1,0:T(8,128)(2,1)}, bf16[2,4,4,64,4224]{4,3,2,1,0:T(8,128)(2,1)}) custom-call(bf16[4,128,2048]{2,1,0:T(8,128)(2,1)} %bitcast.94, bf16[4,128,2048]{2,1,0:T(8,128)(2,1)} %bitcast.83, f32[1,2048]{1,0:T(1,128)} %get-tuple-element.111.gain, f32[1,2048]{1,0:T(1,128)} %get-tuple-element.110.shift, ...), custom_call_target="tpu_custom_call" | custom-call | tf_op jit(solution)/shard_map/middle_forward/pallas_call | solution.py:569
  200.1 40.1 %feed_forward.1 = (bf16[512,2048]{1,0:T(8,128)(2,1)}, bf16[512,2048]{1,0:T(8,128)(2,1)}, bf16[2048,1408]{1,0:T(8,128)(2,1)}, bf16[2048,1408]{1,0:T(8,128)(2,1)}, bf16[2048,1408]{1,0:T(8,128)(2,1)}) custom-call(bf16[512,2048]{1,0:T(8,128)(2,1)} %bitcast.102, bf16[512,2048]{1,0:T(8,128)(2,1)} %bitcast.86, bf16[2048,4224]{1,0:T(8,128)(2,1)} %bitcast.85), custom_call_target="tpu_custom_call" | custom-call | tf_op jit(solution)/shard_map/feed_forward/pallas_call | solution.py:1289
  240.2 66.8 %middle_backward.1 = (f32[128,2048]{1,0:T(8,128)}, bf16[4,128,2048]{2,1,0:T(8,128)(2,1)}, f32[2,2048]{1,0:T(2,128)}, f32[64,1408]{1,0:T(8,128)}, f32[64,1408]{1,0:T(8,128)}, /*index=5*/f32[64,1408]{1,0:T(8,128)}) custom-call(bf16[4,128,2048]{2,1,0:T(8,128)(2,1)} %bitcast.93, bf16[4,128,2048]{2,1,0:T(8,128)(2,1)} %bitcast.87, ...), custom_call_target="tpu_custom_call" | custom-call | tf_op jit(solution)/shard_map/middle_backward/pallas_call | solution.py:642
  307.0 3.5 fusion.3
  311.5 7.4 %dattended_out.1.up_ref = bf16[2,4,256,128]{3,2,1,0:T(8,128)(2,1)} custom-call(bf16[2,4,256,128]{3,2,1,0:T(8,128)(2,1)} %bitcast.98), custom_call_target="tpu_custom_call" | custom-call | tf_op jit(solution)/shard_map/dattended_out/pallas_call | solution.py:534
  320.7 43.0 %attend_back.1 = (bf16[2,4,256,128]{3,2,1,0:T(8,128)(2,1)}, bf16[2,16,2,256,128]{4,3,2,1,0:T(8,128)(2,1)}) custom-call(s32[32]{0:T(128)} %select_reduce_fusion.slots, s32[16]{0:T(128)} %select_reduce_fusion.1.places, s32[8]{0:T(128)} %get-tuple-element.109.rows_of, bf16[2,16,3,256,128]{4,3,2,1,0:T(8,128)(2,1)} %bitcast.73, ...), custom_call_target="tpu_custom_call" | custom-call | tf_op jit(solution)/shard_map/attend_back/pallas_call | solution.py:1216
  363.6 44.1 %collect_heads.1 = (bf16[2,4,3,256,128]{4,3,2,1,0:T(8,128)(2,1)}, bf16[4,128,2048]{2,1,0:T(8,128)(2,1)}) custom-call(bf16[2,4,4,2,256,128]{5,4,3,2,1,0:T(8,128)(2,1)} %bitcast.92, bf16[2,4,256,128]{3,2,1,0:T(8,128)(2,1)} %get-tuple-element.55.dq, bf16[4,128,2048]{2,1,0:T(8,128)(2,1)} %bitcast.99, f32[128,2048]{1,0:T(8,128)} %get-tuple-element.49.hidden), custom_call_target="tpu_custom_call" | custom-call | tf_op jit(solution)/shard_map/collect_heads/pallas_call | solution.py:737
  407.8 11.4 %project_back.1 = (bf16[512,2048]{1,0:T(8,128)(2,1)}, bf16[2048,1536]{1,0:T(8,128)(2,1)}, f32[1,1536]{1,0:T(1,128)}) custom-call(bf16[2,4,3,256,128]{4,3,2,1,0:T(8,128)(2,1)} %get-tuple-element.58.dp_ref, bf16[512,2048]{1,0:T(8,128)(2,1)} %get-tuple-element.59.low_ref, bf16[2048,2176]{1,0:T(8,128)(2,1)} %bitcast.81), custom_call_target="tpu_custom_call" | custom-call | tf_op jit(solution)/shard_map/project_back/pallas_call | solution.py:1332
  419.3 1.4 fusion.10.vectors
  420.7 2.6 convolution_convert_fusion
  423.3 59.7 %last_backward.1 = (bf16[4,128,2048]{2,1,0:T(8,128)(2,1)}, f32[8,2048]{1,0:T(8,128)}, f32[64,1536]{1,0:T(8,128)}, f32[64,512]{1,0:T(8,128)}) custom-call(bf16[4,128,2048]{2,1,0:T(8,128)(2,1)} %bitcast.100, bf16[4,128,2048]{2,1,0:T(8,128)(2,1)} %bitcast.84, f32[128,2048]{1,0:T(8,128)} %get-tuple-element.61.dhidden, ...), custom_call_target="tpu_custom_call" | custom-call | tf_op jit(solution)/shard_map/last_backward/pallas_call | solution.py:838
  484.3 1.8 copy.89
  487.8 1.3 copy.96
  490.1 1.3 copy.97
  (79 shorter events, 22.0 us)
Async XLA Ops:
  45.6 4.2 copy-start.10
  45.6 4.3 copy-start.12
  126.3 4.3 copy-start.5
  126.3 4.3 copy-start.6
  126.3 4.3 copy-start.7
  407.8 11.5 %copy-start.9 = (f32[2,2048]{1,0:T(2,128)S(1)}, f32[2,2048]{1,0:T(2,128)}, u32[]{:S(2)}) copy-start(f32[2,2048]{1,0:T(2,128)} %get-tuple-element.62) | copy-start | bytes 49156
  407.8 12.9 %copy-start.11 = (bf16[4,128,2048]{2,1,0:T(8,128)(2,1)S(1)}, bf16[4,128,2048]{2,1,0:T(8,128)(2,1)}, u32[]{:S(2)}) copy-start(bf16[4,128,2048]{2,1,0:T(8,128)(2,1)} %get-tuple-element.53) | copy-start | bytes 6291460
  423.3 64.4 %copy-start = (bf16[4,128,2048]{2,1,0:T(8,128)(2,1)S(1)}, bf16[4,128,2048]{2,1,0:T(8,128)(2,1)}, u32[]{:S(2)}) copy-start(bf16[4,128,2048]{2,1,0:T(8,128)(2,1)} %get-tuple-element.57) | copy-start | bytes 6291460
  487.7 2.3 copy-start.1
  490.1 1.3 copy-start.8
  490.1 2.0 copy-start.4
  490.1 2.7 copy-start.3
  490.1 3.5 copy-start.2

commit v3 on v2

--- a/solution.py
+++ b/solution.py
@@ -156,28 +156,26 @@
 
 
 class Gather:
-    def __init__(self, net, local, src, out, me):
-        self.net, self.local, self.src, self.out, self.me = net, local, src, out, me
+    def __init__(self, net, local, src, place, me):
+        self.net, self.local, self.src, self.place, self.me = net, local, src, place, me
         self.core = []
         c, y, z, x = me
         along_y = lambda d: at(c, y + d, z, x)
         along_z = lambda d: at(c, y, z + d, x)
 
-        def rows(first, half):
-            return pl.ds(first, 32) if half is None else pl.ds(first + 16 * half, 16)
+        def spot(far_y, far_z, first, half):
+            if half is None:
+                return place(c, up(y, far_y), up(z, far_z), first, 32)
+            return place(c, up(y, far_y), up(z, far_z), first + 16 * half, 16)
 
         self.one = (
-            RingGather(net, along_y, lambda d, half=None: out.at[c, up(y, d), z, rows(0, half)]),
-            RingGather(net, along_z, lambda d, half=None: out.at[c, y, up(z, d), rows(32, half)]),
+            RingGather(net, along_y, lambda d, half=None: spot(d, 0, 0, half)),
+            RingGather(net, along_z, lambda d, half=None: spot(0, d, 32, half)),
         )
         self.two = {}
         for k in range(4):
-            self.two[0, k] = RingGather(
-                net, along_z, lambda d, half=None, k=k: out.at[c, up(y, k), up(z, d), rows(0, half)]
-            )
-            self.two[1, k] = RingGather(
-                net, along_y, lambda d, half=None, k=k: out.at[c, up(y, d), up(z, k), rows(32, half)]
-            )
+            self.two[0, k] = RingGather(net, along_z, lambda d, half=None, k=k: spot(k, d, 0, half))
+            self.two[1, k] = RingGather(net, along_y, lambda d, half=None, k=k: spot(d, k, 32, half))
 
     def hand_over(self, piece):
         c, y, z, x = self.me
@@ -185,14 +183,14 @@
 
     def start(self):
         c, y, z, x = self.me
-        src = self.src
-        self.own = self.local.copy(src, self.out.at[c, y, z])
+        src, own = self.src, self.place(c, y, z, 0, 64)
+        self.own = self.local.copy(src, own)
         halves = (src.at[pl.ds(0, 32)], src.at[pl.ds(32, 32)])
         for way in range(2):
             self.one[way].start(halves[way])
         for way in range(2):
             self.two[way, 0].start(halves[way])
-        self.core.append(self.net.send(src, self.out.at[c, y, z], at(1 - c, y, z, x)))
+        self.core.append(self.net.send(src, own, at(1 - c, y, z, x)))
 
     def near(self):
         for way in range(2):
@@ -204,6 +202,8 @@
         for k in (3, 1):
             for way in range(2):
                 self.hand_over(self.one[way].out(k))
+
+    def middle(self):
         self.pass_on(0)
         for way in range(2):
             self.one[way].arrive()
@@ -229,6 +229,13 @@
         for copy in self.core:
             copy.wait_recv()
         self.own.wait()
+
+
+def flat_rows(ref):
+    def place(c, y, z, first, count):
+        return ref.at[pl.ds(pl.multiple_of(((c * 4 + y) * 4 + z) * 64 + first, 16), count)]
+
+    return place
 
 
 GATHER_COPIES = 10 * RING_GATHER + 31
@@ -365,6 +372,9 @@
             copy.wait()
         self.ring.start()
 
+    def start_held(self):
+        self.ring.start()
+
     def middle(self):
         self.ring.middle()
 
@@ -374,15 +384,15 @@
             terms = self.ring.terms(half)
 
             def loop(i, carry, half=half, terms=terms):
-                rows = pl.ds(pl.multiple_of(i * 16, 16), 16)
-                own = pl.ds(pl.multiple_of(64 * half + i * 16, 16), 16)
+                rows = pl.ds(pl.multiple_of(i * 32, 32), 32)
+                own = pl.ds(pl.multiple_of(64 * half + i * 32, 32), 32)
                 value = self.held[self.x, own, :].astype(F32)
                 for term in terms:
                     value += term[rows, :].astype(F32)
                 step(own, value)
                 return carry
 
-            lax.fori_loop(0, 4, loop, 0)
+            lax.fori_loop(0, 2, loop, 0)
 
     def gather(self, block, out):
         x = self.x
@@ -449,114 +459,192 @@
     )
 
 
-def gather_front(shard):
-    def kernel(src, out, ss, rs, ls):
+def assemble_vectors(weights, gains, bias, spots):
+    for s in range(32):
+        block = weights[s * 64 : s * 64 + 16, 2048:2176].astype(F32)
+        for k in range(4):
+            side = (k % 2) * 64
+            gains[k : k + 1, s * 64 : s * 64 + 64] = block[k // 2 : k // 2 + 1, side : side + 64]
+        spots[s : s + 1, :] = block[2:3, :]
+    values = spots[...].astype(BF)
+    shard = lax.broadcasted_iota(jnp.int32, (32, 64), 0)
+    lane = lax.broadcasted_iota(jnp.int32, (32, 64), 1)
+    total = jnp.zeros((24, 64), F32)
+    for e in range(2):
+        pick = jnp.where(lane == 2 * shard + e, 1.0, 0.0).astype(BF)
+        total += tn(values, pick)[e * 24 : e * 24 + 24]
+    for n in range(24):
+        bias[0:1, n * 64 : n * 64 + 64] = total[n : n + 1]
+
+
+def front_forward(shard, tokens, tables):
+    def kernel(src, x_ref, t_ref, front, gains, low, out, weights, norm, blocks, bias, spots, ss, rs, ls):
         me = here()
+        c, y, z, x = me
+        net, local = Net(ss, rs), Local(ls)
         greet(y_peers(*me) + z_peers(*me) + core_peer(*me))
-        net, local = Net(ss, rs), Local(ls)
-        gather = Gather(net, local, src, out, me)
+        gather = Gather(net, local, src, flat_rows(weights), me)
         gather.start()
+
+        def centre(i, carry):
+            rows = pl.ds(pl.multiple_of(i * 32, 32), 32)
+            norm[rows, :] = normed(x_ref[rows, :].astype(F32))[0]
+            return carry
+
+        lax.fori_loop(0, 4, centre, 0)
         gather.near()
+        lax.fori_loop(4, 8, centre, 0)
+        gather.middle()
+        lax.fori_loop(8, 16, centre, 0)
         gather.far()
         gather.finish()
-        net.finish()
-
-    width = shard.shape[1]
-    return remote_call(
-        kernel, "gather_front", 0, [ANY], [((2, 4, 4, 64, width), BF, ANY)], [], GATHER_COPIES, 1
-    )(shard)[0]
-
-
-def spread_heads(qkv):
-    def kernel(src, out, ss, rs, ls):
-        me = here()
-        c, y, z, x = me
-        greet(y_peers(*me) + z_peers(*me))
-        net, local = Net(ss, rs), Local(ls)
-        kv = pl.ds(0, 2)
-        owns = [local.copy(src.at[0, z], out.at[0, y, z]), local.copy(src.at[1, y], out.at[1, y, z])]
-        first, second = {}, {}
+        keep = local.copy(weights, front)
+        assemble_vectors(weights, gains, bias, spots)
+
+        def scale(i, carry):
+            rows = pl.ds(pl.multiple_of(i * 32, 32), 32)
+            low[rows, :] = (norm[rows, :] * gains[0:1, :] + gains[1:2, :]).astype(BF)
+            return carry
+
+        lax.fori_loop(0, 16, scale, 0)
+
+        def project(t):
+            columns = slice(t * 512, t * 512 + 512)
+            for m in range(2):
+                acc = jnp.dot(low[m * 256 : m * 256 + 256, :], weights[:, columns], preferred_element_type=F32)
+                acc = acc + bias[:, columns]
+                for h in range(4):
+                    part = acc[:, h * 128 : h * 128 + 128]
+                    if t < 2:
+                        part = turn(part, t_ref[0], t_ref[1])
+                    blocks[m, h, (t + 2) % 3] = part.astype(BF)
+
         along_y = lambda d: at(c, y + d, z, x)
         along_z = lambda d: at(c, y, z + d, x)
+        kv = pl.ds(0, 2)
 
         def part(half):
             return kv if half is None else half
 
+        rings = {}
         for k in range(4):
-            second[0, k] = RingGather(
+            rings[0, k] = RingGather(
                 net, along_y, lambda d, half=None, k=k: out.at[0, up(y, d), up(z, k), part(half)]
             )
-            second[1, k] = RingGather(
+            rings[1, k] = RingGather(
                 net, along_z, lambda d, half=None, k=k: out.at[1, up(y, k), up(z, d), part(half)]
             )
+        project(1)
+        project(2)
+        first = {}
         for d in STEPS:
-            first[0, d] = net.send(src.at[0, up(z, d)], out.at[0, y, z], along_z(d))
-            first[1, d] = net.send(src.at[1, up(y, d)], out.at[1, y, z], along_y(d))
-        second[0, 0].start(src.at[0, z, kv])
-        second[1, 0].start(src.at[1, y, kv])
+            first[0, d] = net.send(blocks.at[0, up(z, d), kv], out.at[0, y, z, kv], along_z(d))
+            first[1, d] = net.send(blocks.at[1, up(y, d), kv], out.at[1, y, z, kv], along_y(d))
+        rings[0, 0].start(blocks.at[0, z, kv])
+        rings[1, 0].start(blocks.at[1, y, kv])
+        project(0)
+        last = []
+        for d in STEPS:
+            last.append(net.send(blocks.at[0, up(z, d), 2], out.at[0, y, z, 2], along_z(d)))
+            last.append(net.send(blocks.at[1, up(y, d), 2], out.at[1, y, z, 2], along_y(d)))
+        owns = [local.copy(blocks.at[0, z], out.at[0, y, z]), local.copy(blocks.at[1, y], out.at[1, y, z])]
         for d in STEPS:
             for m in range(2):
                 first[m, d].wait_recv()
-                ring = second[m, 4 - d]
+                ring = rings[m, 4 - d]
                 ring.start(ring.out(0))
         for k in (0, 3, 1, 2):
             for m in range(2):
-                second[m, k].from_back()
-                second[m, k].from_ahead()
-        for ring in second.values():
+                rings[m, k].from_back()
+                rings[m, k].from_ahead()
+        for ring in rings.values():
             ring.arrive()
-        for copy in owns:
-            copy.wait()
-        net.finish()
-
-    return remote_call(
-        kernel, "spread_heads", 1, [ANY], [((2, 4, 4, 3, 256, 128), BF, ANY)], [], 6 + 8 * RING_GATHER, 2
-    )(qkv)[0]
-
-
-def swap_rows(blocks, cid, name):
-    def kernel(src, out, ss, rs, ls):
-        me = here()
-        c, y, z, x = me
-        greet(y_peers(*me) + z_peers(*me))
-        net, local = Net(ss, rs), Local(ls)
-        owns = [local.copy(src.at[0, z], out.at[0, z]), local.copy(src.at[1, y], out.at[1, y])]
-        copies = []
-        for d in STEPS:
-            copies.append(net.send(src.at[0, up(z, d)], out.at[0, z], at(c, y, z + d, x)))
-            copies.append(net.send(src.at[1, up(y, d)], out.at[1, y], at(c, y + d, z, x)))
-        for copy in copies:
+        for copy in last:
             copy.wait_recv()
         for copy in owns:
             copy.wait()
+        keep.wait()
         net.finish()
 
-    return remote_call(kernel, name, cid, [ANY], [((2, 4, 256, 128), BF, ANY)], [], 6, 2)(blocks)[0]
-
-
-def middle_forward(parts, inputs, gain, shift, shard):
     width = shard.shape[1]
-
-    def kernel(parts, inputs, gain, shift, shard, hidden, second, weights, held, spare, base, low, ss, rs, ls):
+    return remote_call(
+        kernel,
+        "front_forward",
+        0,
+        [ANY, IN_VMEM, IN_VMEM],
+        [
+            ((D, width), BF, ANY),
+            ((4, D), F32, IN_VMEM),
+            ((512, D), BF, IN_VMEM),
+            ((2, 4, 4, 3, 256, 128), BF, ANY),
+        ],
+        [
+            pltpu.VMEM((D, width), BF),
+            pltpu.VMEM((512, D), F32),
+            pltpu.VMEM((2, 4, 3, 256, 128), BF),
+            pltpu.VMEM((1, 1536), F32),
+            pltpu.VMEM((32, 128), F32),
+        ],
+        GATHER_COPIES + 12 + 8 * RING_GATHER,
+        4,
+    )(shard, tokens, tables)
+
+
+class Swap:
+    def __init__(self, net, local, src, out, me):
+        c, y, z, x = me
+        self.owns = [local.copy(src.at[0, z], out.at[0, z]), local.copy(src.at[1, y], out.at[1, y])]
+        self.copies = []
+        for d in STEPS:
+            self.copies.append(net.send(src.at[0, up(z, d)], out.at[0, z], at(c, y, z + d, x)))
+            self.copies.append(net.send(src.at[1, up(y, d)], out.at[1, y], at(c, y + d, z, x)))
+
+    def arrive(self):
+        for copy in self.copies:
+            copy.wait_recv()
+        for copy in self.owns:
+            copy.wait()
+
+
+SWAP_COPIES, SWAP_LOCALS = 6, 2
+TURNED = pl.ds(1536, 512)
+
+
+def middle_forward(heads, front, inputs, gains, shard):
+    width = shard.shape[1]
+
+    def kernel(
+        heads, front, inputs, gains, shard, attended, hidden, second, weights,
+        swapped, out_w, held, spare, base, low, ss, rs, ls,
+    ):
         me = here()
         c, y, z, x = me
         net, local = Net(ss, rs), Local(ls)
-        sums = SumX(net, local, parts, held, spare, me)
-        sums.load()
+        sums = SumX(net, local, None, held, spare, me)
+        load = local.copy(front.at[:, TURNED], out_w)
         residual = local.copy(inputs.at[x], base)
         greet(y_peers(*me) + z_peers(*me) + core_peer(*me) + x_peers(*me))
-        gather = Gather(net, local, shard, weights, me)
+        swap = Swap(net, local, heads, swapped, me)
+        gather = Gather(net, local, shard, flat_rows(weights), me)
         gather.start()
-        sums.start()
+        load.wait()
+        swap.arrive()
+        for m in range(2):
+            for h in range(4):
+                attended[m * 256 : m * 256 + 256, h * 128 : h * 128 + 128] = swapped[m, h]
+        for q in range(4):
+            held[q] = nt(attended[q * 128 : q * 128 + 128, :], out_w[...]).astype(BF)
+        sums.start_held()
         gather.near()
         sums.middle()
+        gather.middle()
         residual.wait()
 
         def step(rows, total):
             value = base[rows, :].astype(F32) + total
             hidden[rows, :] = value
             norm, _ = normed(value)
-            low[rows, :] = (norm * gain[...] + shift[...]).astype(BF)
+            low[rows, :] = (norm * gains[2:3, :] + gains[3:4, :]).astype(BF)
 
         sums.totals(step)
         sums.gather(low, second)
@@ -570,54 +658,58 @@
         kernel,
         "middle_forward",
         3,
-        [ANY, ANY, IN_VMEM, IN_VMEM, ANY],
+        [ANY, ANY, ANY, IN_VMEM, ANY],
         [
+            ((512, 512), BF, IN_VMEM),
             ((128, D), F32, IN_VMEM),
             ((4, 128, D), BF, ANY),
-            ((2, 4, 4, 64, width), BF, ANY),
+            ((D, width), BF, ANY),
         ],
-        sum_scratch() + [pltpu.VMEM((128, D), BF), pltpu.VMEM((128, D), BF)],
-        GATHER_COPIES + SUM_COPIES,
-        SUM_LOCALS + 2,
-    )(parts, inputs, gain, shift, shard)
-
-
-def middle_backward(parts, cotangent, hidden, gain, grads):
+        [pltpu.VMEM((2, 4, 256, 128), BF), pltpu.VMEM((D, 512), BF)]
+        + sum_scratch()
+        + [pltpu.VMEM((128, D), BF), pltpu.VMEM((128, D), BF)],
+        SWAP_COPIES + GATHER_COPIES + SUM_COPIES,
+        SWAP_LOCALS + SUM_LOCALS + 3,
+    )(heads, front, inputs, gains, shard)
+
+
+def middle_backward(parts, cotangent, hidden, gains, attended, front, grads):
     widths = [g.shape[-1] for g in grads]
     count = len(grads)
 
-    def kernel(parts, cotangent, hidden, gain, *rest):
+    def kernel(parts, cotangent, hidden, gains, attended, front, *rest):
         grad_refs = rest[:count]
-        dhidden, hidden_low, vectors = rest[count : count + 3]
-        outs = rest[count + 3 : 2 * count + 3]
-        held, spare, base, low = rest[2 * count + 3 : 2 * count + 7]
-        scratch = rest[2 * count + 7 : -3]
+        dhidden, vectors, output_grad, upstream = rest[count : count + 4]
+        outs = rest[count + 4 : 2 * count + 4]
+        held, spare, base, low, hidden_low, out_w, blocks = rest[2 * count + 4 : 2 * count + 11]
+        scratch = rest[2 * count + 11 : -3]
         ss, rs, ls = rest[-3:]
         me = here()
         c, y, z, x = me
         net, local = Net(ss, rs), Local(ls)
         sums = SumX(net, local, parts, held, spare, me)
         sums.load()
-        upstream = local.copy(cotangent.at[x], base)
+        upper = local.copy(cotangent.at[x], base)
+        load = local.copy(front.at[:, TURNED], out_w)
         greet(y_peers(*me) + z_peers(*me) + core_peer(*me) + x_peers(*me))
         scatters = [
             Scatter(net, local, grad_refs[k], outs[k], scratch[8 * k : 8 * k + 8], me)
             for k in range(count)
         ]
+        sums.start()
         for scatter in scatters:
             scatter.start()
-        sums.start()
-        for scatter in scatters:
+        scatters[0].first()
+        sums.middle()
+        for scatter in scatters[1:]:
             scatter.first()
-        sums.middle()
-        for scatter in scatters:
-            scatter.first_middle()
-        upstream.wait()
+        scatters[0].first_middle()
+        upper.wait()
         vectors[...] = jnp.zeros_like(vectors)
 
         def step(rows, dsecond):
             norm, inverse = normed(hidden[rows, :])
-            value = base[rows, :].astype(F32) + norm_pullback(dsecond, norm, inverse, gain[...])
+            value = base[rows, :].astype(F32) + norm_pullback(dsecond, norm, inverse, gains[2:3, :])
             dhidden[rows, :] = value
             low[rows, :] = value.astype(BF)
             vectors[0:1, :] += jnp.sum(dsecond * norm, axis=0, keepdims=True)
@@ -625,31 +717,54 @@
 
         sums.totals(step)
         sums.gather(low, hidden_low)
+        for scatter in scatters[1:]:
+            scatter.first_middle()
         scatters[0].second()
         sums.gather_middle()
         for scatter in scatters[1:]:
             scatter.second()
+        load.wait()
+        sums.finish()
+        for q in range(4):
+            rows = slice((q % 2) * 128, (q % 2) * 128 + 128)
+            result = jnp.dot(hidden_low[q], out_w[...], preferred_element_type=F32).astype(BF)
+            for h in range(4):
+                blocks[q // 2, h, rows, :] = result[:, h * 128 : h * 128 + 128]
+        swap = Swap(net, local, blocks, upstream, me)
         for scatter in scatters:
             scatter.second_middle()
+        whole = hidden_low[...].reshape(512, D)
+        output_grad[...] = tn(whole, attended[...]).astype(BF)
         for scatter in scatters:
             scatter.third()
-        sums.finish()
+        swap.arrive()
         net.finish()
 
-    scratch = sum_scratch() + [pltpu.VMEM((128, D), BF), pltpu.VMEM((128, D), BF)]
+    scratch = sum_scratch() + [
+        pltpu.VMEM((128, D), BF),
+        pltpu.VMEM((128, D), BF),
+        pltpu.VMEM((4, 128, D), BF),
+        pltpu.VMEM((D, 512), BF),
+        pltpu.VMEM((2, 4, 256, 128), BF),
+    ]
     for width in widths:
         scratch += scatter_scratch(width)
     return remote_call(
         kernel,
         "middle_backward",
         4,
-        [ANY, ANY, IN_VMEM, IN_VMEM] + [ANY] * count,
-        [((128, D), F32, IN_VMEM), ((4, 128, D), BF, ANY), ((2, D), F32, IN_VMEM)]
+        [ANY, ANY, IN_VMEM, IN_VMEM, IN_VMEM, ANY] + [ANY] * count,
+        [
+            ((128, D), F32, IN_VMEM),
+            ((2, D), F32, IN_VMEM),
+            ((D, 512), BF, IN_VMEM),
+            ((2, 4, 256, 128), BF, ANY),
+        ]
         + [((64, width), F32, IN_VMEM) for width in widths],
         scratch,
-        SUM_COPIES + SCATTER_COPIES * count,
-        SUM_LOCALS + 1 + count,
-    )(parts, cotangent, hidden, gain, *grads)
+        SUM_COPIES + SCATTER_COPIES * count + SWAP_COPIES,
+        SUM_LOCALS + SWAP_LOCALS + 2 + count,
+    )(parts, cotangent, hidden, gains, attended, front, *grads)
 
 
 def collect_heads(dkv, dq, parts, hidden):
@@ -682,11 +797,11 @@
             rings[1, k] = RingSum(
                 net, along_z, lambda d, half, k=k: mine.at[1, up(y, k), up(z, d), half], got.at[1, k], add
             )
+        sums.start()
         for copy in loads:
             copy.wait()
         for ring in rings.values():
             ring.start()
-        sums.start()
         lates = [
             local.copy(dq.at[0, z], dproject.at[0, z, 2]),
             local.copy(dq.at[1, y], dproject.at[1, y, 2]),
@@ -695,9 +810,15 @@
         for d in STEPS:
             two.append(net.send(dq.at[0, up(z, d)], dproject.at[0, z, 2], along_z(d)))
             two.append(net.send(dq.at[1, up(y, d)], dproject.at[1, y, 2], along_y(d)))
+        sums.middle()
         for ring in rings.values():
             ring.middle()
-        sums.middle()
+
+        def step(rows, total):
+            low[rows, :] = (hidden[rows, :] + total).astype(BF)
+
+        sums.totals(step)
+        sums.gather(low, outputs)
         for k in order:
             for m, spot in ((0, z), (1, y)):
                 ring = rings[m, k]
@@ -721,11 +842,6 @@
                 lates.append(local.copy(summed.at[0, 0], dproject.at[0, z, kv]))
                 lates.append(local.copy(summed.at[1, 0], dproject.at[1, y, kv]))
 
-        def step(rows, total):
-            low[rows, :] = (hidden[rows, :] + total).astype(BF)
-
-        sums.totals(step)
-        sums.gather(low, outputs)
         sums.gather_middle()
         for copy in two:
             copy.wait_recv()
@@ -752,11 +868,11 @@
     )(dkv, dq, parts, hidden)
 
 
-def last_backward(parts, inputs, dhidden, gain, vectors, grads):
+def last_backward(parts, inputs, dhidden, gains, vectors, grads):
     widths = [g.shape[-1] for g in grads]
     count = len(grads)
 
-    def kernel(parts, inputs, dhidden, gain, vectors, *rest):
+    def kernel(parts, inputs, dhidden, gains, vectors, *rest):
         grad_refs = rest[:count]
         input_grad, sums_out = rest[count : count + 2]
         outs = rest[count + 2 : 2 * count + 2]
@@ -774,20 +890,18 @@
             Scatter(net, local, grad_refs[k], outs[k], scratch[8 * k : 8 * k + 8], me)
             for k in range(count)
         ]
+        sums.start()
         for scatter in scatters:
             scatter.start()
-        sums.start()
+        sums.middle()
         for scatter in scatters:
             scatter.first()
-        sums.middle()
-        for scatter in scatters:
-            scatter.first_middle()
         residual.wait()
         small[0, ...] = vectors[...]
 
         def step(rows, dfirst):
             norm, inverse = normed(base[rows, :].astype(F32))
-            value = dhidden[rows, :] + norm_pullback(dfirst, norm, inverse, gain[...])
+            value = dhidden[rows, :] + norm_pullback(dfirst, norm, inverse, gains[0:1, :])
             low[rows, :] = value.astype(BF)
             small[0, 0:1, :] += jnp.sum(dfirst * norm, axis=0, keepdims=True)
             small[0, 1:2, :] += jnp.sum(dfirst, axis=0, keepdims=True)
@@ -798,8 +912,7 @@
         ]
         sums.gather(low, input_grad)
         for scatter in scatters:
-            scatter.second()
-        sums.gather_middle()
+            scatter.first_middle()
         for copy in copies:
             copy.wait_recv()
         small[1, ...] = small[0, ...]
@@ -808,18 +921,21 @@
         copies = [
             net.send(small.at[1], got.at[1, d - 1], at(c, y + d, z, x)) for d in STEPS
         ]
+        sums.gather_middle()
+        for scatter in scatters:
+            scatter.second()
         for copy in copies:
             copy.wait_recv()
         small[2, ...] = small[1, ...] + got[1, 0] + got[1, 1] + got[1, 2]
         copies = [
             net.send(small.at[2], got.at[2, d - 1], at(c, y, z + d, x)) for d in STEPS
         ]
+        for scatter in scatters:
+            scatter.second_middle()
         for copy in copies:
             copy.wait_recv()
         small[3, ...] = small[2, ...] + got[2, 0] + got[2, 1] + got[2, 2]
         copy = net.send(small.at[3], got.at[3, 0], at(1 - c, y, z, x))
-        for scatter in scatters:
-            scatter.second_middle()
         for scatter in scatters:
             scatter.third()
         copy.wait_recv()
@@ -845,55 +961,13 @@
         scratch,
         SUM_COPIES + 10 + SCATTER_COPIES * count,
         SUM_LOCALS + 1 + count,
-    )(parts, inputs, dhidden, gain, vectors, *grads)
+    )(parts, inputs, dhidden, gains, vectors, *grads)
 
 
 def turn(values, cosine, sine):
     lane = lax.rem(lax.broadcasted_iota(jnp.int32, values.shape, 1), HEAD_DIM)
     swapped = jnp.where(lane < ROT // 2, -pltpu.roll(values, 120, 1), pltpu.roll(values, 8, 1))
     return values * cosine + swapped * sine
-
-
-def project_heads(tokens, gain, shift, front, bias, tables):
-    def kernel(x_ref, gain_ref, shift_ref, w_hbm, b_ref, t_ref, out_ref, low_ref, weights, sems):
-        loads = []
-        for t in range(3):
-            columns = pl.ds(t * 512, 512)
-            loads.append(pltpu.make_async_copy(w_hbm.at[:, columns], weights.at[t], sems.at[t]))
-            loads[t].start()
-
-        def step(i, carry):
-            rows = pl.ds(pl.multiple_of(i * 32, 32), 32)
-            norm, _ = normed(x_ref[rows, :].astype(F32))
-            low_ref[rows, :] = (norm * gain_ref[...] + shift_ref[...]).astype(BF)
-            return carry
-
-        lax.fori_loop(0, 16, step, 0)
-        for t in (1, 2, 0):
-            loads[t].wait()
-            for m in range(2):
-                acc = jnp.dot(
-                    low_ref[m * 256 : m * 256 + 256, :], weights[t], preferred_element_type=F32
-                )
-                acc = acc + b_ref[:, t * 512 : t * 512 + 512]
-                for h in range(4):
-                    part = acc[:, h * 128 : h * 128 + 128]
-                    if t < 2:
-                        part = turn(part, t_ref[0], t_ref[1])
-                    out_ref[m, h, (t + 2) % 3] = part.astype(BF)
-
-    return pl.pallas_call(
-        kernel,
-        name="project_heads",
-        in_specs=[IN_VMEM, IN_VMEM, IN_VMEM, ANY, IN_VMEM, IN_VMEM],
-        out_specs=[IN_VMEM, IN_VMEM],
-        out_shape=[
-            jax.ShapeDtypeStruct((2, 4, 3, 256, 128), BF),
-            jax.ShapeDtypeStruct((512, D), BF),
-        ],
-        scratch_shapes=[pltpu.VMEM((3, D, 512), BF), pltpu.SemaphoreType.DMA((3,))],
-        compiler_params=pltpu.CompilerParams(vmem_limit_bytes=VMEM_LIMIT),
-    )(tokens, gain, shift, front, bias, tables)
 
 
 def two_heads(block):
@@ -1401,61 +1475,45 @@
 
     vectors = jnp.concatenate(
         [
-            jnp.stack([attend_gain, attend_shift, mixer_gain, mixer_shift], axis=1),
-            jnp.pad(project_bias.reshape(1, 48), ((0, 63), (0, 0))),
-            jnp.zeros((64, 76), BF),
-        ],
-        axis=1,
-    )
+            attend_gain,
+            attend_shift,
+            mixer_gain,
+            mixer_shift,
+            project_bias.transpose(2, 0, 1).reshape(48),
+            jnp.zeros((80,), BF),
+        ]
+    ).reshape(3, 128)
     front_shard = jnp.concatenate(
-        [project_weight.reshape(64, 1536), output_weight.T, vectors], axis=1
+        [project_weight.reshape(64, 1536), output_weight.T, jnp.pad(vectors, ((0, 61), (0, 0)))], axis=1
     )
     back_shard = jnp.concatenate([gate_weight, up_weight, down_weight.T], axis=1)
-    front = gather_front(front_shard).reshape(D, 2176)
-    gains = front[:, 2048:2052].astype(F32).T
-    first_gain, first_shift = gains[0:1], gains[1:2]
-    second_gain, second_shift = gains[2:3], gains[3:4]
-    bias = (
-        front.reshape(32, 64, 2176)[:, 0, 2052:2100]
-        .reshape(32, 3, 8, 2)
-        .transpose(1, 2, 0, 3)
-        .astype(F32)
-        .reshape(1, 1536)
-    )
-    output_t = front[:, 1536:2048]
 
     tokens = inputs.reshape(512, D)
     quarters = inputs.reshape(4, 128, D)
-    qkv, first_low = project_heads(tokens, first_gain, first_shift, front, bias, own_tables)
-    spread = spread_heads(qkv).reshape(2, 16, 3, 256, 128)
+    front, gains, first_low, spread = front_forward(front_shard, tokens, own_tables)
+    spread = spread.reshape(2, 16, 3, 256, 128)
     attended_heads, attended_full, logs = attend(slots, places, rows_of, spread)
-    attended_low = (
-        swap_rows(attended_heads, 2, "attended_back").transpose(0, 2, 1, 3).reshape(512, 512)
-    )
-    branch = nt(attended_low, output_t).astype(BF).reshape(4, 128, D)
-    hidden, second_low, back = middle_forward(branch, quarters, second_gain, second_shift, back_shard)
+    attended_low, hidden, second_low, back = middle_forward(
+        attended_heads, front, quarters, gains, back_shard
+    )
 
     mixer_part, second_part, gate_grad, up_grad, down_grad = feed_forward(
-        second_low.reshape(512, D), cotangent.reshape(512, D), back.reshape(D, 3 * UNITS)
+        second_low.reshape(512, D), cotangent.reshape(512, D), back
     )
 
     def shards(grad):
         return grad.reshape(2, 4, 4, 64, grad.shape[1])
 
-    dhidden, hidden_low, mixer_vectors, gate_grad, up_grad, down_grad = middle_backward(
+    dhidden, mixer_vectors, output_grad, upstream, gate_grad, up_grad, down_grad = middle_backward(
         second_part.reshape(4, 128, D),
         cotangent.reshape(4, 128, D),
         hidden,
-        second_gain,
+        gains,
+        attended_low,
+        front,
         [shards(gate_grad), shards(up_grad), shards(down_grad)],
     )
 
-    hidden_low = hidden_low.reshape(512, D)
-    dattended = jnp.dot(hidden_low, output_t, preferred_element_type=F32).astype(BF)
-    upstream = swap_rows(
-        dattended.reshape(2, 256, 4, 128).transpose(0, 2, 1, 3), 5, "dattended_out"
-    )
-    output_grad = shards(tn(hidden_low, attended_low).astype(BF))
     dq, dkv = attend_back(
         slots, places, rows_of, spread, attended_full, logs, upstream, all_tables
     )
@@ -1473,9 +1531,9 @@
         first_part.reshape(4, 128, D),
         quarters,
         dhidden,
-        first_gain,
+        gains,
         small,
-        [shards(project_grad), output_grad],
+        [shards(project_grad), shards(output_grad)],
     )
     own = lax.dynamic_slice(small, (0, shard_index * 64), (4, 64))
     bias_grad = lax.dynamic_slice(

time: 497 us -> 444 us (0.89); the launches traced: 494 us -> 436 us
  Pallas kernels: 449 us -> 408 us
  matrix products: 10.4 us -> 0 us
  local copies, waits for them, and re-layouts: 23.5 us -> 15.9 us
    pallas_call x7 -> x3, Pallas kernels: 228 us -> 194 us  [the longest x1 69.1 us: front_forward(): remote_call(kernel, 'front_forward', 0, [ANY, IN_VMEM, IN_VMEM], [((D, wi...]
    dot_general x3 -> x0, matrix products: 10.4 us -> none  [the longest x1 4.26 us: nt(): lax.dot_general(left, right, (((1,), (1,)), ((), ())), preferred_element_...]
    pallas_call x1, Pallas kernels: 59.7 us -> 51 us  [last_backward(): remote_call(kernel, 'last_backward', 7, [ANY, ANY, IN_VMEM, IN_VMEM, IN_V...]
where the time goes in v3:
time: 444 us; the launch traced here: 436 us
  Pallas kernels  408 us (92%)
  local copies, waits for them, and re-layouts  15.9 us (4%)
  other arithmetic  11.8 us (3%)
    pallas_call x1, Pallas kernels, front_forward(): remote_call(kernel, 'front_forward', 0, [ANY, IN_VMEM, IN_VMEM], [((D, wi...  69.1 us
    pallas_call x1, Pallas kernels, middle_forward(): remote_call(kernel, 'middle_forward', 3, [ANY, ANY, ANY, IN_VMEM, ANY], [...  62.4 us
    pallas_call x1, Pallas kernels, middle_backward(): remote_call(kernel, 'middle_backward', 4, [ANY, ANY, IN_VMEM, IN_VMEM, IN...  62.1 us
    pallas_call x1, Pallas kernels, last_backward(): remote_call(kernel, 'last_backward', 7, [ANY, ANY, IN_VMEM, IN_VMEM, IN_V...  51 us
    pallas_call x1, Pallas kernels, collect_heads(): remote_call(kernel, 'collect_heads', 6, [ANY, ANY, ANY, IN_VMEM], [((2, 4...  44.9 us
    pallas_call x1, Pallas kernels, attend_back(): pl.pallas_call(kernel, name='attend_back', grid_spec=grid_spec, out_shape...  42.9 us
    pallas_call x1, Pallas kernels, feed_forward(): pl.pallas_call(kernel, name='feed_forward', in_specs=[ANY, ANY, ANY], out...  40.3 us
    pallas_call x1, Pallas kernels, attend(): pl.pallas_call(kernel, name='attend', grid_spec=grid_spec, out_shape=[jax...  23.8 us

profile of v3, /device:TPU:1, one launch (start us, length us, event | category | flops | bytes accessed | tf_op | source)
XLA Modules:
  0.0 436.4 jit_solution(10839315354892357305)
XLA Ops:
  0.6 1.3 select_reduce_fusion.slots
  2.7 1.4 select_reduce_fusion.1.places
  4.8 2.8 concatenate.20
  7.6 0.9 copy.48
  8.5 1.6 fusion.1.src
  10.1 0.8 select_reduce_fusion.2
  10.9 0.8 fusion.4
  13.0 69.1 %front_forward.1 = (bf16[2048,2176]{1,0:T(8,128)(2,1)}, f32[4,2048]{1,0:T(4,128)}, bf16[512,2048]{1,0:T(8,128)(2,1)}, bf16[2,4,4,3,256,128]{5,4,3,2,1,0:T(8,128)(2,1)}) custom-call(bf16[64,2176]{1,0:T(8,128)(2,1)} %fusion.1.src, bf16[512,2048]{1,0:T(8,128)(2,1)} %bitcast.49, f32[2,256,128]{2,1,0:T(8,128)} %pad_maximum_fusion.1.t_ref), custom_call_target="tpu_custom_call" | custom-call | tf_op jit(solution)/shard_map/front_forward/pallas_call | solution.py:570
  82.1 23.8 %attend.1 = (bf16[2,4,256,128]{3,2,1,0:T(8,128)(2,1)}, f32[2,4,256,128]{3,2,1,0:T(8,128)}, f32[2,8,256]{2,1,0:T(8,128)}) custom-call(s32[32]{0:T(128)} %select_reduce_fusion.slots, s32[16]{0:T(128)} %select_reduce_fusion.1.places, s32[8]{0:T(128)} %get-tuple-element.117.rows_of, bf16[2,16,3,256,128]{4,3,2,1,0:T(8,128)(2,1)} %bitcast.43, ...), custom_call_target="tpu_custom_call" | custom-call | tf_op jit(solution)/shard_map/attend/pallas_call | solution.py:1131
  106.0 0.8 pad_maximum_fusion.shard
  106.8 62.4 %middle_forward.1 = (bf16[512,512]{1,0:T(8,128)(2,1)}, f32[128,2048]{1,0:T(8,128)}, bf16[4,128,2048]{2,1,0:T(8,128)(2,1)}, bf16[2048,4224]{1,0:T(8,128)(2,1)}) custom-call(bf16[2,4,256,128]{3,2,1,0:T(8,128)(2,1)} %get-tuple-element.49.heads, bf16[2048,2176]{1,0:T(8,128)(2,1)} %get-tuple-element.50.front.w_hbm, bf16[4,128,2048]{2,1,0:T(8,128)(2,1)} %bitcast.50, ...), custom_call_target="tpu_custom_call" | custom-call | tf_op jit(solution)/shard_map/middle_forward/pallas_call | solution.py:657
  169.2 40.3 %feed_forward.1 = (bf16[512,2048]{1,0:T(8,128)(2,1)}, bf16[512,2048]{1,0:T(8,128)(2,1)}, bf16[2048,1408]{1,0:T(8,128)(2,1)}, bf16[2048,1408]{1,0:T(8,128)(2,1)}, bf16[2048,1408]{1,0:T(8,128)(2,1)}) custom-call(bf16[512,2048]{1,0:T(8,128)(2,1)} %bitcast.65, bf16[512,2048]{1,0:T(8,128)(2,1)} %bitcast.52, bf16[2048,4224]{1,0:T(8,128)(2,1)} %get-tuple-element.53.w_hbm), custom_call_target="tpu_custom_call" | custom-call | tf_op jit(solution)/shard_map/feed_forward/pallas_call | solution.py:1363
  209.5 62.1 %middle_backward.1 = (f32[128,2048]{1,0:T(8,128)}, f32[2,2048]{1,0:T(2,128)}, bf16[2048,512]{1,0:T(8,128)(2,1)}, bf16[2,4,256,128]{3,2,1,0:T(8,128)(2,1)}, f32[6...) custom-call(bf16[4,128,2048]{2,1,0:T(8,128)(2,1)} %bitcast.59, bf16[4,128,2048]{2,1,0:T(8,128)(2,1)} %bitcast.53, ...), custom_call_target="tpu_custom_call" | custom-call | tf_op jit(solution)/shard_map/middle_backward/pallas_call | solution.py:752
  273.4 42.9 %attend_back.1 = (bf16[2,4,256,128]{3,2,1,0:T(8,128)(2,1)}, bf16[2,16,2,256,128]{4,3,2,1,0:T(8,128)(2,1)}) custom-call(s32[32]{0:T(128)} %select_reduce_fusion.slots, s32[16]{0:T(128)} %select_reduce_fusion.1.places, s32[8]{0:T(128)} %get-tuple-element.117.rows_of, bf16[2,16,3,256,128]{4,3,2,1,0:T(8,128)(2,1)} %bitcast.46, ...), custom_call_target="tpu_custom_call" | custom-call | tf_op jit(solution)/shard_map/attend_back/pallas_call | solution.py:1290
  316.3 44.9 %collect_heads.1 = (bf16[2,4,3,256,128]{4,3,2,1,0:T(8,128)(2,1)}, bf16[4,128,2048]{2,1,0:T(8,128)(2,1)}) custom-call(bf16[2,4,4,2,256,128]{5,4,3,2,1,0:T(8,128)(2,1)} %bitcast.58, bf16[2,4,256,128]{3,2,1,0:T(8,128)(2,1)} %get-tuple-element.62.dq, bf16[4,128,2048]{2,1,0:T(8,128)(2,1)} %bitcast.63, f32[128,2048]{1,0:T(8,128)} %get-tuple-element.55.hidden), custom_call_target="tpu_custom_call" | custom-call | tf_op jit(solution)/shard_map/collect_heads/pallas_call | solution.py:853
  361.2 11.2 %project_back.1 = (bf16[512,2048]{1,0:T(8,128)(2,1)}, bf16[2048,1536]{1,0:T(8,128)(2,1)}, f32[1,1536]{1,0:T(1,128)}) custom-call(bf16[2,4,3,256,128]{4,3,2,1,0:T(8,128)(2,1)} %get-tuple-element.65.dp_ref, bf16[512,2048]{1,0:T(8,128)(2,1)} %get-tuple-element.66.low_ref, bf16[2048,2176]{1,0:T(8,128)(2,1)} %get-tuple-element.50.front.w_hbm), custom_call_target="tpu_custom_call" | custom-call | tf_op jit(solution)/shard_map/project_back/pallas_call | solution.py:1406
  372.5 1.4 fusion.2.vectors
  373.9 51.0 %last_backward.1 = (bf16[4,128,2048]{2,1,0:T(8,128)(2,1)}, f32[8,2048]{1,0:T(8,128)}, f32[64,1536]{1,0:T(8,128)}, f32[64,512]{1,0:T(8,128)}) custom-call(bf16[4,128,2048]{2,1,0:T(8,128)(2,1)} %bitcast.64, bf16[4,128,2048]{2,1,0:T(8,128)(2,1)} %bitcast.51, f32[128,2048]{1,0:T(8,128)} %get-tuple-element.68.dhidden, f32[4,2048]{1,0:T(4,128)} %get-tuple-element.51.gains, ...), custom_call_target="tpu_custom_call" | custom-call | tf_op jit(solution)/shard_map/last_backward/pallas_call | solution.py:954
  424.9 0.8 constant_dynamic-slice_fusion
  426.2 1.8 copy.50
  428.0 0.8 slice_reduce_fusion
  429.6 1.3 copy.57
  430.9 1.0 copy-done.1
  432.0 1.3 copy.58
  (51 shorter events, 8.9 us)
Async XLA Ops:
  82.1 23.8 %copy-start.5 = (bf16[1408,64]{0,1:T(8,128)(2,1)S(1)}, bf16[1408,64]{0,1:T(8,128)(2,1)}, u32[]{:S(2)}) copy-start(bf16[1408,64]{0,1:T(8,128)(2,1)} %param.28) | copy-start | bytes 540676
  82.1 23.8 %copy-start.6 = (bf16[64,1408]{1,0:T(8,128)(2,1)S(1)}, bf16[64,1408]{1,0:T(8,128)(2,1)}, u32[]{:S(2)}) copy-start(bf16[64,1408]{1,0:T(8,128)(2,1)} %param.27) | copy-start | bytes 540676
  82.1 23.8 %copy-start.7 = (bf16[64,1408]{1,0:T(8,128)(2,1)S(1)}, bf16[64,1408]{1,0:T(8,128)(2,1)}, u32[]{:S(2)}) copy-start(bf16[64,1408]{1,0:T(8,128)(2,1)} %param.26) | copy-start | bytes 540676
  361.2 11.3 %copy-start.9 = (f32[2,2048]{1,0:T(2,128)S(1)}, f32[2,2048]{1,0:T(2,128)}, u32[]{:S(2)}) copy-start(f32[2,2048]{1,0:T(2,128)} %get-tuple-element.69) | copy-start | bytes 49156
  373.9 55.7 %copy-start = (bf16[4,128,2048]{2,1,0:T(8,128)(2,1)S(1)}, bf16[4,128,2048]{2,1,0:T(8,128)(2,1)}, u32[]{:S(2)}) copy-start(bf16[4,128,2048]{2,1,0:T(8,128)(2,1)} %get-tuple-element.64) | copy-start | bytes 6291460
  429.6 2.3 copy-start.1
  432.0 1.3 copy-start.8
  432.0 2.0 copy-start.4
  432.0 2.7 copy-start.3
  432.0 3.5 copy-start.2

commit v4 on v3

--- a/solution.py
+++ b/solution.py
@@ -43,7 +43,7 @@
 class Net:
     def __init__(self, send_sems, recv_sems):
         self.send_sems, self.recv_sems = send_sems, recv_sems
-        self.sent = []
+        self.sent, self.gone = [], set()
 
     def send(self, src, dst, device):
         n = len(self.sent)
@@ -60,8 +60,13 @@
         return copy
 
     def finish(self):
-        for copy in self.sent:
-            copy.wait_send()
+        for n, copy in enumerate(self.sent):
+            if n not in self.gone:
+                copy.wait_send()
+
+    def wait_sent(self, copy):
+        copy.wait_send()
+        self.gone.add([other is copy for other in self.sent].index(True))
 
 
 class Local:
@@ -103,10 +108,18 @@
         self.net, self.device, self.mine, self.spare, self.add = net, device, mine, spare, add
 
     def start(self):
+        self.start_far()
+        self.start_near()
+
+    def start_far(self):
         send, mine, spare = self.net.send, self.mine, self.spare
         ahead, back = self.device(1), self.device(3)
         self.far_ahead = send(mine(2, 0), spare.at[0], ahead)
         self.far_back = send(mine(2, 1), spare.at[1], back)
+
+    def start_near(self):
+        send, mine, spare = self.net.send, self.mine, self.spare
+        ahead, back = self.device(1), self.device(3)
         self.near = [send(mine(1, 1), spare.at[3], ahead), send(mine(3, 0), spare.at[2], back)]
 
     def middle(self):
@@ -121,6 +134,10 @@
     def arrive(self):
         for copy in self.near:
             copy.wait_recv()
+
+    def sent(self):
+        for copy in [self.far_ahead, self.far_back] + self.near:
+            self.net.wait_sent(copy)
 
     def terms(self, half):
         return [self.spare.at[4 if half == 0 else 3], self.spare.at[2 if half == 0 else 5]]
@@ -295,8 +312,14 @@
         self.own = self.local.copy(self.grads.at[c], self.held)
         self.zero = self.net.send(self.grads.at[1 - c], self.other, at(1 - c, y, z, x))
 
+    def send_filled(self, block):
+        c, y, z, x = self.me
+        self.own = None
+        self.zero = self.net.send(block, self.other, at(1 - c, y, z, x))
+
     def first(self):
-        self.own.wait()
+        if self.own is not None:
+            self.own.wait()
         self.zero.wait_recv()
         held, other = self.held, self.other
 
@@ -347,10 +370,19 @@
                 self.out[pl.ds(first + 16 * half, 16), :] = value
 
 
+def quarters_of(net, out, me):
+    c, y, z, x = me
+
+    def piece(d, half=None):
+        return out.at[up(x, d)] if half is None else out.at[up(x, d), pl.ds(64 * half, 64)]
+
+    return RingGather(net, lambda d: at(c, y, z, x + d), piece)
+
+
 class SumX:
     def __init__(self, net, local, parts, held, spare, me):
         c, y, z, x = me
-        self.local, self.parts, self.held, self.x, self.net = local, parts, held, x, net
+        self.local, self.parts, self.held, self.x, self.net, self.me = local, parts, held, x, net, me
         self.along = lambda d: at(c, y, z, x + d)
         self.ring = RingSum(
             net, self.along, lambda d, half: held.at[up(x, d), pl.ds(64 * half, 64)], spare, self.add
@@ -396,12 +428,7 @@
 
     def gather(self, block, out):
         x = self.x
-
-        def piece(d, half=None):
-            whole = out.at[up(x, d)]
-            return whole if half is None else out.at[up(x, d), pl.ds(64 * half, 64)]
-
-        self.back = RingGather(self.net, self.along, piece)
+        self.back = quarters_of(self.net, out, self.me)
         self.mine = self.local.copy(block, out.at[x])
         self.back.start(block)
 
@@ -438,6 +465,7 @@
 
 ANY = pl.BlockSpec(memory_space=pl.ANY)
 IN_VMEM = pl.BlockSpec(memory_space=pltpu.VMEM)
+IN_SMEM = pl.BlockSpec(memory_space=pltpu.SMEM)
 
 
 def remote_call(body, name, cid, ins, outs, scratch, copies, locals_):
@@ -462,29 +490,38 @@
 def assemble_vectors(weights, gains, bias, spots):
     for s in range(32):
         block = weights[s * 64 : s * 64 + 16, 2048:2176].astype(F32)
-        for k in range(4):
-            side = (k % 2) * 64
-            gains[k : k + 1, s * 64 : s * 64 + 64] = block[k // 2 : k // 2 + 1, side : side + 64]
-        spots[s : s + 1, :] = block[2:3, :]
+        gains[0:4, s * 64 : s * 64 + 64] = block[0:4, :64]
+        spots[s : s + 1, :] = block[4:5, :]
     values = spots[...].astype(BF)
+    head = lax.broadcasted_iota(jnp.int32, (32, 128), 0)
+    held = lax.broadcasted_iota(jnp.int32, (32, 128), 1)
     shard = lax.broadcasted_iota(jnp.int32, (32, 64), 0)
     lane = lax.broadcasted_iota(jnp.int32, (32, 64), 1)
-    total = jnp.zeros((24, 64), F32)
+    total = jnp.zeros((32, 64), F32)
     for e in range(2):
-        pick = jnp.where(lane == 2 * shard + e, 1.0, 0.0).astype(BF)
-        total += tn(values, pick)[e * 24 : e * 24 + 24]
+        pick = jnp.where((held == 2 * head + e) & (head < 24), 1.0, 0.0).astype(BF)
+        spread = jnp.where(lane == 2 * shard + e, 1.0, 0.0).astype(BF)
+        total += jnp.dot(nt(pick, values).astype(BF), spread, preferred_element_type=F32)
     for n in range(24):
         bias[0:1, n * 64 : n * 64 + 64] = total[n : n + 1]
 
 
-def front_forward(shard, tokens, tables):
-    def kernel(src, x_ref, t_ref, front, gains, low, out, weights, norm, blocks, bias, spots, ss, rs, ls):
+def front_forward(shard, tokens, group_place, base, steps):
+    def kernel(
+        src, x_ref, group_ref, base_ref, steps_ref, front, gains, low, out,
+        weights, norm, blocks, bias, spots, turns, ss, rs, ls,
+    ):
         me = here()
         c, y, z, x = me
         net, local = Net(ss, rs), Local(ls)
         greet(y_peers(*me) + z_peers(*me) + core_peer(*me))
         gather = Gather(net, local, src, flat_rows(weights), me)
         gather.start()
+        for n in range(2):
+            rows = slice(n * 128, n * 128 + 128)
+            cosine, sine = turn_tables(base_ref, steps_ref, group_ref[(y * 4 + z) * 2 + n])
+            turns[0, rows, :] = cosine
+            turns[1, rows, :] = sine
 
         def centre(i, carry):
             rows = pl.ds(pl.multiple_of(i * 32, 32), 32)
@@ -516,7 +553,7 @@
                 for h in range(4):
                     part = acc[:, h * 128 : h * 128 + 128]
                     if t < 2:
-                        part = turn(part, t_ref[0], t_ref[1])
+                        part = turn(part, turns[0], turns[1])
                     blocks[m, h, (t + 2) % 3] = part.astype(BF)
 
         along_y = lambda d: at(c, y + d, z, x)
@@ -571,7 +608,7 @@
         kernel,
         "front_forward",
         0,
-        [ANY, IN_VMEM, IN_VMEM],
+        [ANY, IN_VMEM, IN_SMEM, IN_VMEM, IN_VMEM],
         [
             ((D, width), BF, ANY),
             ((4, D), F32, IN_VMEM),
@@ -584,10 +621,11 @@
             pltpu.VMEM((2, 4, 3, 256, 128), BF),
             pltpu.VMEM((1, 1536), F32),
             pltpu.VMEM((32, 128), F32),
+            pltpu.VMEM((2, 256, 128), F32),
         ],
         GATHER_COPIES + 12 + 8 * RING_GATHER,
         4,
-    )(shard, tokens, tables)
+    )(shard, tokens, group_place, base, steps)
 
 
 class Swap:
@@ -673,56 +711,81 @@
     )(heads, front, inputs, gains, shard)
 
 
-def middle_backward(parts, cotangent, hidden, gains, attended, front, grads):
-    widths = [g.shape[-1] for g in grads]
-    count = len(grads)
-
-    def kernel(parts, cotangent, hidden, gains, attended, front, *rest):
-        grad_refs = rest[:count]
-        dhidden, vectors, output_grad, upstream = rest[count : count + 4]
-        outs = rest[count + 4 : 2 * count + 4]
-        held, spare, base, low, hidden_low, out_w, blocks = rest[2 * count + 4 : 2 * count + 11]
-        scratch = rest[2 * count + 11 : -3]
-        ss, rs, ls = rest[-3:]
+def other_half(c, k, size):
+    core = 1 - c if k < 2 else c
+    return pl.ds(pl.multiple_of(core * 1024 + (k % 2) * size, size), size)
+
+
+def shard_block(k):
+    return pl.ds((k % 2) * 2, 2)
+
+
+def middle_backward(parts, cotangent, hidden, gains, attended, front, second_low, dup, mixed, branch, gate_grad):
+    def kernel(
+        parts, cotangent, hidden, gains, attended, front, second_low, dup, mixed, branch, gate_grad,
+        dhidden, vectors, output_grad, upstream, out_block, gate_out, up_out, down_out,
+        held, spare, low, hidden_low, out_w, blocks, lows, dys, extra, *rest,
+    ):
+        scratch, (ss, rs, ls) = rest[:-3], rest[-3:]
         me = here()
         c, y, z, x = me
         net, local = Net(ss, rs), Local(ls)
         sums = SumX(net, local, parts, held, spare, me)
         sums.load()
-        upper = local.copy(cotangent.at[x], base)
+        loads = [local.copy(second_low, lows), local.copy(cotangent, dys)]
         load = local.copy(front.at[:, TURNED], out_w)
         greet(y_peers(*me) + z_peers(*me) + core_peer(*me) + x_peers(*me))
-        scatters = [
-            Scatter(net, local, grad_refs[k], outs[k], scratch[8 * k : 8 * k + 8], me)
-            for k in range(count)
+        gate, up_, down_ = [
+            Scatter(net, local, grads, out, scratch[8 * k : 8 * k + 8], me)
+            for k, (grads, out) in enumerate(((gate_grad, gate_out), (None, up_out), (None, down_out)))
         ]
+        gate.start()
         sums.start()
-        for scatter in scatters:
-            scatter.start()
-        scatters[0].first()
+
+        def multiply(left, right, k, to):
+            value = tn(left[:, other_half(c, k, 512)], right[...]).astype(BF)
+            to[shard_block(k)] = value.reshape(2, 4, 64, UNITS)
+
+        loads[0].wait()
+        for k in range(2):
+            multiply(lows, dup, k, down_.held)
+        up_.send_filled(down_.held)
+        gate.first()
         sums.middle()
-        for scatter in scatters[1:]:
-            scatter.first()
-        scatters[0].first_middle()
-        upper.wait()
+        for k in range(2, 4):
+            multiply(lows, dup, k, up_.held)
+        loads[1].wait()
+        for k in range(2):
+            multiply(dys, mixed, k, extra)
+        down_.send_filled(extra)
+        up_.first()
+        net.wait_sent(up_.zero)
+        gate.first_middle()
         vectors[...] = jnp.zeros_like(vectors)
 
         def step(rows, dsecond):
             norm, inverse = normed(hidden[rows, :])
-            value = base[rows, :].astype(F32) + norm_pullback(dsecond, norm, inverse, gains[2:3, :])
+            upper = dys[pl.ds(pl.multiple_of(x * 128 + rows.start, 32), 32), :].astype(F32)
+            value = upper + norm_pullback(dsecond, norm, inverse, gains[2:3, :])
             dhidden[rows, :] = value
             low[rows, :] = value.astype(BF)
             vectors[0:1, :] += jnp.sum(dsecond * norm, axis=0, keepdims=True)
             vectors[1:2, :] += jnp.sum(dsecond, axis=0, keepdims=True)
 
         sums.totals(step)
+        sums.ring.sent()
         sums.gather(low, hidden_low)
-        for scatter in scatters[1:]:
-            scatter.first_middle()
-        scatters[0].second()
+        for k in range(2, 4):
+            multiply(dys, mixed, k, down_.held)
+        down_.first()
+        up_.first_middle()
+        gate.second()
         sums.gather_middle()
-        for scatter in scatters[1:]:
-            scatter.second()
+        late = SumX(net, local, branch, held, spare, me)
+        late.load()
+        late.start()
+        down_.first_middle()
+        up_.second()
         load.wait()
         sums.finish()
         for q in range(4):
@@ -731,51 +794,59 @@
             for h in range(4):
                 blocks[q // 2, h, rows, :] = result[:, h * 128 : h * 128 + 128]
         swap = Swap(net, local, blocks, upstream, me)
-        for scatter in scatters:
-            scatter.second_middle()
+        late.middle()
+        gate.second_middle()
+        down_.second()
         whole = hidden_low[...].reshape(512, D)
         output_grad[...] = tn(whole, attended[...]).astype(BF)
-        for scatter in scatters:
-            scatter.third()
+        up_.second_middle()
+        gate.third()
+        down_.second_middle()
+
+        def last(rows, total):
+            out_block[rows, :] = (hidden[rows, :] + total).astype(BF)
+
+        late.totals(last)
+        up_.third()
+        down_.third()
         swap.arrive()
         net.finish()
 
     scratch = sum_scratch() + [
-        pltpu.VMEM((128, D), BF),
         pltpu.VMEM((128, D), BF),
         pltpu.VMEM((4, 128, D), BF),
         pltpu.VMEM((D, 512), BF),
         pltpu.VMEM((2, 4, 256, 128), BF),
+        pltpu.VMEM((512, D), BF),
+        pltpu.VMEM((512, D), BF),
+        pltpu.VMEM((4, 4, 64, UNITS), BF),
     ]
-    for width in widths:
-        scratch += scatter_scratch(width)
     return remote_call(
         kernel,
         "middle_backward",
         4,
-        [ANY, ANY, IN_VMEM, IN_VMEM, IN_VMEM, ANY] + [ANY] * count,
+        [ANY, ANY, IN_VMEM, IN_VMEM, IN_VMEM, ANY, ANY, IN_VMEM, IN_VMEM, ANY, ANY],
         [
             ((128, D), F32, IN_VMEM),
             ((2, D), F32, IN_VMEM),
             ((D, 512), BF, IN_VMEM),
             ((2, 4, 256, 128), BF, ANY),
+            ((128, D), BF, IN_VMEM),
         ]
-        + [((64, width), F32, IN_VMEM) for width in widths],
-        scratch,
-        SUM_COPIES + SCATTER_COPIES * count + SWAP_COPIES,
-        SUM_LOCALS + SWAP_LOCALS + 2 + count,
-    )(parts, cotangent, hidden, gains, attended, front, *grads)
-
-
-def collect_heads(dkv, dq, parts, hidden):
-    def kernel(dkv, dq, parts, hidden, dproject, outputs, mine, got, summed, held, spare, low, ss, rs, ls):
+        + [((64, UNITS), F32, IN_VMEM)] * 3,
+        scratch + scatter_scratch(UNITS) * 3,
+        SUM_COPIES + RING_SUM + SCATTER_COPIES * 3 + SWAP_COPIES,
+        SUM_LOCALS + 4 + SWAP_LOCALS + 3 + 1,
+    )(parts, cotangent, hidden, gains, attended, front, second_low, dup, mixed, branch, gate_grad)
+
+
+def collect_heads(dkv, dq, block):
+    def kernel(dkv, dq, block, dproject, outputs, mine, got, summed, ss, rs, ls):
         me = here()
         c, y, z, x = me
         net, local = Net(ss, rs), Local(ls)
         order = (1, 3, 2, 0)
         loads = [local.copy(dkv.at[m], mine.at[m]) for m in range(2)]
-        sums = SumX(net, local, parts, held, spare, me)
-        sums.load()
         greet(y_peers(*me) + z_peers(*me) + x_peers(*me))
         kv = pl.ds(0, 2)
         along_y = lambda d: at(c, y + d, z, x)
@@ -797,7 +868,9 @@
             rings[1, k] = RingSum(
                 net, along_z, lambda d, half, k=k: mine.at[1, up(y, k), up(z, d), half], got.at[1, k], add
             )
-        sums.start()
+        whole = quarters_of(net, outputs, me)
+        own = local.copy(block, outputs.at[x])
+        whole.start(block)
         for copy in loads:
             copy.wait()
         for ring in rings.values():
@@ -810,25 +883,18 @@
         for d in STEPS:
             two.append(net.send(dq.at[0, up(z, d)], dproject.at[0, z, 2], along_z(d)))
             two.append(net.send(dq.at[1, up(y, d)], dproject.at[1, y, 2], along_y(d)))
-        sums.middle()
         for ring in rings.values():
             ring.middle()
-
-        def step(rows, total):
-            low[rows, :] = (hidden[rows, :] + total).astype(BF)
-
-        sums.totals(step)
-        sums.gather(low, outputs)
         for k in order:
             for m, spot in ((0, z), (1, y)):
                 ring = rings[m, k]
                 ring.arrive()
                 for half in range(2):
-                    own, terms = ring.mine(0, half), ring.terms(half)
-
-                    def total(i, carry, m=m, k=k, half=half, own=own, terms=terms):
+                    kept, terms = ring.mine(0, half), ring.terms(half)
+
+                    def total(i, carry, m=m, k=k, half=half, kept=kept, terms=terms):
                         rows = pl.ds(pl.multiple_of(i * 64, 64), 64)
-                        value = own[rows, :].astype(F32)
+                        value = kept[rows, :].astype(F32)
                         for term in terms:
                             value += term[rows, :].astype(F32)
                         summed[m, k, half, rows, :] = value.astype(BF)
@@ -842,62 +908,86 @@
                 lates.append(local.copy(summed.at[0, 0], dproject.at[0, z, kv]))
                 lates.append(local.copy(summed.at[1, 0], dproject.at[1, y, kv]))
 
-        sums.gather_middle()
+        whole.from_back()
+        whole.from_ahead()
         for copy in two:
             copy.wait_recv()
         for copy in lates:
             copy.wait()
-        sums.finish()
+        own.wait()
+        whole.arrive()
         net.finish()
 
     return remote_call(
         kernel,
         "collect_heads",
         6,
-        [ANY, ANY, ANY, IN_VMEM],
+        [ANY, ANY, IN_VMEM],
         [((2, 4, 3, 256, 128), BF, ANY), ((4, 128, D), BF, ANY)],
         [
             pltpu.VMEM((2, 4, 4, 2, 256, 128), BF),
             pltpu.VMEM((2, 4, 6, 256, 128), BF),
             pltpu.VMEM((2, 4, 2, 256, 128), BF),
-        ]
-        + sum_scratch()
-        + [pltpu.VMEM((128, D), BF)],
-        8 * RING_SUM + 6 + 6 + SUM_COPIES,
-        2 + 4 + SUM_LOCALS,
-    )(dkv, dq, parts, hidden)
-
-
-def last_backward(parts, inputs, dhidden, gains, vectors, grads):
-    widths = [g.shape[-1] for g in grads]
-    count = len(grads)
-
-    def kernel(parts, inputs, dhidden, gains, vectors, *rest):
-        grad_refs = rest[:count]
-        input_grad, sums_out = rest[count : count + 2]
-        outs = rest[count + 2 : 2 * count + 2]
-        held, spare, base, low, small, got = rest[2 * count + 2 : 2 * count + 8]
-        scratch = rest[2 * count + 8 : -3]
-        ss, rs, ls = rest[-3:]
+        ],
+        8 * RING_SUM + 6 + 6 + RING_GATHER,
+        2 + 4 + 1,
+    )(dkv, dq, block)
+
+
+def last_backward(dproject, first_low, front, inputs, dhidden, gains, mixer_vectors, output_grad):
+    def kernel(
+        dproject, first_low, front, inputs, dhidden, gains, mixer_vectors, output_grad,
+        input_grad, sums_out, project_out, output_out,
+        wide, weights, lows, held, spare, base, low, extra, small, got, *rest,
+    ):
+        scratch, (ss, rs, ls) = rest[:-3], rest[-3:]
         me = here()
         c, y, z, x = me
         net, local = Net(ss, rs), Local(ls)
-        sums = SumX(net, local, parts, held, spare, me)
-        sums.load()
+        load = local.copy(front.at[:, pl.ds(0, 1536)], weights)
+        load_low = local.copy(first_low, lows)
         residual = local.copy(inputs.at[x], base)
         greet(y_peers(*me) + z_peers(*me) + core_peer(*me) + x_peers(*me))
-        scatters = [
-            Scatter(net, local, grad_refs[k], outs[k], scratch[8 * k : 8 * k + 8], me)
-            for k in range(count)
-        ]
-        sums.start()
-        for scatter in scatters:
-            scatter.start()
+        project = Scatter(net, local, None, project_out, scratch[:8], me)
+        output = Scatter(net, local, output_grad, output_out, scratch[8:], me)
+        output.start()
+        sums = SumX(net, local, None, held, spare, me)
+        for m in range(2):
+            for t in range(3):
+                for h in range(4):
+                    to = t * 512 + h * 128
+                    wide[m * 256 : m * 256 + 256, to : to + 128] = dproject[m, h, (t + 2) % 3]
+        load.wait()
+
+        def quarter(d):
+            q = up(x, d)
+            rows = wide[pl.ds(pl.multiple_of(q * 128, 128), 128), :]
+            held[q] = nt(rows, weights[...]).astype(BF)
+
+        quarter(2)
+        sums.ring.start_far()
+        quarter(1)
+        quarter(3)
+        sums.ring.start_near()
+
+        def multiply(k, to):
+            value = tn(lows[:, other_half(c, k, 512)], wide[...]).astype(BF)
+            to[shard_block(k)] = value.reshape(2, 4, 64, 1536)
+
+        load_low.wait()
+        for k in range(2):
+            multiply(k, extra)
+        project.send_filled(extra)
         sums.middle()
-        for scatter in scatters:
-            scatter.first()
+        quarter(0)
+        for k in range(2, 4):
+            multiply(k, project.held)
+        output.first()
+        small[0, ...] = jnp.zeros_like(small[0])
+        small[0, 2:4, :] = mixer_vectors[...]
+        small[0, 4:5, 0:1536] = jnp.sum(wide[...].astype(F32), axis=0, keepdims=True)
+        project.first()
         residual.wait()
-        small[0, ...] = vectors[...]
 
         def step(rows, dfirst):
             norm, inverse = normed(base[rows, :].astype(F32))
@@ -907,67 +997,74 @@
             small[0, 1:2, :] += jnp.sum(dfirst, axis=0, keepdims=True)
 
         sums.totals(step)
-        copies = [
-            net.send(small.at[0], got.at[0, d - 1], at(c, y, z, x + d)) for d in STEPS
-        ]
+        copies = [net.send(small.at[0], got.at[0, d - 1], at(c, y, z, x + d)) for d in STEPS]
         sums.gather(low, input_grad)
-        for scatter in scatters:
-            scatter.first_middle()
+        output.first_middle()
+        project.first_middle()
         for copy in copies:
             copy.wait_recv()
         small[1, ...] = small[0, ...]
         for n in range(3):
             small[1, 0:4, :] += got[0, n, 0:4, :]
-        copies = [
-            net.send(small.at[1], got.at[1, d - 1], at(c, y + d, z, x)) for d in STEPS
-        ]
+        copies = [net.send(small.at[1], got.at[1, d - 1], at(c, y + d, z, x)) for d in STEPS]
         sums.gather_middle()
-        for scatter in scatters:
-            scatter.second()
+        output.second()
+        project.second()
         for copy in copies:
             copy.wait_recv()
         small[2, ...] = small[1, ...] + got[1, 0] + got[1, 1] + got[1, 2]
-        copies = [
-            net.send(small.at[2], got.at[2, d - 1], at(c, y, z + d, x)) for d in STEPS
-        ]
-        for scatter in scatters:
-            scatter.second_middle()
+        copies = [net.send(small.at[2], got.at[2, d - 1], at(c, y, z + d, x)) for d in STEPS]
+        output.second_middle()
+        project.second_middle()
         for copy in copies:
             copy.wait_recv()
         small[3, ...] = small[2, ...] + got[2, 0] + got[2, 1] + got[2, 2]
         copy = net.send(small.at[3], got.at[3, 0], at(1 - c, y, z, x))
-        for scatter in scatters:
-            scatter.third()
+        output.third()
+        project.third()
         copy.wait_recv()
         sums_out[...] = small[3, ...] + got[3, 0]
         sums.finish()
         net.finish()
 
-    scratch = sum_scratch() + [
-        pltpu.VMEM((128, D), BF),
-        pltpu.VMEM((128, D), BF),
-        pltpu.VMEM((4, 8, D), F32),
-        pltpu.VMEM((4, 3, 8, D), F32),
-    ]
-    for width in widths:
-        scratch += scatter_scratch(width)
+    scratch = (
+        [pltpu.VMEM((512, 1536), BF), pltpu.VMEM((D, 1536), BF), pltpu.VMEM((512, D), BF)]
+        + sum_scratch()
+        + [
+            pltpu.VMEM((128, D), BF),
+            pltpu.VMEM((128, D), BF),
+            pltpu.VMEM((4, 4, 64, 1536), BF),
+            pltpu.VMEM((4, 8, D), F32),
+            pltpu.VMEM((4, 3, 8, D), F32),
+        ]
+    )
     return remote_call(
         kernel,
         "last_backward",
         7,
-        [ANY, ANY, IN_VMEM, IN_VMEM, IN_VMEM] + [ANY] * count,
-        [((4, 128, D), BF, ANY), ((8, D), F32, IN_VMEM)]
-        + [((64, width), F32, IN_VMEM) for width in widths],
-        scratch,
-        SUM_COPIES + 10 + SCATTER_COPIES * count,
-        SUM_LOCALS + 1 + count,
-    )(parts, inputs, dhidden, gains, vectors, *grads)
+        [IN_VMEM, ANY, ANY, ANY, IN_VMEM, IN_VMEM, IN_VMEM, ANY],
+        [
+            ((4, 128, D), BF, ANY),
+            ((8, D), F32, IN_VMEM),
+            ((64, 1536), F32, IN_VMEM),
+            ((64, 512), F32, IN_VMEM),
+        ],
+        scratch + scatter_scratch(1536) + scatter_scratch(512),
+        SUM_COPIES + 10 + SCATTER_COPIES * 2,
+        SUM_LOCALS + 4,
+    )(dproject, first_low, front, inputs, dhidden, gains, mixer_vectors, output_grad)
 
 
 def turn(values, cosine, sine):
     lane = lax.rem(lax.broadcasted_iota(jnp.int32, values.shape, 1), HEAD_DIM)
     swapped = jnp.where(lane < ROT // 2, -pltpu.roll(values, 120, 1), pltpu.roll(values, 8, 1))
     return values * cosine + swapped * sine
+
+
+def turn_tables(base, steps, block):
+    cosine, sine = base[0], base[1]
+    far_cosine, far_sine = steps[0, pl.ds(block, 1), :], steps[1, pl.ds(block, 1), :]
+    return far_cosine * cosine - far_sine * sine, far_sine * cosine + far_cosine * sine
 
 
 def two_heads(block):
@@ -993,6 +1090,24 @@
 
 def nt(left, right):
     return lax.dot_general(left, right, (((1,), (1,)), ((), ())), preferred_element_type=F32)
+
+
+def plan_blocks(group_place, slots, places):
+    _, y, z, _ = here()
+
+    def one(j, carry):
+        slots[group_place[j]] = j
+        return carry
+
+    lax.fori_loop(0, 32, one, 0)
+    for b in range(8):
+        places[b] = group_place[(y * 4 + b // 2) * 2 + b % 2]
+        places[8 + b] = group_place[((b // 2) * 4 + z) * 2 + b % 2]
+
+
+def row_of(m, i):
+    _, y, z, _ = here()
+    return jnp.where(m == 0, y * 4 + i, i * 4 + z)
 
 
 def unit_of(places, m, n):
@@ -1029,13 +1144,14 @@
 UNITS_EACH = 36
 
 
-def attend(slots, places, rows_of, spread):
+def attend(group_place, spread):
     def kernel(
-        slots, places, rows_of, k_ref, v_ref, q_ref, o_ref, full_ref, log_ref,
-        keys, values_t, queries, scores_0, scores_1, weights_0, weights_1, results, sums,
+        group_ref, k_ref, v_ref, q_ref, o_ref, full_ref, log_ref,
+        slots, places, keys, values_t, queries, scores_0, scores_1, weights_0, weights_1, results, sums,
     ):
         scores, weights = (scores_0, scores_1), (weights_0, weights_1)
         m = pl.program_id(0)
+        plan_blocks(group_ref, slots, places)
 
         def lay(slot, rows, to):
             keys[to, :] = k_ref[0, slot, 0, rows, :]
@@ -1043,7 +1159,7 @@
 
         lay_blocks(slots, lay)
         for b in range(8):
-            row = rows_of[m * 4 + b // 2]
+            row = row_of(m, b // 2)
             block = q_ref[0, row, 0, (b % 2) * 128 : (b % 2) * 128 + 128, :]
             queries[b] = (two_heads_t(block) * 0.125).astype(BF)
         offset = key_minus_query()
@@ -1104,19 +1220,21 @@
             log_ref[0, b : b + 1, :] = sums[b, 0:1, :] + jnp.log2(total)
 
     grid_spec = pltpu.PrefetchScalarGridSpec(
-        num_scalar_prefetch=3,
+        num_scalar_prefetch=1,
         grid=(2,),
         in_specs=[
-            pl.BlockSpec((1, 16, 1, 256, 128), lambda m, s, p, r: (m, 0, 0, 0, 0)),
-            pl.BlockSpec((1, 16, 1, 256, 128), lambda m, s, p, r: (m, 0, 1, 0, 0)),
-            pl.BlockSpec((1, 16, 1, 256, 128), lambda m, s, p, r: (m, 0, 2, 0, 0)),
+            pl.BlockSpec((1, 16, 1, 256, 128), lambda m, g: (m, 0, 0, 0, 0)),
+            pl.BlockSpec((1, 16, 1, 256, 128), lambda m, g: (m, 0, 1, 0, 0)),
+            pl.BlockSpec((1, 16, 1, 256, 128), lambda m, g: (m, 0, 2, 0, 0)),
         ],
         out_specs=[
-            pl.BlockSpec((1, 4, 256, 128), lambda m, s, p, r: (m, 0, 0, 0)),
-            pl.BlockSpec((1, 4, 256, 128), lambda m, s, p, r: (m, 0, 0, 0)),
-            pl.BlockSpec((1, 8, 256), lambda m, s, p, r: (m, 0, 0)),
+            pl.BlockSpec((1, 4, 256, 128), lambda m, g: (m, 0, 0, 0)),
+            pl.BlockSpec((1, 4, 256, 128), lambda m, g: (m, 0, 0, 0)),
+            pl.BlockSpec((1, 8, 256), lambda m, g: (m, 0, 0)),
         ],
         scratch_shapes=[
+            pltpu.SMEM((32,), jnp.int32),
+            pltpu.SMEM((16,), jnp.int32),
             pltpu.VMEM((4096, 128), BF),
             pltpu.VMEM((128, 4096), BF),
             pltpu.VMEM((8, 128, 256), BF),
@@ -1138,21 +1256,20 @@
             jax.ShapeDtypeStruct((2, 8, 256), F32),
         ],
         compiler_params=pltpu.CompilerParams(vmem_limit_bytes=VMEM_LIMIT),
-    )(slots, places, rows_of, spread, spread, spread)
-
-
-def attend_back(slots, places, rows_of, spread, full, logs, upstream, tables):
-    base, steps = tables
-
+    )(group_place, spread, spread, spread)
+
+
+def attend_back(group_place, spread, full, logs, upstream, base, steps):
     def kernel(
-        slots, places, rows_of, k_ref, v_ref, q_ref, full_ref, log_ref, up_ref, base_ref, steps_ref,
+        group_ref, k_ref, v_ref, q_ref, full_ref, log_ref, up_ref, base_ref, steps_ref,
         dq_ref, dkv_ref,
-        keys, keys_t, values, dkeys, dvalues, queries, queries_t, grads, grads_t, delta,
+        slots, places, keys, keys_t, values, dkeys, dvalues, queries, queries_t, grads, grads_t, delta,
         scores_0, scores_1, dprobs_0, dprobs_1, probs_0, probs_1, dscores_0, dscores_1, results,
     ):
         scores, dprobs = (scores_0, scores_1), (dprobs_0, dprobs_1)
         probs_low, dscores = (probs_0, probs_1), (dscores_0, dscores_1)
         m = pl.program_id(0)
+        plan_blocks(group_ref, slots, places)
 
         def lay(slot, rows, to):
             block = k_ref[0, slot, 0, rows, :]
@@ -1165,7 +1282,7 @@
         lay_blocks(slots, lay)
         for b in range(8):
             rows = slice((b % 2) * 128, (b % 2) * 128 + 128)
-            block = q_ref[0, rows_of[m * 4 + b // 2], 0, rows, :]
+            block = q_ref[0, row_of(m, b // 2), 0, rows, :]
             queries[b] = (two_heads(block) * 0.125).astype(BF)
             queries_t[b] = (two_heads_t(block) * 0.125).astype(BF)
             ups = up_ref[0, b // 2, rows, :]
@@ -1223,13 +1340,8 @@
         gather(last, 1, acc)
 
         def turned_back(values, place):
-            cosine, sine = base_ref[0], base_ref[1]
-            far_cosine, far_sine = steps_ref[0, pl.ds(place, 1), :], steps_ref[1, pl.ds(place, 1), :]
-            return turn(
-                values,
-                far_cosine * cosine - far_sine * sine,
-                -(far_sine * cosine + far_cosine * sine),
-            )
+            cosine, sine = turn_tables(base_ref, steps_ref, place)
+            return turn(values, cosine, -sine)
 
         for b in range(8):
             rows = slice((b % 2) * 128, (b % 2) * 128 + 128)
@@ -1249,23 +1361,25 @@
         lax.fori_loop(0, 16, flush, 0)
 
     grid_spec = pltpu.PrefetchScalarGridSpec(
-        num_scalar_prefetch=3,
+        num_scalar_prefetch=1,
         grid=(2,),
         in_specs=[
-            pl.BlockSpec((1, 16, 1, 256, 128), lambda m, s, p, r: (m, 0, 0, 0, 0)),
-            pl.BlockSpec((1, 16, 1, 256, 128), lambda m, s, p, r: (m, 0, 1, 0, 0)),
-            pl.BlockSpec((1, 16, 1, 256, 128), lambda m, s, p, r: (m, 0, 2, 0, 0)),
-            pl.BlockSpec((1, 4, 256, 128), lambda m, s, p, r: (m, 0, 0, 0)),
-            pl.BlockSpec((1, 8, 256), lambda m, s, p, r: (m, 0, 0)),
-            pl.BlockSpec((1, 4, 256, 128), lambda m, s, p, r: (m, 0, 0, 0)),
-            pl.BlockSpec((2, 128, 128), lambda m, s, p, r: (0, 0, 0)),
-            pl.BlockSpec((2, 32, 128), lambda m, s, p, r: (0, 0, 0)),
+            pl.BlockSpec((1, 16, 1, 256, 128), lambda m, g: (m, 0, 0, 0, 0)),
+            pl.BlockSpec((1, 16, 1, 256, 128), lambda m, g: (m, 0, 1, 0, 0)),
+            pl.BlockSpec((1, 16, 1, 256, 128), lambda m, g: (m, 0, 2, 0, 0)),
+            pl.BlockSpec((1, 4, 256, 128), lambda m, g: (m, 0, 0, 0)),
+            pl.BlockSpec((1, 8, 256), lambda m, g: (m, 0, 0)),
+            pl.BlockSpec((1, 4, 256, 128), lambda m, g: (m, 0, 0, 0)),
+            pl.BlockSpec((2, 128, 128), lambda m, g: (0, 0, 0)),
+            pl.BlockSpec((2, 32, 128), lambda m, g: (0, 0, 0)),
         ],
         out_specs=[
-            pl.BlockSpec((1, 4, 256, 128), lambda m, s, p, r: (m, 0, 0, 0)),
-            pl.BlockSpec((1, 16, 2, 256, 128), lambda m, s, p, r: (m, 0, 0, 0, 0)),
+            pl.BlockSpec((1, 4, 256, 128), lambda m, g: (m, 0, 0, 0)),
+            pl.BlockSpec((1, 16, 2, 256, 128), lambda m, g: (m, 0, 0, 0, 0)),
         ],
         scratch_shapes=[
+            pltpu.SMEM((32,), jnp.int32),
+            pltpu.SMEM((16,), jnp.int32),
             pltpu.VMEM((4096, 128), BF),
             pltpu.VMEM((128, 4096), BF),
             pltpu.VMEM((4096, 128), BF),
@@ -1296,7 +1410,7 @@
             jax.ShapeDtypeStruct((2, 16, 2, 256, 128), BF),
         ],
         compiler_params=pltpu.CompilerParams(vmem_limit_bytes=VMEM_LIMIT),
-    )(slots, places, rows_of, spread, spread, spread, full, logs, upstream, base, steps)
+    )(group_place, spread, spread, spread, full, logs, upstream, base, steps)
 
 
 def tn(left, right):
@@ -1305,8 +1419,8 @@
 
 def feed_forward(second_low, dy, weights):
     def kernel(
-        low_hbm, dy_hbm, w_hbm, branch, dsecond, gate_out, up_out, down_out,
-        low, dys, gate_w, up_w, down_w, gate, up, dmixed, mixed, dgate, dup, chunks, sems, chunk_sems,
+        low_hbm, dy_hbm, w_hbm, branch, dsecond, gate_out, dup, mixed,
+        low, dys, gate_w, up_w, down_w, gate, up, dmixed, dgate, chunks, sems, chunk_sems,
     ):
         def load(n, src, dst):
             copy = pltpu.make_async_copy(src, dst, sems.at[n])
@@ -1345,17 +1459,14 @@
         lax.fori_loop(0, 32, step, 0)
         dsecond[...] = (nt(dgate[...], gate_w[...]) + nt(dup[...], up_w[...])).astype(BF)
         busy = {}
-        n = 0
-        for left, right, out in ((low, dgate, gate_out), (low, dup, up_out), (dys, mixed, down_out)):
-            for k in range(4):
-                rows = pl.ds(k * 512, 512)
-                slot = n % 2
-                if slot in busy:
-                    busy[slot].wait()
-                chunks[slot] = tn(left[:, rows], right[...]).astype(BF)
-                busy[slot] = pltpu.make_async_copy(chunks.at[slot], out.at[rows, :], chunk_sems.at[slot])
-                busy[slot].start()
-                n += 1
+        for k in range(4):
+            rows = pl.ds(k * 512, 512)
+            slot = k % 2
+            if slot in busy:
+                busy[slot].wait()
+            chunks[slot] = tn(low[:, rows], dgate[...]).astype(BF)
+            busy[slot] = pltpu.make_async_copy(chunks.at[slot], gate_out.at[rows, :], chunk_sems.at[slot])
+            busy[slot].start()
         branch[...] = nt(mixed[...], down_w[...]).astype(BF)
         busy[0].wait()
         busy[1].wait()
@@ -1364,13 +1475,15 @@
         kernel,
         name="feed_forward",
         in_specs=[ANY, ANY, ANY],
-        out_specs=[IN_VMEM, IN_VMEM, ANY, ANY, ANY],
-        out_shape=[jax.ShapeDtypeStruct((512, D), BF)] * 2 + [jax.ShapeDtypeStruct((D, UNITS), BF)] * 3,
+        out_specs=[IN_VMEM, IN_VMEM, ANY, IN_VMEM, IN_VMEM],
+        out_shape=[jax.ShapeDtypeStruct((512, D), BF)] * 2
+        + [jax.ShapeDtypeStruct((D, UNITS), BF)]
+        + [jax.ShapeDtypeStruct((512, UNITS), BF)] * 2,
         scratch_shapes=[pltpu.VMEM((512, D), BF)] * 2
         + [pltpu.VMEM((D, UNITS), BF)] * 3
         + [pltpu.VMEM((512, UNITS), F32)] * 3
-        + [pltpu.VMEM((512, UNITS), BF)] * 3
         + [
+            pltpu.VMEM((512, UNITS), BF),
             pltpu.VMEM((2, 512, UNITS), BF),
             pltpu.SemaphoreType.DMA((5,)),
             pltpu.SemaphoreType.DMA((2,)),
@@ -1379,63 +1492,15 @@
     )(second_low, dy, weights)
 
 
-def project_back(dproject, first_low, front):
-    def kernel(dp_ref, low_ref, w_hbm, dfirst, grad_out, bias_out, wide, weights, chunks, sems, chunk_sems):
-        load = pltpu.make_async_copy(w_hbm.at[:, pl.ds(0, 1536)], weights, sems.at[0])
-        load.start()
-        for m in range(2):
-            for t in range(3):
-                for h in range(4):
-                    to = t * 512 + h * 128
-                    wide[m * 256 : m * 256 + 256, to : to + 128] = dp_ref[m, h, (t + 2) % 3]
-        bias_out[...] = jnp.sum(wide[...].astype(F32), axis=0, keepdims=True)
-        busy = {}
-        for k in range(4):
-            rows = pl.ds(k * 512, 512)
-            slot = k % 2
-            if slot in busy:
-                busy[slot].wait()
-            chunks[slot] = tn(low_ref[:, rows], wide[...]).astype(BF)
-            busy[slot] = pltpu.make_async_copy(chunks.at[slot], grad_out.at[rows, :], chunk_sems.at[slot])
-            busy[slot].start()
-        load.wait()
-        dfirst[...] = nt(wide[...], weights[...]).astype(BF)
-        busy[0].wait()
-        busy[1].wait()
-
-    return pl.pallas_call(
-        kernel,
-        name="project_back",
-        in_specs=[IN_VMEM, IN_VMEM, ANY],
-        out_specs=[IN_VMEM, ANY, IN_VMEM],
-        out_shape=[
-            jax.ShapeDtypeStruct((512, D), BF),
-            jax.ShapeDtypeStruct((D, 1536), BF),
-            jax.ShapeDtypeStruct((1, 1536), F32),
-        ],
-        scratch_shapes=[
-            pltpu.VMEM((512, 1536), BF),
-            pltpu.VMEM((D, 1536), BF),
-            pltpu.VMEM((2, 512, 1536), BF),
-            pltpu.SemaphoreType.DMA((1,)),
-            pltpu.SemaphoreType.DMA((2,)),
-        ],
-        compiler_params=pltpu.CompilerParams(vmem_limit_bytes=VMEM_LIMIT),
-    )(dproject, first_low, front)
-
-
-def rotary_tables(places):
+def angle_tables():
     lane = np.arange(128) % HEAD_DIM
-    power = 10000.0 ** (-jnp.arange(0, ROT, 2, dtype=F32) / ROT)
-    hot = (lane[None, :] % (ROT // 2) == np.arange(ROT // 2)[:, None]) & (lane[None, :] < ROT)
-    frequency = jnp.sum(jnp.where(hot, power[:, None], 0.0), axis=0)
-    angles = places.astype(F32)[:, None] * frequency[None, :]
-    return jnp.stack([jnp.cos(angles), jnp.sin(angles)])
-
-
-def angle_tables():
-    near = jnp.arange(128, dtype=jnp.int32)
-    return rotary_tables(near), rotary_tables(near[:32] * 128)
+    power = 10000.0 ** (-2.0 * (lane % (ROT // 2)) / ROT)
+    frequency = np.where(lane < ROT, power, 0.0)
+    tables = []
+    for places in (np.arange(128), np.arange(32) * 128):
+        angles = places[:, None] * frequency[None, :]
+        tables.append(jnp.asarray(np.stack([np.cos(angles), np.sin(angles)]).astype(np.float32)))
+    return tables
 
 
 def body(
@@ -1453,87 +1518,52 @@
     up_weight,
     down_weight,
 ):
-    ctx = lax.axis_index("ctx")
-    y, z = ctx // 4, lax.rem(ctx, 4)
-    shard_index = lax.axis_index("dp") * 16 + ctx
-
-    blocks = jnp.arange(32, dtype=jnp.int32)
-    hits = group_place[None, :] == blocks[:, None]
-    slots = jnp.sum(jnp.where(hits, blocks[None, :], 0), axis=1)
-    four = jnp.arange(4, dtype=jnp.int32)
-    rows_of = jnp.concatenate([y * 4 + four, four * 4 + z])
-    held_slots = (rows_of[:, None] * 2 + jnp.arange(2, dtype=jnp.int32)[None, :]).reshape(16)
-    chosen = held_slots[:, None] == blocks[None, :]
-    places = jnp.sum(jnp.where(chosen, group_place[None, :], 0), axis=1)
-    own_slots = ctx * 2 + jnp.arange(2, dtype=jnp.int32)
-    own_blocks = jnp.sum(
-        jnp.where(own_slots[:, None] == blocks[None, :], group_place[None, :], 0), axis=1
-    )
-    own_places = (own_blocks[:, None] * 128 + jnp.arange(128, dtype=jnp.int32)[None, :]).reshape(256)
-    own_tables = rotary_tables(own_places)
-    all_tables = angle_tables()
-
+    shard_index = lax.axis_index("dp") * 16 + lax.axis_index("ctx")
+    base, steps = angle_tables()
+
+    vectors = jnp.stack([attend_gain, attend_shift, mixer_gain, mixer_shift])
     vectors = jnp.concatenate(
         [
-            attend_gain,
-            attend_shift,
-            mixer_gain,
-            mixer_shift,
-            project_bias.transpose(2, 0, 1).reshape(48),
-            jnp.zeros((80,), BF),
+            jnp.pad(vectors, ((0, 0), (0, 64))),
+            jnp.pad(project_bias.reshape(1, 48), ((0, 0), (0, 80))),
+            jnp.zeros((59, 128), BF),
         ]
-    ).reshape(3, 128)
+    )
     front_shard = jnp.concatenate(
-        [project_weight.reshape(64, 1536), output_weight.T, jnp.pad(vectors, ((0, 61), (0, 0)))], axis=1
+        [project_weight.reshape(64, 1536), output_weight.T, vectors], axis=1
     )
     back_shard = jnp.concatenate([gate_weight, up_weight, down_weight.T], axis=1)
 
     tokens = inputs.reshape(512, D)
     quarters = inputs.reshape(4, 128, D)
-    front, gains, first_low, spread = front_forward(front_shard, tokens, own_tables)
+    front, gains, first_low, spread = front_forward(front_shard, tokens, group_place, base, steps)
     spread = spread.reshape(2, 16, 3, 256, 128)
-    attended_heads, attended_full, logs = attend(slots, places, rows_of, spread)
+    attended_heads, attended_full, logs = attend(group_place, spread)
     attended_low, hidden, second_low, back = middle_forward(
         attended_heads, front, quarters, gains, back_shard
     )
 
-    mixer_part, second_part, gate_grad, up_grad, down_grad = feed_forward(
-        second_low.reshape(512, D), cotangent.reshape(512, D), back
-    )
-
-    def shards(grad):
-        return grad.reshape(2, 4, 4, 64, grad.shape[1])
-
-    dhidden, mixer_vectors, output_grad, upstream, gate_grad, up_grad, down_grad = middle_backward(
+    second_low = second_low.reshape(512, D)
+    dy = cotangent.reshape(512, D)
+    branch, second_part, gate_grad, dup, mixed = feed_forward(second_low, dy, back)
+    dhidden, mixer_vectors, output_grad, upstream, out_block, gate_grad, up_grad, down_grad = middle_backward(
         second_part.reshape(4, 128, D),
-        cotangent.reshape(4, 128, D),
+        dy,
         hidden,
         gains,
         attended_low,
         front,
-        [shards(gate_grad), shards(up_grad), shards(down_grad)],
+        second_low,
+        dup,
+        mixed,
+        branch.reshape(4, 128, D),
+        gate_grad.reshape(2, 4, 4, 64, UNITS),
     )
 
-    dq, dkv = attend_back(
-        slots, places, rows_of, spread, attended_full, logs, upstream, all_tables
-    )
-    dproject, outputs = collect_heads(dkv.reshape(2, 4, 4, 2, 256, 128), dq, mixer_part.reshape(4, 128, D), hidden)
-    first_part, project_grad, bias_part = project_back(dproject, first_low, front)
-    small = jnp.concatenate(
-        [
-            jnp.zeros((2, D), F32),
-            mixer_vectors,
-            jnp.pad(bias_part, ((0, 0), (0, D - 1536))),
-            jnp.zeros((3, D), F32),
-        ]
-    )
+    dq, dkv = attend_back(group_place, spread, attended_full, logs, upstream, base, steps)
+    dproject, outputs = collect_heads(dkv.reshape(2, 4, 4, 2, 256, 128), dq, out_block)
     input_grad, small, project_grad, output_grad = last_backward(
-        first_part.reshape(4, 128, D),
-        quarters,
-        dhidden,
-        gains,
-        small,
-        [shards(project_grad), shards(output_grad)],
+        dproject, first_low, front, quarters, dhidden, gains, mixer_vectors, output_grad.reshape(2, 4, 4, 64, 512)
     )
     own = lax.dynamic_slice(small, (0, shard_index * 64), (4, 64))
     bias_grad = lax.dynamic_slice(

time: 444 us -> 408 us (0.919)
  Pallas kernels: 408 us -> 383 us
  other arithmetic: 11.8 us -> 3.13 us
    pallas_call x4 -> x3, Pallas kernels: 176 us -> 159 us  [the longest x1 69.3 us: front_forward(): remote_call(kernel, 'front_forward', 0, [ANY, IN_VMEM, IN_SMEM, IN_VMEM,...]
    pallas_call x1, Pallas kernels: 40.3 us -> 32.2 us  [feed_forward(): pl.pallas_call(kernel, name='feed_forward', in_specs=[ANY, ANY, ANY], out...]
where the time goes in v4:
time: 408 us; the launch traced here: 401 us
  Pallas kernels  383 us (94%)
  local copies, waits for them, and re-layouts  13.1 us (3%)
    pallas_call x1, Pallas kernels, front_forward(): remote_call(kernel, 'front_forward', 0, [ANY, IN_VMEM, IN_SMEM, IN_VMEM,...  69.3 us
    pallas_call x1, Pallas kernels, middle_forward(): remote_call(kernel, 'middle_forward', 3, [ANY, ANY, ANY, IN_VMEM, ANY], [...  62.5 us
    pallas_call x1, Pallas kernels, middle_backward(): remote_call(kernel, 'middle_backward', 4, [ANY, ANY, IN_VMEM, IN_VMEM, IN...  62.1 us
    pallas_call x1, Pallas kernels, last_backward(): remote_call(kernel, 'last_backward', 7, [IN_VMEM, ANY, ANY, ANY, IN_VMEM,...  59 us
    pallas_call x1, Pallas kernels, attend_back(): pl.pallas_call(kernel, name='attend_back', grid_spec=grid_spec, out_shape...  43.6 us
    pallas_call x1, Pallas kernels, feed_forward(): pl.pallas_call(kernel, name='feed_forward', in_specs=[ANY, ANY, ANY], out...  32.2 us
    pallas_call x1, Pallas kernels, collect_heads(): remote_call(kernel, 'collect_heads', 6, [ANY, ANY, IN_VMEM], [((2, 4, 3,...  30.4 us
    pallas_call x1, Pallas kernels, attend(): pl.pallas_call(kernel, name='attend', grid_spec=grid_spec, out_shape=[jax...  24.2 us

profile of v4, /device:TPU:1, one launch (start us, length us, event | category | flops | bytes accessed | tf_op | source)
XLA Modules:
  0.0 400.6 jit_solution(12118054206652418144)
XLA Ops:
  0.6 0.8 copy.34
  1.5 0.7 fusion.13
  2.2 0.9 copy.41
  3.2 1.6 fusion.6.src
  4.8 69.3 %front_forward.1 = (bf16[2048,2176]{1,0:T(8,128)(2,1)}, f32[4,2048]{1,0:T(4,128)}, bf16[512,2048]{1,0:T(8,128)(2,1)}, bf16[2,4,4,3,256,128]{5,4,3,2,1,0:T(8,128)(2,1)}) custom-call(bf16[64,2176]{1,0:T(8,128)(2,1)} %fusion.6.src, bf16[512,2048]{1,0:T(8,128)(2,1)} %bitcast.44, s32[32]{0:T(128)} %group_ref.5, f32[2,128,128]{2,1,0:T(8,128)} %constant.29.clone.base_ref, ...), custom_call_target="tpu_custom_call" | custom-call | tf_op jit(solution)/shard_map/front_forward/pallas_call | solution.py:607
  74.1 24.2 %attend.1 = (bf16[2,4,256,128]{3,2,1,0:T(8,128)(2,1)}, f32[2,4,256,128]{3,2,1,0:T(8,128)}, f32[2,8,256]{2,1,0:T(8,128)}) custom-call(s32[32]{0:T(128)} %group_ref.5, bf16[2,16,3,256,128]{4,3,2,1,0:T(8,128)(2,1)} %bitcast.38, bf16[2,16,3,256,128]{4,3,2,1,0:T(8,128)(2,1)} %bitcast.39, bf16[2,16,3,256,128]{4,3,2,1,0:T(8,128)(2,1)} %bitcast.40), custom_call_target="tpu_custom_call" | custom-call | tf_op jit(solution)/shard_map/attend/pallas_call | solution.py:1249
  98.4 0.8 pad_maximum_fusion.shard
  99.2 62.5 %middle_forward.1 = (bf16[512,512]{1,0:T(8,128)(2,1)}, f32[128,2048]{1,0:T(8,128)}, bf16[4,128,2048]{2,1,0:T(8,128)(2,1)}, bf16[2048,4224]{1,0:T(8,128)(2,1)}) custom-call(bf16[2,4,256,128]{3,2,1,0:T(8,128)(2,1)} %get-tuple-element.47.heads, bf16[2048,2176]{1,0:T(8,128)(2,1)} %get-tuple-element.48.front, bf16[4,128,2048]{2,1,0:T(8,128)(2,1)} %bitcast.45, ...), custom_call_target="tpu_custom_call" | custom-call | tf_op jit(solution)/shard_map/middle_forward/pallas_call | solution.py:695
  161.7 32.2 %feed_forward.1 = (bf16[512,2048]{1,0:T(8,128)(2,1)}, bf16[512,2048]{1,0:T(8,128)(2,1)}, bf16[2048,1408]{1,0:T(8,128)(2,1)}, bf16[512,1408]{1,0:T(8,128)(2,1)}, bf16[512,1408]{1,0:T(8,128)(2,1)}) custom-call(bf16[512,2048]{1,0:T(8,128)(2,1)} %bitcast.49, bf16[512,2048]{1,0:T(8,128)(2,1)} %bitcast.47, bf16[2048,4224]{1,0:T(8,128)(2,1)} %get-tuple-element.51.w_hbm), custom_call_target="tpu_custom_call" | custom-call | tf_op jit(solution)/shard_map/feed_forward/pallas_call | solution.py:1474
  193.9 62.1 %middle_backward.1 = (f32[128,2048]{1,0:T(8,128)}, f32[2,2048]{1,0:T(2,128)}, bf16[2048,512]{1,0:T(8,128)(2,1)}, bf16[2,4,256,128]{3,2,1,0:T(8,128)(2,1)}, bf16[...) custom-call(bf16[4,128,2048]{2,1,0:T(8,128)(2,1)} %bitcast.57, ...), custom_call_target="tpu_custom_call" | custom-call | tf_op jit(solution)/shard_map/middle_backward/pallas_call | solution.py:824
  255.9 43.6 %attend_back.1 = (bf16[2,4,256,128]{3,2,1,0:T(8,128)(2,1)}, bf16[2,16,2,256,128]{4,3,2,1,0:T(8,128)(2,1)}) custom-call(s32[32]{0:T(128)} %group_ref.5, bf16[2,16,3,256,128]{4,3,2,1,0:T(8,128)(2,1)} %bitcast.41, bf16[2,16,3,256,128]{4,3,2,1,0:T(8,128)(2,1)} %bitcast.42, bf16[2,16,3,256,128]{4,3,2,1,0:T(8,128)(2,1)} %bitcast.43, ...), custom_call_target="tpu_custom_call" | custom-call | tf_op jit(solution)/shard_map/attend_back/pallas_call | solution.py:1404
  299.5 30.4 %collect_heads.1 = (bf16[2,4,3,256,128]{4,3,2,1,0:T(8,128)(2,1)}, bf16[4,128,2048]{2,1,0:T(8,128)(2,1)}) custom-call(bf16[2,4,4,2,256,128]{5,4,3,2,1,0:T(8,128)(2,1)} %bitcast.52, bf16[2,4,256,128]{3,2,1,0:T(8,128)(2,1)} %get-tuple-element.61.dq, bf16[128,2048]{1,0:T(8,128)(2,1)} %get-tuple-element.62.block), custom_call_target="tpu_custom_call" | custom-call | tf_op jit(solution)/shard_map/collect_heads/pallas_call | solution.py:921
  329.9 59.0 %last_backward.1 = (bf16[4,128,2048]{2,1,0:T(8,128)(2,1)}, f32[8,2048]{1,0:T(8,128)}, f32[64,1536]{1,0:T(8,128)}, f32[64,512]{1,0:T(8,128)}) custom-call(bf16[2,4,3,256,128]{4,3,2,1,0:T(8,128)(2,1)} %get-tuple-element.64.dproject, bf16[512,2048]{1,0:T(8,128)(2,1)} %get-tuple-element.65.first_low, bf16[2048,2176]{1,0:T(8,128)(2,1)} %get-tuple-element.48.front, ...), custom_call_target="tpu_custom_call" | custom-call | tf_op jit(solution)/shard_map/last_backward/pallas_call | solution.py:1041
  388.9 0.8 constant_dynamic-slice_fusion.1
  390.1 1.8 copy.43
  391.9 0.8 slice_reduce_fusion
  392.9 0.7 copy.39
  393.6 1.3 copy.50
  394.9 1.0 copy-done.1
  395.9 1.3 copy.51
  397.2 0.7 copy.52
  397.9 0.7 copy.53
  398.6 0.7 copy.54
  399.4 0.7 copy.55
  (22 shorter events, 0.8 us)
Async XLA Ops:
  74.1 24.3 %copy-start.5 = (bf16[1408,64]{0,1:T(8,128)(2,1)S(1)}, bf16[1408,64]{0,1:T(8,128)(2,1)}, u32[]{:S(2)}) copy-start(bf16[1408,64]{0,1:T(8,128)(2,1)} %param.27) | copy-start | bytes 540676
  74.1 24.2 %copy-start.6 = (bf16[64,1408]{1,0:T(8,128)(2,1)S(1)}, bf16[64,1408]{1,0:T(8,128)(2,1)}, u32[]{:S(2)}) copy-start(bf16[64,1408]{1,0:T(8,128)(2,1)} %param.26) | copy-start | bytes 540676
  74.1 24.2 %copy-start.7 = (bf16[64,1408]{1,0:T(8,128)(2,1)S(1)}, bf16[64,1408]{1,0:T(8,128)(2,1)}, u32[]{:S(2)}) copy-start(bf16[64,1408]{1,0:T(8,128)(2,1)} %param.25) | copy-start | bytes 540676
  329.9 63.7 %copy-start = (bf16[4,128,2048]{2,1,0:T(8,128)(2,1)S(1)}, bf16[4,128,2048]{2,1,0:T(8,128)(2,1)}, u32[]{:S(2)}) copy-start(bf16[4,128,2048]{2,1,0:T(8,128)(2,1)} %get-tuple-element.63) | copy-start | bytes 6291460
  393.6 2.3 copy-start.1
  395.9 1.3 copy-start.8
  395.9 2.0 copy-start.4
  395.9 2.7 copy-start.3
  395.9 3.5 copy-start.2

commit v5 on v4

--- a/solution.py
+++ b/solution.py
@@ -11,6 +11,7 @@
 MESH = pl.DeviceIdType.MESH
 D = 2048
 UNITS = 1408
+GATE_SPLIT = 512
 HEAD_DIM = 64
 ROT = 16
 EPSILON = 1e-05
@@ -235,8 +236,6 @@
             self.hand_over(self.two[way, k].out(1))
 
     def far(self):
-        for k in (3, 1, 2):
-            self.pass_on(k)
         for k in (0, 3, 1, 2):
             for way in range(2):
                 self.two[way, k].arrive()
@@ -370,23 +369,18 @@
                 self.out[pl.ds(first + 16 * half, 16), :] = value
 
 
-def quarters_of(net, out, me):
-    c, y, z, x = me
-
-    def piece(d, half=None):
-        return out.at[up(x, d)] if half is None else out.at[up(x, d), pl.ds(64 * half, 64)]
-
-    return RingGather(net, lambda d: at(c, y, z, x + d), piece)
-
-
 class SumX:
-    def __init__(self, net, local, parts, held, spare, me):
+    def __init__(self, net, local, parts, held, spare, me, first=0, count=128):
         c, y, z, x = me
-        self.local, self.parts, self.held, self.x, self.net, self.me = local, parts, held, x, net, me
+        self.local, self.parts, self.held, self.x, self.net = local, parts, held, x, net
+        self.first, self.count = first, count
         self.along = lambda d: at(c, y, z, x + d)
-        self.ring = RingSum(
-            net, self.along, lambda d, half: held.at[up(x, d), pl.ds(64 * half, 64)], spare, self.add
-        )
+        self.ring = RingSum(net, self.along, lambda d, half: self.piece(held, d, half), spare, self.add)
+
+    def piece(self, ref, d, half=None):
+        size = self.count // 2
+        start, rows = (self.first, self.count) if half is None else (self.first + size * half, size)
+        return ref.at[up(self.x, d), pl.ds(start, rows)]
 
     def add(self, total, term):
         def one(i, carry):
@@ -394,10 +388,12 @@
             total[rows, :] = (total[rows, :].astype(F32) + term[rows, :].astype(F32)).astype(BF)
             return carry
 
-        lax.fori_loop(0, 4, one, 0)
+        lax.fori_loop(0, self.count // 32, one, 0)
 
     def load(self):
-        self.loads = [self.local.copy(self.parts.at[up(self.x, d)], self.held.at[up(self.x, d)]) for d in (2, 1, 3, 0)]
+        self.loads = [
+            self.local.copy(self.piece(self.parts, d), self.piece(self.held, d)) for d in (2, 1, 3, 0)
+        ]
 
     def start(self):
         for copy in self.loads:
@@ -417,20 +413,20 @@
 
             def loop(i, carry, half=half, terms=terms):
                 rows = pl.ds(pl.multiple_of(i * 32, 32), 32)
-                own = pl.ds(pl.multiple_of(64 * half + i * 32, 32), 32)
+                own = pl.ds(pl.multiple_of(self.first + self.count // 2 * half + i * 32, 32), 32)
                 value = self.held[self.x, own, :].astype(F32)
                 for term in terms:
                     value += term[rows, :].astype(F32)
                 step(own, value)
                 return carry
 
-            lax.fori_loop(0, 2, loop, 0)
+            lax.fori_loop(0, self.count // 64, loop, 0)
 
     def gather(self, block, out):
-        x = self.x
-        self.back = quarters_of(self.net, out, self.me)
-        self.mine = self.local.copy(block, out.at[x])
-        self.back.start(block)
+        self.back = RingGather(self.net, self.along, lambda d, half=None: self.piece(out, d, half))
+        rows = block.at[pl.ds(self.first, self.count)]
+        self.mine = self.local.copy(rows, self.piece(out, 0))
+        self.back.start(rows)
 
     def gather_middle(self):
         self.back.from_back()
@@ -447,6 +443,14 @@
 
 def sum_scratch():
     return [pltpu.VMEM((4, 128, D), BF), pltpu.VMEM((6, 64, D), BF)]
+
+
+def two_sums_scratch():
+    return [pltpu.VMEM((4, 128, D), BF), pltpu.VMEM((6, 32, D), BF), pltpu.VMEM((6, 32, D), BF)]
+
+
+def two_sums(net, local, held, spares, me):
+    return [SumX(net, local, None, held, spares[n], me, 64 * n, 64) for n in range(2)]
 
 
 def normed(values):
@@ -533,6 +537,8 @@
         lax.fori_loop(4, 8, centre, 0)
         gather.middle()
         lax.fori_loop(8, 16, centre, 0)
+        for k in (3, 1, 2):
+            gather.pass_on(k)
         gather.far()
         gather.finish()
         keep = local.copy(weights, front)
@@ -653,12 +659,12 @@
 
     def kernel(
         heads, front, inputs, gains, shard, attended, hidden, second, weights,
-        swapped, out_w, held, spare, base, low, ss, rs, ls,
+        swapped, out_w, held, spare_0, spare_1, base, low, ss, rs, ls,
     ):
         me = here()
         c, y, z, x = me
         net, local = Net(ss, rs), Local(ls)
-        sums = SumX(net, local, None, held, spare, me)
+        early, late = two_sums(net, local, held, (spare_0, spare_1), me)
         load = local.copy(front.at[:, TURNED], out_w)
         residual = local.copy(inputs.at[x], base)
         greet(y_peers(*me) + z_peers(*me) + core_peer(*me) + x_peers(*me))
@@ -672,9 +678,10 @@
                 attended[m * 256 : m * 256 + 256, h * 128 : h * 128 + 128] = swapped[m, h]
         for q in range(4):
             held[q] = nt(attended[q * 128 : q * 128 + 128, :], out_w[...]).astype(BF)
-        sums.start_held()
+        early.start_held()
         gather.near()
-        sums.middle()
+        early.middle()
+        late.start_held()
         gather.middle()
         residual.wait()
 
@@ -684,12 +691,20 @@
             norm, _ = normed(value)
             low[rows, :] = (norm * gains[2:3, :] + gains[3:4, :]).astype(BF)
 
-        sums.totals(step)
-        sums.gather(low, second)
+        early.totals(step)
+        early.gather(low, second)
+        late.middle()
+        gather.pass_on(3)
+        late.totals(step)
+        late.gather(low, second)
+        gather.pass_on(1)
+        early.gather_middle()
+        gather.pass_on(2)
+        late.gather_middle()
         gather.far()
-        sums.gather_middle()
         gather.finish()
-        sums.finish()
+        early.finish()
+        late.finish()
         net.finish()
 
     return remote_call(
@@ -704,9 +719,9 @@
             ((D, width), BF, ANY),
         ],
         [pltpu.VMEM((2, 4, 256, 128), BF), pltpu.VMEM((D, 512), BF)]
-        + sum_scratch()
+        + two_sums_scratch()
         + [pltpu.VMEM((128, D), BF), pltpu.VMEM((128, D), BF)],
-        SWAP_COPIES + GATHER_COPIES + SUM_COPIES,
+        SWAP_COPIES + GATHER_COPIES + 2 * SUM_COPIES,
         SWAP_LOCALS + SUM_LOCALS + 3,
     )(heads, front, inputs, gains, shard)
 
@@ -735,11 +750,20 @@
         loads = [local.copy(second_low, lows), local.copy(cotangent, dys)]
         load = local.copy(front.at[:, TURNED], out_w)
         greet(y_peers(*me) + z_peers(*me) + core_peer(*me) + x_peers(*me))
-        gate, up_, down_ = [
+        left, right = pl.ds(0, GATE_SPLIT), pl.ds(GATE_SPLIT, UNITS - GATE_SPLIT)
+        gate, gate_two, up_, down_ = [
             Scatter(net, local, grads, out, scratch[8 * k : 8 * k + 8], me)
-            for k, (grads, out) in enumerate(((gate_grad, gate_out), (None, up_out), (None, down_out)))
+            for k, (grads, out) in enumerate(
+                (
+                    (gate_grad.at[:, :, :, :, left], gate_out.at[:, left]),
+                    (gate_grad.at[:, :, :, :, right], gate_out.at[:, right]),
+                    (None, up_out),
+                    (None, down_out),
+                )
+            )
         ]
         gate.start()
+        gate_two.start()
         sums.start()
 
         def multiply(left, right, k, to):
@@ -751,6 +775,7 @@
             multiply(lows, dup, k, down_.held)
         up_.send_filled(down_.held)
         gate.first()
+        gate_two.first()
         sums.middle()
         for k in range(2, 4):
             multiply(lows, dup, k, up_.held)
@@ -761,6 +786,7 @@
         up_.first()
         net.wait_sent(up_.zero)
         gate.first_middle()
+        gate_two.first_middle()
         vectors[...] = jnp.zeros_like(vectors)
 
         def step(rows, dsecond):
@@ -780,6 +806,7 @@
         down_.first()
         up_.first_middle()
         gate.second()
+        gate_two.second()
         sums.gather_middle()
         late = SumX(net, local, branch, held, spare, me)
         late.load()
@@ -796,11 +823,13 @@
         swap = Swap(net, local, blocks, upstream, me)
         late.middle()
         gate.second_middle()
+        gate_two.second_middle()
         down_.second()
         whole = hidden_low[...].reshape(512, D)
         output_grad[...] = tn(whole, attended[...]).astype(BF)
         up_.second_middle()
         gate.third()
+        gate_two.third()
         down_.second_middle()
 
         def last(rows, total):
@@ -834,9 +863,12 @@
             ((128, D), BF, IN_VMEM),
         ]
         + [((64, UNITS), F32, IN_VMEM)] * 3,
-        scratch + scatter_scratch(UNITS) * 3,
-        SUM_COPIES + RING_SUM + SCATTER_COPIES * 3 + SWAP_COPIES,
-        SUM_LOCALS + 4 + SWAP_LOCALS + 3 + 1,
+        scratch
+        + scatter_scratch(GATE_SPLIT)
+        + scatter_scratch(UNITS - GATE_SPLIT)
+        + scatter_scratch(UNITS) * 2,
+        SUM_COPIES + RING_SUM + SCATTER_COPIES * 4 + SWAP_COPIES,
+        SUM_LOCALS + 4 + SWAP_LOCALS + 4 + 2,
     )(parts, cotangent, hidden, gains, attended, front, second_low, dup, mixed, branch, gate_grad)
 
 
@@ -868,9 +900,8 @@
             rings[1, k] = RingSum(
                 net, along_z, lambda d, half, k=k: mine.at[1, up(y, k), up(z, d), half], got.at[1, k], add
             )
-        whole = quarters_of(net, outputs, me)
-        own = local.copy(block, outputs.at[x])
-        whole.start(block)
+        whole = SumX(net, local, None, None, None, me)
+        whole.gather(block, outputs)
         for copy in loads:
             copy.wait()
         for ring in rings.values():
@@ -908,14 +939,12 @@
                 lates.append(local.copy(summed.at[0, 0], dproject.at[0, z, kv]))
                 lates.append(local.copy(summed.at[1, 0], dproject.at[1, y, kv]))
 
-        whole.from_back()
-        whole.from_ahead()
+        whole.gather_middle()
         for copy in two:
             copy.wait_recv()
         for copy in lates:
             copy.wait()
-        own.wait()
-        whole.arrive()
+        whole.finish()
         net.finish()
 
     return remote_call(
@@ -938,7 +967,7 @@
     def kernel(
         dproject, first_low, front, inputs, dhidden, gains, mixer_vectors, output_grad,
         input_grad, sums_out, project_out, output_out,
-        wide, weights, lows, held, spare, base, low, extra, small, got, *rest,
+        wide, weights, lows, held, spare_0, spare_1, base, low, extra, small, got, *rest,
     ):
         scratch, (ss, rs, ls) = rest[:-3], rest[-3:]
         me = here()
@@ -951,7 +980,7 @@
         project = Scatter(net, local, None, project_out, scratch[:8], me)
         output = Scatter(net, local, output_grad, output_out, scratch[8:], me)
         output.start()
-        sums = SumX(net, local, None, held, spare, me)
+        early, late = two_sums(net, local, held, (spare_0, spare_1), me)
         for m in range(2):
             for t in range(3):
                 for h in range(4):
@@ -965,10 +994,10 @@
             held[q] = nt(rows, weights[...]).astype(BF)
 
         quarter(2)
-        sums.ring.start_far()
+        early.ring.start_far()
         quarter(1)
         quarter(3)
-        sums.ring.start_near()
+        early.ring.start_near()
 
         def multiply(k, to):
             value = tn(lows[:, other_half(c, k, 512)], wide[...]).astype(BF)
@@ -978,15 +1007,13 @@
         for k in range(2):
             multiply(k, extra)
         project.send_filled(extra)
-        sums.middle()
+        early.middle()
+        late.ring.start_far()
+        late.ring.start_near()
         quarter(0)
-        for k in range(2, 4):
-            multiply(k, project.held)
-        output.first()
         small[0, ...] = jnp.zeros_like(small[0])
         small[0, 2:4, :] = mixer_vectors[...]
         small[0, 4:5, 0:1536] = jnp.sum(wide[...].astype(F32), axis=0, keepdims=True)
-        project.first()
         residual.wait()
 
         def step(rows, dfirst):
@@ -996,18 +1023,26 @@
             small[0, 0:1, :] += jnp.sum(dfirst * norm, axis=0, keepdims=True)
             small[0, 1:2, :] += jnp.sum(dfirst, axis=0, keepdims=True)
 
-        sums.totals(step)
+        early.totals(step)
+        early.gather(low, input_grad)
+        late.middle()
+        for k in range(2, 4):
+            multiply(k, project.held)
+        output.first()
+        project.first()
+        late.totals(step)
+        late.gather(low, input_grad)
         copies = [net.send(small.at[0], got.at[0, d - 1], at(c, y, z, x + d)) for d in STEPS]
-        sums.gather(low, input_grad)
         output.first_middle()
         project.first_middle()
+        early.gather_middle()
         for copy in copies:
             copy.wait_recv()
         small[1, ...] = small[0, ...]
         for n in range(3):
             small[1, 0:4, :] += got[0, n, 0:4, :]
         copies = [net.send(small.at[1], got.at[1, d - 1], at(c, y + d, z, x)) for d in STEPS]
-        sums.gather_middle()
+        late.gather_middle()
         output.second()
         project.second()
         for copy in copies:
@@ -1024,12 +1059,13 @@
         project.third()
         copy.wait_recv()
         sums_out[...] = small[3, ...] + got[3, 0]
-        sums.finish()
+        early.finish()
+        late.finish()
         net.finish()
 
     scratch = (
         [pltpu.VMEM((512, 1536), BF), pltpu.VMEM((D, 1536), BF), pltpu.VMEM((512, D), BF)]
-        + sum_scratch()
+        + two_sums_scratch()
         + [
             pltpu.VMEM((128, D), BF),
             pltpu.VMEM((128, D), BF),
@@ -1050,7 +1086,7 @@
             ((64, 512), F32, IN_VMEM),
         ],
         scratch + scatter_scratch(1536) + scatter_scratch(512),
-        SUM_COPIES + 10 + SCATTER_COPIES * 2,
+        2 * SUM_COPIES + 10 + SCATTER_COPIES * 2,
         SUM_LOCALS + 4,
     )(dproject, first_low, front, inputs, dhidden, gains, mixer_vectors, output_grad)
 
@@ -1119,10 +1155,18 @@
     return block, tile, places[m * 8 + block] * 128 - tile * TILE
 
 
-def key_minus_query():
-    return lax.broadcasted_iota(jnp.int32, (TILE, 256), 0) - lax.rem(
-        lax.broadcasted_iota(jnp.int32, (TILE, 256), 1), 128
-    )
+def lay_mask(steps, bars):
+    row = lax.broadcasted_iota(jnp.int32, (1024, 128), 0) - 513
+    lane = lax.broadcasted_iota(jnp.int32, (1024, 128), 1)
+    steps[...] = jnp.where(jnp.minimum(row, 127) == lane, 1.0, 0.0).astype(BF)
+    bar = lax.broadcasted_iota(jnp.int32, (128, 256), 0)
+    query = lax.rem(lax.broadcasted_iota(jnp.int32, (128, 256), 1), 128)
+    bars[...] = jnp.where(bar >= query, LOW, 0.0).astype(BF)
+
+
+def with_mask(keys, steps, behind):
+    first = 512 - jnp.minimum(behind, 512)
+    return jnp.concatenate([keys, steps[pl.ds(pl.multiple_of(first, 128), TILE), :]], axis=1)
 
 
 def tile_of(t):
@@ -1147,7 +1191,7 @@
 def attend(group_place, spread):
     def kernel(
         group_ref, k_ref, v_ref, q_ref, o_ref, full_ref, log_ref,
-        slots, places, keys, values_t, queries, scores_0, scores_1, weights_0, weights_1, results, sums,
+        slots, places, keys, values_t, queries, scores_0, scores_1, weights_0, weights_1, results, tops, steps, bars,
     ):
         scores, weights = (scores_0, scores_1), (weights_0, weights_1)
         m = pl.program_id(0)
@@ -1155,34 +1199,32 @@
 
         def lay(slot, rows, to):
             keys[to, :] = k_ref[0, slot, 0, rows, :]
-            values_t[:, to] = v_ref[0, slot, 0, rows, :].T
+            values_t[:128, to] = v_ref[0, slot, 0, rows, :].T
 
         lay_blocks(slots, lay)
         for b in range(8):
             row = row_of(m, b // 2)
             block = q_ref[0, row, 0, (b % 2) * 128 : (b % 2) * 128 + 128, :]
-            queries[b] = (two_heads_t(block) * 0.125).astype(BF)
-        offset = key_minus_query()
+            queries[b, :128] = (two_heads_t(block) * 0.125).astype(BF)
+        lay_mask(steps, bars)
+        for b in range(8):
+            queries[b, 128:] = bars[...]
+        values_t[128:, :] = jnp.ones((16, 4096), BF)
 
         def multiply(n, odd):
+            block, tile, behind = unit_of(places, m, n)
+            scores[odd][...] = jnp.dot(
+                with_mask(keys[tile_of(tile), :], steps, behind), queries[block], preferred_element_type=F32
+            )
+
+        def soften(n, odd, top):
             block, tile, _ = unit_of(places, m, n)
-            scores[odd][...] = jnp.dot(
-                keys[tile_of(tile), :], queries[block], preferred_element_type=F32
-            )
-
-        def soften(n, odd, top, total):
-            block, tile, limit = unit_of(places, m, n)
-            value = jnp.where(offset <= limit, scores[odd][...] * LOG2E, LOW)
-            first = tile == 0
-            top = jnp.where(first, LOW, top)
+            value = scores[odd][...] * LOG2E
+            top = jnp.where(tile == 0, LOW, top)
             new_top = jnp.maximum(top, jnp.max(value, axis=0, keepdims=True))
-            exps = jnp.exp2(value - new_top)
-            shrink = jnp.exp2(top - new_top)
-            total = total * shrink + jnp.sum(exps, axis=0, keepdims=True)
-            weights[odd][...] = exps.astype(BF)
-            sums[block, 0:1, :] = new_top
-            sums[block, 1:2, :] = total
-            return new_top, total, shrink
+            weights[odd][...] = jnp.exp2(value - new_top).astype(BF)
+            tops[block, 0:1, :] = new_top
+            return new_top, jnp.exp2(top - new_top)
 
         def gather(n, odd, shrink, acc):
             block, tile, _ = unit_of(places, m, n)
@@ -1192,32 +1234,31 @@
             results[block] = acc
             return acc
 
-        row = jnp.zeros((1, 256), F32)
         multiply(0, 0)
         multiply(1, 1)
-        top, total, shrink = soften(0, 0, row, row)
+        top, shrink = soften(0, 0, jnp.zeros((1, 256), F32))
 
         def step(k, carry):
-            top, total, shrink, acc = carry
+            top, shrink, acc = carry
             for n, odd in ((2 * k + 1, 1), (2 * k + 2, 0)):
                 multiply(n + 1, 1 - odd)
                 acc = gather(n - 1, 1 - odd, shrink, acc)
-                top, total, shrink = soften(n, odd, top, total)
-            return top, total, shrink, acc
-
-        carry = (top, total, shrink, jnp.zeros((128, 256), F32))
-        top, total, shrink, acc = lax.fori_loop(0, UNITS_EACH // 2 - 1, step, carry)
+                top, shrink = soften(n, odd, top)
+            return top, shrink, acc
+
+        carry = (top, shrink, jnp.zeros((144, 256), F32))
+        top, shrink, acc = lax.fori_loop(0, UNITS_EACH // 2 - 1, step, carry)
         last = UNITS_EACH - 1
         acc = gather(last - 1, 0, shrink, acc)
-        _, _, shrink = soften(last, 1, top, total)
+        _, shrink = soften(last, 1, top)
         gather(last, 1, shrink, acc)
         for b in range(8):
             rows = slice((b % 2) * 128, (b % 2) * 128 + 128)
-            total = sums[b, 1:2, :]
-            result = one_block(results[b] / total)
+            total = results[b, 128:129, :]
+            result = one_block(results[b, :128, :] / total)
             full_ref[0, b // 2, rows, :] = result
             o_ref[0, b // 2, rows, :] = result.astype(BF)
-            log_ref[0, b : b + 1, :] = sums[b, 0:1, :] + jnp.log2(total)
+            log_ref[0, b : b + 1, :] = tops[b, 0:1, :] + jnp.log2(total)
 
     grid_spec = pltpu.PrefetchScalarGridSpec(
         num_scalar_prefetch=1,
@@ -1236,14 +1277,16 @@
             pltpu.SMEM((32,), jnp.int32),
             pltpu.SMEM((16,), jnp.int32),
             pltpu.VMEM((4096, 128), BF),
-            pltpu.VMEM((128, 4096), BF),
-            pltpu.VMEM((8, 128, 256), BF),
+            pltpu.VMEM((144, 4096), BF),
+            pltpu.VMEM((8, 256, 256), BF),
             pltpu.VMEM((TILE, 256), F32),
             pltpu.VMEM((TILE, 256), F32),
             pltpu.VMEM((TILE, 256), BF),
             pltpu.VMEM((TILE, 256), BF),
-            pltpu.VMEM((8, 128, 256), F32),
+            pltpu.VMEM((8, 144, 256), F32),
             pltpu.VMEM((8, 8, 256), F32),
+            pltpu.VMEM((1024, 128), BF),
+            pltpu.VMEM((128, 256), BF),
         ],
     )
     return pl.pallas_call(
@@ -1264,7 +1307,7 @@
         group_ref, k_ref, v_ref, q_ref, full_ref, log_ref, up_ref, base_ref, steps_ref,
         dq_ref, dkv_ref,
         slots, places, keys, keys_t, values, dkeys, dvalues, queries, queries_t, grads, grads_t, delta,
-        scores_0, scores_1, dprobs_0, dprobs_1, probs_0, probs_1, dscores_0, dscores_1, results,
+        scores_0, scores_1, dprobs_0, dprobs_1, probs_0, probs_1, dscores_0, dscores_1, results, steps, bars,
     ):
         scores, dprobs = (scores_0, scores_1), (dprobs_0, dprobs_1)
         probs_low, dscores = (probs_0, probs_1), (dscores_0, dscores_1)
@@ -1284,28 +1327,29 @@
             rows = slice((b % 2) * 128, (b % 2) * 128 + 128)
             block = q_ref[0, row_of(m, b // 2), 0, rows, :]
             queries[b] = (two_heads(block) * 0.125).astype(BF)
-            queries_t[b] = (two_heads_t(block) * 0.125).astype(BF)
+            queries_t[b, :128] = (two_heads_t(block) * 0.125).astype(BF)
             ups = up_ref[0, b // 2, rows, :]
             grads[b] = two_heads(ups).astype(BF)
             grads_t[b] = two_heads_t(ups).astype(BF)
             product = (ups.astype(F32) * full_ref[0, b // 2, rows, :]).T
             delta[b, 0:1, :128] = jnp.sum(product[:HEAD_DIM], axis=0, keepdims=True)
             delta[b, 0:1, 128:] = jnp.sum(product[HEAD_DIM:], axis=0, keepdims=True)
-        offset = key_minus_query()
+        lay_mask(steps, bars)
+        for b in range(8):
+            queries_t[b, 128:] = bars[...]
 
         def multiply(n, odd):
-            block, tile, _ = unit_of(places, m, n)
+            block, tile, behind = unit_of(places, m, n)
             scores[odd][...] = jnp.dot(
-                keys[tile_of(tile), :], queries_t[block], preferred_element_type=F32
+                with_mask(keys[tile_of(tile), :], steps, behind), queries_t[block], preferred_element_type=F32
             )
             dprobs[odd][...] = jnp.dot(
                 values[tile_of(tile), :], grads_t[block], preferred_element_type=F32
             )
 
         def soften(n, odd):
-            block, _, limit = unit_of(places, m, n)
+            block, _, _ = unit_of(places, m, n)
             value = jnp.exp2(scores[odd][...] * LOG2E - log_ref[0, pl.ds(block, 1), :])
-            value = jnp.where(offset <= limit, value, 0.0)
             probs_low[odd][...] = value.astype(BF)
             dscores[odd][...] = (
                 value * (dprobs[odd][...] - delta[block, 0:1, :])
@@ -1386,7 +1430,7 @@
             pltpu.VMEM((4096, 128), F32),
             pltpu.VMEM((4096, 128), F32),
             pltpu.VMEM((8, 256, 128), BF),
-            pltpu.VMEM((8, 128, 256), BF),
+            pltpu.VMEM((8, 256, 256), BF),
             pltpu.VMEM((8, 256, 128), BF),
             pltpu.VMEM((8, 128, 256), BF),
             pltpu.VMEM((8, 8, 256), F32),
@@ -1399,6 +1443,8 @@
             pltpu.VMEM((TILE, 256), BF),
             pltpu.VMEM((TILE, 256), BF),
             pltpu.VMEM((8, 128, 256), F32),
+            pltpu.VMEM((1024, 128), BF),
+            pltpu.VMEM((128, 256), BF),
         ],
     )
     return pl.pallas_call(

time: 408 us -> 412 us (level)
    pallas_call x1, Pallas kernels: 59 us -> 63.1 us  [last_backward(): remote_call(kernel, 'last_backward', 7, [IN_VMEM, ANY, ANY, ANY, IN_VMEM,...]
where the time goes in v5:
time: 412 us; the launch traced here: 405 us
  Pallas kernels  387 us (94%)
  local copies, waits for them, and re-layouts  13.1 us (3%)
    pallas_call x1, Pallas kernels, front_forward(): remote_call(kernel, 'front_forward', 0, [ANY, IN_VMEM, IN_SMEM, IN_VMEM,...  69.3 us
    pallas_call x1, Pallas kernels, middle_backward(): remote_call(kernel, 'middle_backward', 4, [ANY, ANY, IN_VMEM, IN_VMEM, IN...  65.6 us
    pallas_call x1, Pallas kernels, last_backward(): remote_call(kernel, 'last_backward', 7, [IN_VMEM, ANY, ANY, ANY, IN_VMEM,...  63.1 us
    pallas_call x1, Pallas kernels, middle_forward(): remote_call(kernel, 'middle_forward', 3, [ANY, ANY, ANY, IN_VMEM, ANY], [...  62.2 us
    pallas_call x1, Pallas kernels, attend_back(): pl.pallas_call(kernel, name='attend_back', grid_spec=grid_spec, out_shape...  42 us
    pallas_call x1, Pallas kernels, feed_forward(): pl.pallas_call(kernel, name='feed_forward', in_specs=[ANY, ANY, ANY], out...  32.2 us
    pallas_call x1, Pallas kernels, collect_heads(): remote_call(kernel, 'collect_heads', 6, [ANY, ANY, IN_VMEM], [((2, 4, 3,...  30 us
    pallas_call x1, Pallas kernels, attend(): pl.pallas_call(kernel, name='attend', grid_spec=grid_spec, out_shape=[jax...  22.7 us

profile of v5, /device:TPU:1, one launch (start us, length us, event | category | flops | bytes accessed | tf_op | source)
XLA Modules:
  0.0 404.6 jit_solution(11353940313623269824)
XLA Ops:
  0.6 0.8 copy.34
  1.5 0.7 fusion.13
  2.2 0.9 copy.41
  3.2 1.6 fusion.6.src
  4.8 69.3 %front_forward.1 = (bf16[2048,2176]{1,0:T(8,128)(2,1)}, f32[4,2048]{1,0:T(4,128)}, bf16[512,2048]{1,0:T(8,128)(2,1)}, bf16[2,4,4,3,256,128]{5,4,3,2,1,0:T(8,128)(2,1)}) custom-call(bf16[64,2176]{1,0:T(8,128)(2,1)} %fusion.6.src, bf16[512,2048]{1,0:T(8,128)(2,1)} %bitcast.44, s32[32]{0:T(128)} %group_ref.5, f32[2,128,128]{2,1,0:T(8,128)} %constant.29.clone.base_ref, ...), custom_call_target="tpu_custom_call" | custom-call | tf_op jit(solution)/shard_map/front_forward/pallas_call | solution.py:613
  74.1 22.7 %attend.1 = (bf16[2,4,256,128]{3,2,1,0:T(8,128)(2,1)}, f32[2,4,256,128]{3,2,1,0:T(8,128)}, f32[2,8,256]{2,1,0:T(8,128)}) custom-call(s32[32]{0:T(128)} %group_ref.5, bf16[2,16,3,256,128]{4,3,2,1,0:T(8,128)(2,1)} %bitcast.38, bf16[2,16,3,256,128]{4,3,2,1,0:T(8,128)(2,1)} %bitcast.39, bf16[2,16,3,256,128]{4,3,2,1,0:T(8,128)(2,1)} %bitcast.40), custom_call_target="tpu_custom_call" | custom-call | tf_op jit(solution)/shard_map/attend/pallas_call | solution.py:1292
  96.9 0.8 pad_maximum_fusion.shard
  97.7 62.2 %middle_forward.1 = (bf16[512,512]{1,0:T(8,128)(2,1)}, f32[128,2048]{1,0:T(8,128)}, bf16[4,128,2048]{2,1,0:T(8,128)(2,1)}, bf16[2048,4224]{1,0:T(8,128)(2,1)}) custom-call(bf16[2,4,256,128]{3,2,1,0:T(8,128)(2,1)} %get-tuple-element.47.heads, bf16[2048,2176]{1,0:T(8,128)(2,1)} %get-tuple-element.48.front, bf16[4,128,2048]{2,1,0:T(8,128)(2,1)} %bitcast.45, ...), custom_call_target="tpu_custom_call" | custom-call | tf_op jit(solution)/shard_map/middle_forward/pallas_call | solution.py:710
  159.9 32.2 %feed_forward.1 = (bf16[512,2048]{1,0:T(8,128)(2,1)}, bf16[512,2048]{1,0:T(8,128)(2,1)}, bf16[2048,1408]{1,0:T(8,128)(2,1)}, bf16[512,1408]{1,0:T(8,128)(2,1)}, bf16[512,1408]{1,0:T(8,128)(2,1)}) custom-call(bf16[512,2048]{1,0:T(8,128)(2,1)} %bitcast.49, bf16[512,2048]{1,0:T(8,128)(2,1)} %bitcast.47, bf16[2048,4224]{1,0:T(8,128)(2,1)} %get-tuple-element.51.w_hbm), custom_call_target="tpu_custom_call" | custom-call | tf_op jit(solution)/shard_map/feed_forward/pallas_call | solution.py:1520
  192.1 65.6 %middle_backward.1 = (f32[128,2048]{1,0:T(8,128)}, f32[2,2048]{1,0:T(2,128)}, bf16[2048,512]{1,0:T(8,128)(2,1)}, bf16[2,4,256,128]{3,2,1,0:T(8,128)(2,1)}, bf16[...) custom-call(bf16[4,128,2048]{2,1,0:T(8,128)(2,1)} %bitcast.57, ...), custom_call_target="tpu_custom_call" | custom-call | tf_op jit(solution)/shard_map/middle_backward/pallas_call | solution.py:853
  257.7 42.0 %attend_back.1 = (bf16[2,4,256,128]{3,2,1,0:T(8,128)(2,1)}, bf16[2,16,2,256,128]{4,3,2,1,0:T(8,128)(2,1)}) custom-call(s32[32]{0:T(128)} %group_ref.5, bf16[2,16,3,256,128]{4,3,2,1,0:T(8,128)(2,1)} %bitcast.41, bf16[2,16,3,256,128]{4,3,2,1,0:T(8,128)(2,1)} %bitcast.42, bf16[2,16,3,256,128]{4,3,2,1,0:T(8,128)(2,1)} %bitcast.43, ...), custom_call_target="tpu_custom_call" | custom-call | tf_op jit(solution)/shard_map/attend_back/pallas_call | solution.py:1450
  299.8 30.0 %collect_heads.1 = (bf16[2,4,3,256,128]{4,3,2,1,0:T(8,128)(2,1)}, bf16[4,128,2048]{2,1,0:T(8,128)(2,1)}) custom-call(bf16[2,4,4,2,256,128]{5,4,3,2,1,0:T(8,128)(2,1)} %bitcast.52, bf16[2,4,256,128]{3,2,1,0:T(8,128)(2,1)} %get-tuple-element.61.dq, bf16[128,2048]{1,0:T(8,128)(2,1)} %get-tuple-element.62.block), custom_call_target="tpu_custom_call" | custom-call | tf_op jit(solution)/shard_map/collect_heads/pallas_call | solution.py:950
  329.8 63.1 %last_backward.1 = (bf16[4,128,2048]{2,1,0:T(8,128)(2,1)}, f32[8,2048]{1,0:T(8,128)}, f32[64,1536]{1,0:T(8,128)}, f32[64,512]{1,0:T(8,128)}) custom-call(bf16[2,4,3,256,128]{4,3,2,1,0:T(8,128)(2,1)} %get-tuple-element.64.dproject, bf16[512,2048]{1,0:T(8,128)(2,1)} %get-tuple-element.65.first_low, bf16[2048,2176]{1,0:T(8,128)(2,1)} %get-tuple-element.48.front, ...), custom_call_target="tpu_custom_call" | custom-call | tf_op jit(solution)/shard_map/last_backward/pallas_call | solution.py:1077
  392.9 0.8 constant_dynamic-slice_fusion.1
  394.2 1.8 copy.43
  396.0 0.8 slice_reduce_fusion
  396.9 0.7 copy.39
  397.6 1.3 copy.50
  398.9 1.0 copy-done.1
  400.0 1.3 copy.51
  401.3 0.7 copy.52
  402.0 0.7 copy.53
  402.7 0.7 copy.54
  403.4 0.7 copy.55
  (22 shorter events, 0.8 us)
Async XLA Ops:
  74.1 22.8 %copy-start.5 = (bf16[1408,64]{0,1:T(8,128)(2,1)S(1)}, bf16[1408,64]{0,1:T(8,128)(2,1)}, u32[]{:S(2)}) copy-start(bf16[1408,64]{0,1:T(8,128)(2,1)} %param.27) | copy-start | bytes 540676
  74.1 22.8 %copy-start.6 = (bf16[64,1408]{1,0:T(8,128)(2,1)S(1)}, bf16[64,1408]{1,0:T(8,128)(2,1)}, u32[]{:S(2)}) copy-start(bf16[64,1408]{1,0:T(8,128)(2,1)} %param.26) | copy-start | bytes 540676
  74.1 22.8 %copy-start.7 = (bf16[64,1408]{1,0:T(8,128)(2,1)S(1)}, bf16[64,1408]{1,0:T(8,128)(2,1)}, u32[]{:S(2)}) copy-start(bf16[64,1408]{1,0:T(8,128)(2,1)} %param.25) | copy-start | bytes 540676
  329.8 67.8 %copy-start = (bf16[4,128,2048]{2,1,0:T(8,128)(2,1)S(1)}, bf16[4,128,2048]{2,1,0:T(8,128)(2,1)}, u32[]{:S(2)}) copy-start(bf16[4,128,2048]{2,1,0:T(8,128)(2,1)} %get-tuple-element.63) | copy-start | bytes 6291460
  397.6 2.3 copy-start.1
  400.0 1.3 copy-start.8
  400.0 2.0 copy-start.4
  400.0 2.7 copy-start.3
  400.0 3.5 copy-start.2
